TPU v7x, 256 devices: a whole 4x4x8 slice. The times are simulated.
256 devices in a mesh: pts: 32 (over x, z_lo, core), lat: 8 (over z_hi, y).
Axes of the slice: x: 4, y: 4, z: 8 (z_hi: 2, z_lo: 4; z = z_hi * 4 + z_lo), core: 2. Of those that a mesh axis runs over, the one named last changes fastest.
Arguments:
- latents: bfloat16 [8192, 128], P('lat'), may hold values from -9 to 9
- keys: bfloat16 [131072, 128], P('pts'), may hold values from -9 to 9
- values: bfloat16 [131072, 128], P('pts'), may hold values from -6 to 6
- sweep: int32 [131072], P('pts'), may hold values from 0 to 15
- sweep_bias: float32 [4, 16], replicated, may hold values from -4 to 4
- grad_out: bfloat16 [8192, 128], P('lat'), may hold values from -6 to 6
Outputs:
- grad_latents: float32 [8192, 128], P(('lat', 'pts'))
- grad_keys: float32 [131072, 128], P(('pts', 'lat'))
- grad_values: float32 [131072, 128], P(('pts', 'lat'))
- grad_bias: float32 [4, 16], replicated
All inputs are finite; a program needn't handle non-finite values.
Results may differ from a plain program's by a relative error of at most 0.011.
Values sent between devices are 32-bit elements; how exact they have to be, the bound alone decides.
A program may use at most 64 MiB of HBM per device.

v0:
```python
import math

import jax
import jax.numpy as jnp
from jax import lax
from jax.sharding import PartitionSpec as P

HEADS = 4
HEAD_DIM = 32
SWEEPS = 16


def heads_of(array):
    return array.reshape(array.shape[0], HEADS, HEAD_DIM)


def bias_columns(sweep_block, sweep_bias):
    onehot = (sweep_block[:, None] == jnp.arange(SWEEPS, dtype=jnp.int32)[None, :]).astype(
        jnp.float32
    )
    columns = jnp.einsum("hs,cs->hc", sweep_bias, onehot, precision=lax.Precision.HIGHEST)
    return (columns, onehot)


def score_tile(query_block, key_block, columns):
    raw = jnp.einsum(
        "rhd,chd->hrc",
        heads_of(query_block),
        heads_of(key_block),
        preferred_element_type=jnp.float32,
    )
    return raw * HEAD_DIM ** (-0.5) + columns[:, None, :]


def product_tile(grad_block, value_block):
    return jnp.einsum(
        "rhd,chd->hrc",
        heads_of(grad_block),
        heads_of(value_block),
        preferred_element_type=jnp.float32,
    )


def tile_grads(
    query_block, grad_block, top_block, total_block, delta_block, key_block, value_block, columns
):
    scores = score_tile(query_block, key_block, columns)
    out_prod = product_tile(grad_block, value_block)
    probs = jnp.exp(scores - top_block[:, :, None]) / total_block[:, :, None]
    score_grad = probs * (out_prod - delta_block[:, :, None])
    scaled = (score_grad * HEAD_DIM ** (-0.5)).astype(jnp.bfloat16)
    return (probs.astype(jnp.bfloat16), score_grad, scaled)


def key_value_grads(probs_low, scaled, query_block, grad_block):
    grad_k = jnp.einsum(
        "hrc,rhd->chd", scaled, heads_of(query_block), preferred_element_type=jnp.float32
    )
    grad_v = jnp.einsum(
        "hrc,rhd->chd", probs_low, heads_of(grad_block), preferred_element_type=jnp.float32
    )
    rows = grad_k.shape[0]
    return jnp.concatenate(
        [grad_k.reshape(rows, HEADS * HEAD_DIM), grad_v.reshape(rows, HEADS * HEAD_DIM)], axis=1
    )


def per_device(latents, keys, values, sweep, sweep_bias, grad_out):
    feature_width = HEADS * HEAD_DIM
    query_count = latents.shape[0]
    key_count = keys.shape[0]
    query_rows = math.gcd(query_count, 512)
    key_rows = math.gcd(key_count, 512)
    query_blocks = latents.reshape(query_count // query_rows, query_rows, feature_width)
    out_blocks = grad_out.reshape(query_count // query_rows, query_rows, feature_width)
    key_data = (
        keys.reshape(-1, key_rows, feature_width),
        values.reshape(-1, key_rows, feature_width),
        sweep.reshape(-1, key_rows),
    )
    lowest = jnp.full((HEADS, query_rows), -jnp.inf, jnp.float32)
    nothing = jnp.zeros((HEADS, query_rows), jnp.float32)

    def block_max(query_block):

        def inner(running, inputs):
            key_block, value_block, sweep_block = inputs
            columns, onehot = bias_columns(sweep_block, sweep_bias)
            scores = score_tile(query_block, key_block, columns)
            return (jnp.maximum(running, jnp.max(scores, axis=-1)), None)

        running, unused = lax.scan(inner, lowest, key_data)
        return running

    local_top = lax.map(block_max, query_blocks)
    row_top = lax.pmax(local_top, "pts")

    def block_sums(inputs):
        query_block, grad_block, top_block = inputs

        def inner(running, pieces):
            key_block, value_block, sweep_block = pieces
            columns, onehot = bias_columns(sweep_block, sweep_bias)
            expo = jnp.exp(score_tile(query_block, key_block, columns) - top_block[:, :, None])
            out_prod = product_tile(grad_block, value_block)
            return (
                (
                    running[0] + jnp.sum(expo, axis=-1),
                    running[1] + jnp.sum(expo * out_prod, axis=-1),
                ),
                None,
            )

        running, unused = lax.scan(inner, (nothing, nothing), key_data)
        return running

    local_totals, local_weighted = lax.map(block_sums, (query_blocks, out_blocks, row_top))
    totals, weighted = lax.psum((local_totals, local_weighted), "pts")
    deltas = weighted / totals
    query_data = (query_blocks, out_blocks, row_top, totals, deltas)

    def per_query(carried, inputs):
        query_block, grad_block, top_block, total_block, delta_block = inputs

        def per_key(grad_q, pieces):
            key_block, value_block, sweep_block = pieces
            columns, onehot = bias_columns(sweep_block, sweep_bias)
            probs_low, score_grad, scaled = tile_grads(
                query_block,
                grad_block,
                top_block,
                total_block,
                delta_block,
                key_block,
                value_block,
                columns,
            )
            grad_q = grad_q + jnp.einsum(
                "hrc,chd->rhd", scaled, heads_of(key_block), preferred_element_type=jnp.float32
            ).reshape(query_rows, feature_width)
            bias_part = jnp.einsum(
                "hc,cs->hs", jnp.sum(score_grad, axis=1), onehot, precision=lax.Precision.HIGHEST
            )
            return (
                grad_q,
                (key_value_grads(probs_low, scaled, query_block, grad_block), bias_part),
            )

        start_q = jnp.zeros((query_rows, feature_width), jnp.float32)
        grad_q, (kv_parts, bias_parts) = lax.scan(per_key, start_q, key_data)
        return (
            (
                carried[0] + kv_parts.reshape(key_count, 2 * feature_width),
                carried[1] + jnp.sum(bias_parts, axis=0),
            ),
            grad_q,
        )

    start = (
        jnp.zeros((key_count, 2 * feature_width), jnp.float32),
        jnp.zeros((HEADS, SWEEPS), jnp.float32),
    )
    (kv_sum, bias_local), grad_blocks = lax.scan(per_query, start, query_data)
    kv_mine = lax.psum_scatter(kv_sum, "lat", scatter_dimension=0, tiled=True)
    grad_latents = lax.psum_scatter(
        grad_blocks.reshape(query_count, feature_width), "pts", scatter_dimension=0, tiled=True
    )
    grad_bias = lax.psum(bias_local, ("pts", "lat"))
    return (grad_latents, kv_mine[:, :feature_width], kv_mine[:, feature_width:], grad_bias)


def solution(mesh):
    return jax.shard_map(
        per_device,
        mesh=mesh,
        in_specs=(P("lat", None), P("pts", None), P("pts", None), P("pts"), P(), P("lat", None)),
        out_specs=(P(("lat", "pts"), None), P(("pts", "lat"), None), P(("pts", "lat"), None), P()),
        check_vma=False,
    )
```

profile of v0, /device:TPU:1, one launch (start us, length us, event | category | flops | bytes accessed | tf_op | source)
XLA Modules:
  0.0 808.5 jit_solution(6692010263929430235)
XLA Ops:
  10.1 1.5 copy.18
  11.7 30.4 %while.78 = (s32[]{:T(128)}, f32[2,4,512]{2,1,0:T(4,128)S(1)}, bf16[2,512,128]{1,2,0:T(8,128)(2,1)S(1)}, bf16[8,512,128]{1,2,0:T(8,128)(2,1)S(1)}, s32[8,512]{1,...) while((s32[]{:T(128)}, f32[2,4,512]{2,1,0:T(4,128)S(1)}, ...), condition=%wide.region_4.5_spmd, body=%wide.region_0.4_spmd.sunk | while | flops 70658048 | bytes 858668 | solution.py:95
  11.7 15.2 %while.83 = (s32[]{:T(128)}, f32[4,512]{1,0:T(4,128)S(1)}, bf16[8,512,128]{1,2,0:T(8,128)(2,1)S(1)}, bf16[512,128]{0,1:T(8,128)(2,1)S(1)}, s32[8,512]{1,0:T(8,12...) while((s32[]{:T(128)}, f32[4,512]{1,0:T(4,128)S(1)}, bf16[8,512,128]{1,2,0:T(8,128)(2,1)S(1)}, ...), condition=%wide.region_3.3_spmd.clone, body=%wide.region_1.2_spmd.clone.sunk | while | flops 70658048 | bytes 579951 | solution.py:92
  26.9 15.1 %while.83 = (s32[]{:T(128)}, f32[4,512]{1,0:T(4,128)S(1)}, bf16[8,512,128]{1,2,0:T(8,128)(2,1)S(1)}, bf16[512,128]{0,1:T(8,128)(2,1)S(1)}, s32[8,512]{1,0:T(8,12...) while((s32[]{:T(128)}, f32[4,512]{1,0:T(4,128)S(1)}, bf16[8,512,128]{1,2,0:T(8,128)(2,1)S(1)}, ...), condition=%wide.region_3.3_spmd.clone, body=%wide.region_1.2_spmd.clone.sunk | while | flops 70658048 | bytes 579951 | solution.py:92
  42.1 134.7 %pmax.7 = f32[2,4,512]{2,1,0:T(4,128)S(1)} all-reduce(f32[2,4,512]{2,1,0:T(4,128)S(1)} %get-tuple-element.312), channel_id=1, replica_groups=mesh['pts'=32,'lat'=8] {'pts'}, use_global_device_ids=true, to_apply=%region_5.6 | all-reduce | flops 4096 | bytes 32768 | tf_op jit(solution)/shard_map/pmax | solution.py:96
  178.2 79.4 %while.80 = (s32[]{:T(128)}, f32[2,4,512]{2,1,0:T(4,128)S(1)}, f32[2,4,512]{2,1,0:T(4,128)S(1)}, bf16[2,512,128]{1,2,0:T(8,128)(2,1)S(1)}, f32[2,4,512]{2,1,0:T(...) while((s32[]{:T(128)}, f32[2,4,512]{2,1,0:T(4,128)S(1)}, ...), condition=%wide.region_11.12_spmd, body=%wide.region_6.11_spmd.sunk | while | flops 144060416 | bytes 10123928 | solution.py:117
  178.3 39.6 %while.84 = (s32[]{:T(128)}, f32[4,512]{1,0:T(4,128)S(1)}, f32[4,512]{1,0:T(4,128)S(1)}, bf16[8,512,128]{1,2,0:T(8,128)(2,1)S(1)}, bf16[512,128]{0,1:T(8,128)(2,...) while((s32[]{:T(128)}, f32[4,512]{1,0:T(4,128)S(1)}, ...), condition=%wide.region_10.10_spmd.clone, body=%wide.region_7.9_spmd.clone.sunk | while | flops 144060416 | bytes 9550227 | solution.py:114
  180.2 1.4 bitcast_reduce_fusion.5
  181.7 1.5 fusion.79
  185.2 1.4 bitcast_reduce_fusion.5
  186.6 1.5 fusion.79
  190.1 1.4 bitcast_reduce_fusion.5
  191.6 1.5 fusion.79
  195.1 1.4 bitcast_reduce_fusion.5
  196.5 1.5 fusion.79
  200.0 1.4 bitcast_reduce_fusion.5
  201.5 1.5 fusion.79
  205.0 1.4 bitcast_reduce_fusion.5
  206.4 1.5 fusion.79
  209.9 1.4 bitcast_reduce_fusion.5
  211.4 1.5 fusion.79
  214.9 1.4 bitcast_reduce_fusion.5
  216.3 1.5 fusion.79
  218.0 39.6 %while.84 = (s32[]{:T(128)}, f32[4,512]{1,0:T(4,128)S(1)}, f32[4,512]{1,0:T(4,128)S(1)}, bf16[8,512,128]{1,2,0:T(8,128)(2,1)S(1)}, bf16[512,128]{0,1:T(8,128)(2,...) while((s32[]{:T(128)}, f32[4,512]{1,0:T(4,128)S(1)}, ...), condition=%wide.region_10.10_spmd.clone, body=%wide.region_7.9_spmd.clone.sunk | while | flops 144060416 | bytes 9550227 | solution.py:114
  219.9 1.4 bitcast_reduce_fusion.5
  221.4 1.5 fusion.79
  224.9 1.4 bitcast_reduce_fusion.5
  226.3 1.5 fusion.79
  229.8 1.4 bitcast_reduce_fusion.5
  231.3 1.5 fusion.79
  234.8 1.4 bitcast_reduce_fusion.5
  236.2 1.5 fusion.79
  241.2 1.5 fusion.79
  244.7 1.4 bitcast_reduce_fusion.5
  246.1 1.5 fusion.79
  249.6 1.4 bitcast_reduce_fusion.5
  251.1 1.5 fusion.79
  256.0 1.5 fusion.79
  257.6 133.2 %all-reduce = (f32[2,4,512]{2,1,0:T(4,128)S(1)}, f32[2,4,512]{2,1,0:T(4,128)S(1)}) all-reduce(f32[2,4,512]{2,1,0:T(4,128)S(1)} %get-tuple-element.313, f32[2,4,512]{2,1,0:T(4,128)S(1)} %get-tuple-element.314), channel_id=1, replica_groups=mesh['pts'=32,'lat'=8] {'pts'}, use_global_device_ids=true, to_apply=%region_12.13 | all-reduce | flops 8192 | bytes 65536 | tf_op jit(solution)/shard_map/psum | solution.py:118
  390.8 140.8 %while.82 = (s32[]{:T(128)}, f32[4096,256]{1,0:T(8,128)}, f32[4,16]{1,0:T(4,128)S(1)}, f32[2,512,128]{2,1,0:T(8,128)}, bf16[2,512,128]{1,2,0:T(8,128)(2,1)S(1)},...) while((s32[]{:T(128)}, f32[4096,256]{1,0:T(8,128)}, ...), condition=%wide.region_19.20_spmd.clone, body=%wide.region_14.19_spmd.clone.sunk | while | flops 351287872 | bytes 49796908 | solution.py:163
  390.9 64.0 %while.85 = (s32[]{:T(128)}, f32[512,128]{0,1:T(8,128)S(1)}, f32[8,512,256]{2,1,0:T(8,128)}, f32[8,4,16]{2,1,0:T(4,128)S(1)}, bf16[8,512,128]{1,2,0:T(8,128)(2,1...) while((s32[]{:T(128)}, f32[512,128]{0,1:T(8,128)S(1)}, ...), condition=%wide.region_17.17_spmd.clone, body=%wide.region_15.16_spmd.clone.sunk | while | flops 349190144 | bytes 31394220 | solution.py:150
  392.9 1.8 exponential_divide_fusion.2
  400.9 1.8 exponential_divide_fusion.2
  408.9 1.8 exponential_divide_fusion.2
  416.9 1.8 exponential_divide_fusion.2
  424.9 1.8 exponential_divide_fusion.2
  432.9 1.8 exponential_divide_fusion.2
  440.9 1.8 exponential_divide_fusion.2
  448.9 1.8 exponential_divide_fusion.2
  455.0 4.7 bitcast_add_fusion.4
  460.7 64.0 %while.85 = (s32[]{:T(128)}, f32[512,128]{0,1:T(8,128)S(1)}, f32[8,512,256]{2,1,0:T(8,128)}, f32[8,4,16]{2,1,0:T(4,128)S(1)}, bf16[8,512,128]{1,2,0:T(8,128)(2,1...) while((s32[]{:T(128)}, f32[512,128]{0,1:T(8,128)S(1)}, ...), condition=%wide.region_17.17_spmd.clone, body=%wide.region_15.16_spmd.clone.sunk | while | flops 349190144 | bytes 31394220 | solution.py:150
  462.6 1.8 exponential_divide_fusion.2
  470.6 1.8 exponential_divide_fusion.2
  478.6 1.8 exponential_divide_fusion.2
  486.6 1.8 exponential_divide_fusion.2
  494.6 1.8 exponential_divide_fusion.2
  502.6 1.8 exponential_divide_fusion.2
  510.6 1.8 exponential_divide_fusion.2
  518.6 1.8 exponential_divide_fusion.2
  524.7 6.0 bitcast_add_fusion.4
  532.4 105.7 %psum.23 = f32[4,16]{1,0:T(4,128)} all-reduce(f32[4,16]{1,0:T(4,128)S(1)} %get-tuple-element.317), channel_id=1, replica_groups=mesh['pts'=32,'lat'=8] {'pts','lat'}, use_global_device_ids=true, to_apply=%region_22.23 | all-reduce | flops 64 | bytes 512 | tf_op jit(solution)/shard_map/psum | solution.py:168
  638.1 24.6 %reduce-scatter.5.cloned.1.call-done = f32[512,256]{1,0:T(8,128)} async-done(((f32[4096,256]{1,0:T(8,128)}), f32[512,256]{1,0:T(8,128)}) %reduce-scatter.5.cloned.1.call-update) | async-done | bytes 524304 | tf_op jit(solution)/shard_map/reduce_scatter | solution.py:164
  662.8 1.9 fusion.15
  664.6 137.1 %reduce-scatter.3.cloned.1.call-done = f32[32,128]{1,0:T(8,128)} async-done(((f32[1024,128]{1,0:T(8,128)}), f32[32,128]{1,0:T(8,128)}) %reduce-scatter.3.cloned.1.call-update) | async-done | bytes 16400 | tf_op jit(solution)/shard_map/reduce_scatter | solution.py:165
  (417 shorter events, 168.8 us)
Async XLA Ops:
  7.2 655.6 %reduce-scatter.5.cloned.1.call-start = ((), (), s32[]{:S(2)}) async-start(), calls=%async_computation.3 | async-start | bytes 4718592 | tf_op jit(solution)/shard_map/reduce_scatter | solution.py:164
  11.7 165.1 %copy-start = (bf16[4096,128]{1,0:T(8,128)(2,1)S(1)}, bf16[4096,128]{1,0:T(8,128)(2,1)}, u32[]{:S(2)}) copy-start(bf16[4096,128]{1,0:T(8,128)(2,1)} %param.20) | copy-start | bytes 3145732
  455.0 4.9 copy-start.1
  459.8 0.8 copy-start.2
  524.7 6.1 copy-start.1
  530.9 0.8 copy-start.2
  531.7 270.0 %reduce-scatter.3.cloned.1.call-start = ((), (), s32[]{:S(2)}) async-start(), calls=%async_computation.2 | async-start | bytes 540672 | tf_op jit(solution)/shard_map/reduce_scatter | solution.py:165
Sparse Core Ops, SparseCore 0:
  531.8 130.9 reduce-scatter.4
  665.8 135.8 reduce-scatter.2
where the time goes:
time: 815 us; the launch traced here: 809 us
  blocking collectives  374 us (46%)
  matrix products  185 us (23%)
  waiting for transfers between devices  162 us (20%)
  local copies, waits for them, and re-layouts  57.3 us (7%)
  between operations  14.1 us (2%)
  other arithmetic  13.1 us (2%)
    reduce_scatter x1, waiting for transfers between devices, per_device(): lax.psum_scatter(grad_blocks.reshape(query_count, feature_width), 'pts',...  137 us
    pmax x1, blocking collectives, per_device(): row_top = lax.pmax(local_top, 'pts')  135 us
    psum x1, blocking collectives, per_device(): totals, weighted = lax.psum((local_totals, local_weighted), 'pts')  133 us
    psum x1, blocking collectives, per_device(): grad_bias = lax.psum(bias_local, ('pts', 'lat'))  106 us
    dot_general x48, matrix products, score_tile(): jnp.einsum('rhd,chd->hrc', heads_of(query_block), heads_of(key_block), pr...  65.5 us
    dot_general x48, matrix products, bias_columns(): jnp.einsum('hs,cs->hc', sweep_bias, onehot, precision=lax.Precision.HIGHEST)  47.6 us
    dot_general x32, matrix products, product_tile(): jnp.einsum('rhd,chd->hrc', heads_of(grad_block), heads_of(value_block), p...  41.1 us
    dynamic_slice x112, local copies, waits for them, and re-layouts, block_max(): running, unused = lax.scan(inner, lowest, key_data)  30.9 us
  transfers between devices with their start and end apart: 2, of which 2 were waited for; matrix products, arithmetic and copies ran while one was open for 0% of the time, Pallas kernels for 0%

commit v1 on v0

v1 whole, which is shorter than its diff:
```python
import functools
import math

import jax
import jax.numpy as jnp
from jax import lax
from jax.experimental import pallas as pl
from jax.experimental.pallas import tpu as pltpu
from jax.sharding import PartitionSpec as P

HEADS = 4
HEAD_DIM = 32
WIDTH = HEADS * HEAD_DIM
SWEEPS = 16
SCALE = HEAD_DIM**-0.5
LOG2E = math.log2(math.e)
TO_LOG2 = SCALE * LOG2E
YS = 4
ONES_ROW = 3 * SWEEPS
BF = jnp.bfloat16
F32 = jnp.float32
MESH = pl.DeviceIdType.MESH
VMEM_BYTES = 56 * 1024 * 1024


def dot(a, b):
    return jnp.dot(a, b, preferred_element_type=F32)


def three_pieces(x):
    hi = x.astype(BF)
    rest = x - hi.astype(F32)
    mid = rest.astype(BF)
    low = (rest - mid.astype(F32)).astype(BF)
    return hi, mid, low


def vmem_specs(count):
    return [pl.BlockSpec(memory_space=pltpu.VMEM)] * count


def stats_kernel(keys_ref, aux_ref, value_rows_ref, q_t_ref, g_t_ref, bias_rows_ref, out_ref, k_aux, q_feat, scores):
    points, latents = keys_ref.shape[0], q_t_ref.shape[1]
    cols = min(256, latents)
    tiles = latents // cols
    chunk = min(512, points)
    chunks = points // chunk

    k_aux[:, :WIDTH] = keys_ref[...]
    k_aux[:, WIDTH:] = aux_ref[...]
    for h in range(HEADS):
        for tile in range(tiles):
            n = h * tiles + tile
            q_feat[n, :WIDTH, :] = jnp.zeros((WIDTH, cols), BF)
            q_feat[n, h * HEAD_DIM : (h + 1) * HEAD_DIM, :] = q_t_ref[
                h * HEAD_DIM : (h + 1) * HEAD_DIM, tile * cols : (tile + 1) * cols
            ]
            q_feat[n, WIDTH : WIDTH + 64, :] = bias_rows_ref[h, :, tile * cols : (tile + 1) * cols]
            q_feat[n, WIDTH + 64 :, :] = jnp.zeros((WIDTH - 64, cols), BF)

    lowest = jnp.full((8, cols), -jnp.inf, F32)

    def score_chunk(n, slot, c, top):
        rows = pl.ds(pl.multiple_of(c * chunk, chunk), chunk)
        s = dot(k_aux[rows, :], q_feat[n]) * TO_LOG2
        scores[slot, rows, :] = s
        return jnp.maximum(top, jnp.max(s.reshape(chunk // 8, 8, cols), axis=0))

    first = lax.fori_loop(0, chunks, lambda c, top: score_chunk(0, 0, c, top), lowest)

    def per_tile(n, top_rows):
        slot = lax.rem(n, 2)
        top = jnp.max(top_rows, axis=0, keepdims=True)
        following = lax.rem(n + 1, HEADS * tiles)
        head = n // tiles

        def body(c, carried):
            next_top, total, out = carried
            next_top = score_chunk(following, 1 - slot, c, next_top)
            rows = pl.ds(pl.multiple_of(c * chunk, chunk), chunk)
            e = jnp.exp2(scores[slot, rows, :] - top)
            total = total + jnp.sum(e.reshape(chunk // 8, 8, cols), axis=0)
            out = out + dot(value_rows_ref[head, :, rows], e.astype(BF))
            return next_top, total, out

        next_top, total, out = lax.fori_loop(
            0, chunks, body, (lowest, jnp.zeros((8, cols), F32), jnp.zeros((48, cols), F32))
        )
        total = jnp.sum(total, axis=0, keepdims=True)
        g = g_t_ref[
            pl.ds(pl.multiple_of(head * HEAD_DIM, HEAD_DIM), HEAD_DIM),
            pl.ds(pl.multiple_of(lax.rem(n, tiles) * cols, cols), cols),
        ].astype(F32)
        weighted = jnp.sum(out[:HEAD_DIM] * g, axis=0, keepdims=True)
        rounded_total = out[HEAD_DIM : HEAD_DIM + 1]
        row = lax.broadcasted_iota(jnp.int32, (8, cols), 0)
        tile = jnp.where(
            row == 0, top, jnp.where(row == 1, total, jnp.where(row == 2, weighted, rounded_total))
        )
        for part in range(cols // 128):
            out_ref[n * (cols // 128) + part] = tile[:, part * 128 : (part + 1) * 128]
        return next_top

    lax.fori_loop(0, HEADS * tiles, per_tile, first)


def local_stats(keys, aux, value_rows, q_t, g_t, bias_rows):
    points, latents = keys.shape[0], q_t.shape[1]
    cols = min(256, latents)
    return pl.pallas_call(
        stats_kernel,
        out_shape=jax.ShapeDtypeStruct((HEADS * latents // 128, 8, 128), F32),
        in_specs=vmem_specs(6),
        out_specs=pl.BlockSpec(memory_space=pltpu.VMEM),
        scratch_shapes=[
            pltpu.VMEM((points, 2 * WIDTH), BF),
            pltpu.VMEM((HEADS * latents // cols, 2 * WIDTH, cols), BF),
            pltpu.VMEM((2, points, cols), F32),
        ],
        compiler_params=pltpu.CompilerParams(vmem_limit_bytes=VMEM_BYTES),
    )(keys, aux, value_rows, q_t, g_t, bias_rows)


def enter(axis, me, count):
    barrier = pltpu.get_barrier_semaphore()

    def greet(k, unused):
        pl.semaphore_signal(
            barrier, inc=1, device_id={axis: lax.rem(me + k, count)}, device_id_type=MESH
        )
        return unused

    lax.fori_loop(1, count, greet, 0)
    return barrier


def combine_kernel(count, stats_ref, out_ref, arrived, mine, final, sent_1, got_1, sent_2, got_2):
    me = lax.axis_index("pts")
    share = stats_ref.shape[0] // count
    barrier = enter("pts", me, count)
    pl.semaphore_wait(barrier, count - 1)

    def piece(k):
        there = lax.rem(me + k, count)
        return pltpu.make_async_remote_copy(
            src_ref=stats_ref.at[pl.ds(there * share, share)],
            dst_ref=arrived.at[me],
            send_sem=sent_1.at[k],
            recv_sem=got_1.at[k],
            device_id={"pts": there},
            device_id_type=MESH,
        )

    def result(k):
        there = lax.rem(me + k, count)
        return pltpu.make_async_remote_copy(
            src_ref=mine,
            dst_ref=final.at[me],
            send_sem=sent_2.at[k],
            recv_sem=got_2.at[k],
            device_id={"pts": there},
            device_id_type=MESH,
        )

    def every(action):
        def step(k, unused):
            action(k)
            return unused

        lax.fori_loop(1, count, step, 0)

    every(lambda k: piece(k).start())
    arrived[me] = stats_ref[pl.ds(me * share, share)]
    every(lambda k: piece(k).wait_recv())
    for part in range(share):
        top = arrived[:, part, 0, :]
        best = jnp.max(top, axis=0, keepdims=True)
        weight = jnp.exp2(top - best)
        total = jnp.sum(weight * arrived[:, part, 1, :], axis=0, keepdims=True)
        weighted = jnp.sum(weight * arrived[:, part, 2, :], axis=0, keepdims=True)
        rounded_total = jnp.sum(weight * arrived[:, part, 3, :], axis=0, keepdims=True)
        offset = (best + jnp.log(total) * LOG2E) * (-1.0 / TO_LOG2)
        row = lax.broadcasted_iota(jnp.int32, (8, 128), 0)
        mine[part] = jnp.where(row == 0, offset, -(weighted / rounded_total))
    every(lambda k: result(k).start())
    final[me] = mine[...]
    every(lambda k: result(k).wait_recv())
    out_ref[...] = final[...].reshape(out_ref.shape)
    every(lambda k: piece(k).wait_send())
    every(lambda k: result(k).wait_send())


def combined_stats(stats, count):
    share = stats.shape[0] // count
    return pl.pallas_call(
        functools.partial(combine_kernel, count),
        out_shape=jax.ShapeDtypeStruct(stats.shape, F32),
        in_specs=vmem_specs(1),
        out_specs=pl.BlockSpec(memory_space=pltpu.VMEM),
        scratch_shapes=[
            pltpu.VMEM((count, share, 8, 128), F32),
            pltpu.VMEM((share, 8, 128), F32),
            pltpu.VMEM((count, share, 8, 128), F32),
            pltpu.SemaphoreType.DMA((count,)),
            pltpu.SemaphoreType.DMA((count,)),
            pltpu.SemaphoreType.DMA((count,)),
            pltpu.SemaphoreType.DMA((count,)),
        ],
        compiler_params=pltpu.CompilerParams(collective_id=0, has_side_effects=True),
    )(stats)


def grads_kernel(
    keys_ref,
    values_ref,
    aux_ref,
    onehot_t_ref,
    k_t_ref,
    q_t_ref,
    g_t_ref,
    latents_ref,
    grad_out_ref,
    bias_rows_ref,
    stats_ref,
    grad_k_ref,
    grad_v_ref,
    grad_q_ref,
    bias_ref,
    k_aux,
    v_aux,
    k_t,
    onehot_t,
    q_feat,
    g_feat,
    q_stack,
    g_stack,
    probs,
    scaled,
    row_sums,
    part_sum,
    from_ring,
    from_z,
    grad_q_t,
    sent,
    got,
    sent_z,
    got_z,
):
    points, latents = keys_ref.shape[0], q_t_ref.shape[1]
    block = points // (2 * YS)
    half = block // 2
    cols = q_feat.shape[2]
    chunks = latents // cols

    lat = lax.axis_index("lat")
    z, y = lat // YS, lax.rem(lat, YS)
    up = z * YS + lax.rem(y + 1, YS)
    down = z * YS + lax.rem(y + YS - 1, YS)
    across = (1 - z) * YS + y

    barrier = pltpu.get_barrier_semaphore()
    for other in (up, down, across):
        pl.semaphore_signal(barrier, inc=1, device_id={"lat": other}, device_id_type=MESH)

    lane = lax.broadcasted_iota(jnp.int32, (latents, WIDTH), 1)
    row16 = lax.broadcasted_iota(jnp.int32, (16, 128), 0)
    for h in range(HEADS):
        mine = (lane >= h * HEAD_DIM) & (lane < (h + 1) * HEAD_DIM)
        for source, stack in ((latents_ref, q_stack), (grad_out_ref, g_stack)):
            stack[h * latents : (h + 1) * latents, :] = jnp.where(
                mine, source[...].astype(F32), 0.0
            ).astype(BF)
        for c in range(chunks):
            n = h * chunks + c
            here = slice(c * cols, (c + 1) * cols)
            for source, feat in ((q_t_ref, q_feat), (g_t_ref, g_feat)):
                feat[n] = jnp.zeros((2 * WIDTH, cols), BF)
                feat[n, h * HEAD_DIM : (h + 1) * HEAD_DIM, :] = source[
                    h * HEAD_DIM : (h + 1) * HEAD_DIM, here
                ]
            q_feat[n, WIDTH : WIDTH + ONES_ROW, :] = bias_rows_ref[h, :ONES_ROW, here]
            for part in range(cols // 128):
                tile = stats_ref[(h * latents + c * cols) // 128 + part]
                for index, feat in ((0, q_feat), (1, g_feat)):
                    hi, mid, low = three_pieces(tile[index : index + 1, :])
                    feat[n, WIDTH + ONES_ROW : WIDTH + ONES_ROW + 16, part * 128 : (part + 1) * 128] = (
                        jnp.where(
                            row16 == 0,
                            hi.astype(F32),
                            jnp.where(
                                row16 == 1,
                                mid.astype(F32),
                                jnp.where(row16 == 2, low.astype(F32), 0.0),
                            ),
                        ).astype(BF)
                    )
    grad_q_t[...] = jnp.zeros_like(grad_q_t)
    bias_ref[...] = jnp.zeros_like(bias_ref)
    lane_row = lax.broadcasted_iota(jnp.int32, (block, 128), 1)

    def compute(step, at_up, at_down):
        for row, at in ((0, at_up), (half, at_down)):
            source = pl.ds(pl.multiple_of(at, half), half)
            rows = pl.ds(row, half)
            k_aux[rows, :WIDTH] = keys_ref[source, :]
            k_aux[rows, WIDTH:] = aux_ref[source, :]
            v_aux[rows, :WIDTH] = values_ref[source, :]
            v_aux[rows, WIDTH:] = aux_ref[source, :]
            k_t[:, row : row + half] = k_t_ref[:, source]
            onehot_t[:, row : row + half] = onehot_t_ref[:, source]
        row_sums[...] = jnp.zeros_like(row_sums)

        def per_chunk(n, unused):
            s = dot(k_aux[...], q_feat[n])
            o = dot(v_aux[...], g_feat[n])
            p = jnp.exp2(s * TO_LOG2)
            score_grad = p * o
            where = pl.ds(pl.multiple_of(n * cols, cols), cols)
            probs[:, where] = p.astype(BF)
            scaled[:, where] = (score_grad * SCALE).astype(BF)
            folded = score_grad[:, :128]
            for part in range(1, cols // 128):
                folded = folded + score_grad[:, part * 128 : (part + 1) * 128]
            row_sums[...] += jnp.where(
                lane_row == n // chunks, jnp.sum(folded, axis=1, keepdims=True), 0.0
            )
            return unused

        lax.fori_loop(0, HEADS * chunks, per_chunk, 0)
        part_sum[step, :, :WIDTH] = dot(scaled[...], q_stack[...])
        part_sum[step, :, WIDTH:] = dot(probs[...], g_stack[...])
        for h in range(HEADS):
            grad_q_t[h * HEAD_DIM : (h + 1) * HEAD_DIM, :] += dot(
                k_t[h * HEAD_DIM : (h + 1) * HEAD_DIM, :], scaled[:, h * latents : (h + 1) * latents]
            )
        for piece in three_pieces(row_sums[...]):
            bias_ref[...] += dot(onehot_t[...], piece)

    def ring(step, upwards):
        rows = pl.ds(0, half) if upwards else pl.ds(half, half)
        return pltpu.make_async_remote_copy(
            src_ref=part_sum.at[step, rows],
            dst_ref=from_ring.at[step, rows],
            send_sem=sent.at[step, 0 if upwards else 1],
            recv_sem=got.at[step, 0 if upwards else 1],
            device_id={"lat": up if upwards else down},
            device_id_type=MESH,
        )

    over = pltpu.make_async_remote_copy(
        src_ref=part_sum.at[YS - 1],
        dst_ref=from_z,
        send_sem=sent_z,
        recv_sem=got_z,
        device_id={"lat": across},
        device_id_type=MESH,
    )

    def per_step(step, unused):
        turn = lax.rem(step, YS)
        owner_z = jnp.where(step < YS, 1 - z, z)
        y_up = lax.rem(y + 2 * YS - 1 - turn, YS)
        y_down = lax.rem(y + 1 + turn, YS)
        compute(
            step,
            (owner_z * YS + y_up) * block,
            (owner_z * YS + y_down) * block + half,
        )

        @pl.when(step == 0)
        def _():
            pl.semaphore_wait(barrier, 3)

        @pl.when(turn > 0)
        def _():
            for upwards in (True, False):
                ring(step - 1, upwards).wait_recv()
            part_sum[step] += from_ring[step - 1]

        @pl.when(turn < YS - 1)
        def _():
            for upwards in (True, False):
                ring(step, upwards).start()

        @pl.when(step == YS - 1)
        def _():
            over.start()

        return unused

    lax.fori_loop(0, 2 * YS, per_step, 0)
    grad_q_ref[...] = grad_q_t[...].T
    over.wait_recv()
    done = part_sum[2 * YS - 1] + from_z[...]
    grad_k_ref[...] = done[:, :WIDTH]
    grad_v_ref[...] = done[:, WIDTH:]
    for step in range(2 * YS):
        if step % YS < YS - 1:
            for upwards in (True, False):
                ring(step, upwards).wait_send()
    over.wait_send()


def gradients(*args):
    keys, q_t = args[0], args[5]
    points, latents = keys.shape[0], q_t.shape[1]
    block = points // (2 * YS)
    cols = min(512, latents)
    return pl.pallas_call(
        grads_kernel,
        out_shape=[
            jax.ShapeDtypeStruct((block, WIDTH), F32),
            jax.ShapeDtypeStruct((block, WIDTH), F32),
            jax.ShapeDtypeStruct((latents, WIDTH), F32),
            jax.ShapeDtypeStruct((SWEEPS, 128), F32),
        ],
        in_specs=vmem_specs(len(args)),
        out_specs=vmem_specs(4),
        scratch_shapes=[
            pltpu.VMEM((block, 2 * WIDTH), BF),
            pltpu.VMEM((block, 2 * WIDTH), BF),
            pltpu.VMEM((WIDTH, block), BF),
            pltpu.VMEM((SWEEPS, block), BF),
            pltpu.VMEM((HEADS * latents // cols, 2 * WIDTH, cols), BF),
            pltpu.VMEM((HEADS * latents // cols, 2 * WIDTH, cols), BF),
            pltpu.VMEM((HEADS * latents, WIDTH), BF),
            pltpu.VMEM((HEADS * latents, WIDTH), BF),
            pltpu.VMEM((block, HEADS * latents), BF),
            pltpu.VMEM((block, HEADS * latents), BF),
            pltpu.VMEM((block, 128), F32),
            pltpu.VMEM((2 * YS, block, 2 * WIDTH), F32),
            pltpu.VMEM((2 * YS, block, 2 * WIDTH), F32),
            pltpu.VMEM((block, 2 * WIDTH), F32),
            pltpu.VMEM((WIDTH, latents), F32),
            pltpu.SemaphoreType.DMA((2 * YS, 2)),
            pltpu.SemaphoreType.DMA((2 * YS, 2)),
            pltpu.SemaphoreType.DMA,
            pltpu.SemaphoreType.DMA,
        ],
        compiler_params=pltpu.CompilerParams(
            collective_id=1, has_side_effects=True, vmem_limit_bytes=VMEM_BYTES
        ),
    )(*args)


def final_kernel(
    count, lats, grad_q_ref, bias_ref, out_ref, bias_out_ref, arrived, by_lat, by_pts, mine,
    sent_q, got_q, sent_l, got_l, sent_p, got_p,
):
    me, lat = lax.axis_index("pts"), lax.axis_index("lat")
    rows = grad_q_ref.shape[0] // count
    barrier = enter("pts", me, count)
    enter("lat", lat, lats)
    pl.semaphore_wait(barrier, count - 1 + lats - 1)

    def over_pts(src, dst, sent, got, k):
        return pltpu.make_async_remote_copy(
            src_ref=src,
            dst_ref=dst,
            send_sem=sent.at[k],
            recv_sem=got.at[k],
            device_id={"pts": lax.rem(me + k, count)},
            device_id_type=MESH,
        )

    def q_copy(k):
        there = lax.rem(me + k, count)
        return over_pts(grad_q_ref.at[pl.ds(there * rows, rows)], arrived.at[me], sent_q, got_q, k)

    def bias_copy(k):
        return over_pts(mine, by_pts.at[me], sent_p, got_p, k)

    def lat_copy(k):
        return pltpu.make_async_remote_copy(
            src_ref=bias_ref,
            dst_ref=by_lat.at[lat],
            send_sem=sent_l.at[k],
            recv_sem=got_l.at[k],
            device_id={"lat": lax.rem(lat + k, lats)},
            device_id_type=MESH,
        )

    def every(stop, action):
        def step(k, unused):
            action(k)
            return unused

        lax.fori_loop(1, stop, step, 0)

    every(lats, lambda k: lat_copy(k).start())
    every(count, lambda k: q_copy(k).start())
    by_lat[lat] = bias_ref[...]
    arrived[me] = grad_q_ref[pl.ds(me * rows, rows)]
    every(lats, lambda k: lat_copy(k).wait_recv())
    mine[...] = jnp.sum(by_lat[...], axis=0)
    every(count, lambda k: bias_copy(k).start())
    by_pts[me] = mine[...]
    every(count, lambda k: q_copy(k).wait_recv())
    out_ref[...] = jnp.sum(arrived[...], axis=0)
    every(count, lambda k: bias_copy(k).wait_recv())
    bias_out_ref[...] = jnp.sum(by_pts[...], axis=0)
    every(lats, lambda k: lat_copy(k).wait_send())
    every(count, lambda k: q_copy(k).wait_send())
    every(count, lambda k: bias_copy(k).wait_send())


def final_sums(grad_q, bias, count, lats):
    rows = grad_q.shape[0] // count
    return pl.pallas_call(
        functools.partial(final_kernel, count, lats),
        out_shape=[
            jax.ShapeDtypeStruct((rows, WIDTH), F32),
            jax.ShapeDtypeStruct((SWEEPS, 128), F32),
        ],
        in_specs=vmem_specs(2),
        out_specs=vmem_specs(2),
        scratch_shapes=[
            pltpu.VMEM((count, rows, WIDTH), F32),
            pltpu.VMEM((lats, SWEEPS, 128), F32),
            pltpu.VMEM((count, SWEEPS, 128), F32),
            pltpu.VMEM((SWEEPS, 128), F32),
            pltpu.SemaphoreType.DMA((count,)),
            pltpu.SemaphoreType.DMA((count,)),
            pltpu.SemaphoreType.DMA((lats,)),
            pltpu.SemaphoreType.DMA((lats,)),
            pltpu.SemaphoreType.DMA((count,)),
            pltpu.SemaphoreType.DMA((count,)),
        ],
        compiler_params=pltpu.CompilerParams(collective_id=2, has_side_effects=True),
    )(grad_q, bias)


def per_device(count, lats, latents, keys, values, sweep, sweep_bias, grad_out):
    rows, points = latents.shape[0], keys.shape[0]
    swept = sweep[:, None]
    column = jnp.arange(WIDTH, dtype=jnp.int32)[None, :]
    marked = (column < ONES_ROW) & (lax.rem(column, SWEEPS) == swept)
    aux = (marked | ((column >= ONES_ROW) & (column < ONES_ROW + 3))).astype(BF)
    onehot_t = (jnp.arange(SWEEPS, dtype=jnp.int32)[:, None] == sweep[None, :]).astype(BF)
    k_t, q_t, g_t = keys.T, latents.T, grad_out.T
    ones_rows = jnp.zeros((HEADS, 16, points), BF).at[:, 0].set(1.0)
    value_rows = jnp.concatenate([values.T.reshape(HEADS, HEAD_DIM, points), ones_rows], axis=1)
    raw = sweep_bias / SCALE
    hi = lax.reduce_precision(raw, 8, 7)
    mid = lax.reduce_precision(raw - hi, 8, 7)
    low = raw - hi - mid
    pieces = jnp.concatenate([hi, mid, low, jnp.zeros((HEADS, 16), F32)], axis=1).astype(BF)
    bias_rows = jnp.broadcast_to(pieces[:, :, None], (HEADS, 64, rows))

    stats = local_stats(keys, aux, value_rows, q_t, g_t, bias_rows)
    stats = combined_stats(stats, count)
    grad_k, grad_v, grad_q, bias = gradients(
        keys, values, aux, onehot_t, k_t, q_t, g_t, latents, grad_out, bias_rows, stats
    )
    grad_q, bias = final_sums(grad_q, bias, count, lats)
    return grad_q, grad_k, grad_v, bias[:, :HEADS].T


def solution(mesh):
    return jax.shard_map(
        functools.partial(per_device, mesh.shape["pts"], mesh.shape["lat"]),
        mesh=mesh,
        in_specs=(P("lat", None), P("pts", None), P("pts", None), P("pts"), P(), P("lat", None)),
        out_specs=(P(("lat", "pts"), None), P(("pts", "lat"), None), P(("pts", "lat"), None), P()),
        check_vma=False,
    )
```

time: 815 us -> 200 us (0.25)
  blocking collectives: 374 us -> 0 us
  matrix products: 185 us -> 0 us
  Pallas kernels: 0 us -> 182 us
  waiting for transfers between devices: 162 us -> 0 us
  local copies, waits for them, and re-layouts: 57.3 us -> 10.6 us
  between operations: 14.1 us -> 0.72 us
    psum x2 -> x0, blocking collectives: 239 us -> none  [the longest x1 133 us: per_device(): totals, weighted = lax.psum((local_totals, local_weighted), 'pts')]
    dot_general x192 -> x0, matrix products: 185 us -> none  [the longest x48 65.5 us: score_tile(): jnp.einsum('rhd,chd->hrc', heads_of(query_block), heads_of(key_block), pr...]
    pallas_call x0 -> x4, Pallas kernels: none -> 182 us  [the longest x1 65.6 us: gradients(): pl.pallas_call(grads_kernel, out_shape=[jax.ShapeDtypeStruct((block, WIDT...]
    reduce_scatter x2 -> x0, waiting for transfers between devices: 162 us -> none  [the longest x1 137 us: per_device(): lax.psum_scatter(grad_blocks.reshape(query_count, feature_width), 'pts',...]
    pmax x1 -> x0, blocking collectives: 135 us -> none  [per_device(): row_top = lax.pmax(local_top, 'pts')]
    dynamic_slice x112 -> x0, local copies, waits for them, and re-layouts: 30.9 us -> none  [block_max(): running, unused = lax.scan(inner, lowest, key_data)]
    dynamic_update_slice x42 -> x0, local copies, waits for them, and re-layouts: 17 us -> none  [the longest x32 16.7 us: per_query(): grad_q, (kv_parts, bias_parts) = lax.scan(per_key, start_q, key_data)]
    add x36 -> x0, other arithmetic: 12.2 us -> none  [the longest x2 10.7 us: per_query(): carried[0] + kv_parts.reshape(key_count, 2 * feature_width)]
  transfers between devices with their start and end apart: 2 -> 0, of which waited for: 2 -> 0; matrix products, arithmetic and copies ran while one was open for 0% -> 0% of each run, Pallas kernels for 0% -> 0%
where the time goes in v1:
time: 200 us; the launch traced here: 199 us
  Pallas kernels  182 us (91%)
  local copies, waits for them, and re-layouts  10.6 us (5%)
  other arithmetic  6.04 us (3%)
    pallas_call x1, Pallas kernels, gradients(): pl.pallas_call(grads_kernel, out_shape=[jax.ShapeDtypeStruct((block, WIDT...  65.6 us
    pallas_call x1, Pallas kernels, local_stats(): pl.pallas_call(stats_kernel, out_shape=jax.ShapeDtypeStruct((HEADS * late...  64.4 us
    pallas_call x1, Pallas kernels, final_sums(): pl.pallas_call(functools.partial(final_kernel, count, lats), out_shape=[j...  29.5 us
    pallas_call x1, Pallas kernels, combined_stats(): pl.pallas_call(functools.partial(combine_kernel, count), out_shape=jax.Sh...  22.6 us
    unnamed x19, local copies, waits for them, and re-layouts  8.35 us

profile of v1, /device:TPU:1, one launch (start us, length us, event | category | flops | bytes accessed | tf_op | source)
XLA Modules:
  0.0 199.4 jit_solution(18029848031572274986)
XLA Ops:
  0.6 0.0 copy-start.2
  0.6 0.0 copy-start.3
  0.7 0.0 copy-start.1
  0.7 0.8 reduce-precision_convert_fusion.1
  1.5 0.1 pad.7.clone
  1.6 0.1 maximum_maximum_fusion
  1.6 0.9 broadcast_in_dim.5.bias_rows_ref
  2.6 3.2 %or_convert_fusion.aux_ref = bf16[4096,128]{1,0:T(8,128)(2,1)} fusion(s32[128]{0:T(128)S(1)} %iota_and_fusion, s32[4096]{0:T(1024)} %param.11, pred[128]{0:T(512)(128)(4,1)S(1)} %get-tuple-element.35, pred[128]{0:T(512)(128)(4,1)S(1)} %get-tuple-element.36), kind=kLoop, calls=%fused_computation | loop fusion | flops 2097152 | bytes 1065728 | tf_op jit(solution)/shard_map/convert_element_type | solution.py:538
  5.8 0.0 copy-done.2
  5.8 0.0 copy-start.4
  5.8 0.8 copy.11
  6.6 0.0 copy-done.3
  6.6 0.8 copy.12
  7.5 0.0 copy-done.1
  7.5 0.5 copy.13
  8.0 0.0 copy-done.4
  8.0 1.3 pad_maximum_fusion.value_rows_ref
  9.3 0.0 copy-start
  9.3 64.4 %shard_map.93.stats_ref = f32[32,8,128]{2,1,0:T(8,128)} custom-call(bf16[4096,128]{1,0:T(8,128)(2,1)} %keys_ref.3, bf16[4096,128]{1,0:T(8,128)(2,1)} %or_convert_fusion.aux_ref, bf16[4,48,4096]{2,1,0:T(8,128)(2,1)} %pad_maximum_fusion.value_rows_ref, bf16[128,1024]{1,0:T(8,128)(2,1)} %bitcast.10, bf16[128,1024]{1,0:T(8,128)(2,1)} %bitcast.12, ...), custom_call_target="tpu_custom_call" | custom-call | tf_op jit(solution)/shard_map/pallas_call | solution.py:110
  73.7 0.0 copy-start.5
  73.7 22.6 %shard_map.94.stats_ref = f32[32,8,128]{2,1,0:T(8,128)} custom-call(f32[32,8,128]{2,1,0:T(8,128)} %shard_map.93.stats_ref), custom_call_target="tpu_custom_call" | custom-call | tf_op jit(solution)/shard_map/pallas_call | solution.py:195
  96.3 0.0 copy-done
  96.3 1.3 copy.10
  97.6 0.0 copy-done.5
  97.6 0.7 fusion.onehot_t_ref
  98.3 65.6 %shard_map.95 = (f32[512,128]{1,0:T(8,128)}, f32[512,128]{1,0:T(8,128)}, f32[1024,128]{1,0:T(8,128)}, f32[16,128]{1,0:T(8,128)}) custom-call(bf16[4096,128]{1,0:T(8,128)(2,1)} %keys_ref.3, bf16[4096,128]{1,0:T(8,128)(2,1)} %values_ref.1, bf16[4096,128]{1,0:T(8,128)(2,1)} %or_convert_fusion.aux_ref, bf16[16,4096]{1,0:T(8,128)(2,1)} %fusion.onehot_t_ref, ...), custom_call_target="tpu_custom_call" | custom-call | tf_op jit(solution)/shard_map/pallas_call | solution.py:409
  163.9 29.5 %shard_map.96 = (f32[32,128]{1,0:T(8,128)}, f32[16,128]{1,0:T(8,128)}) custom-call(f32[1024,128]{1,0:T(8,128)} %get-tuple-element.22.grad_q_ref, f32[16,128]{1,0:T(8,128)} %get-tuple-element.23.bias_ref), custom_call_target="tpu_custom_call" | custom-call | tf_op jit(solution)/shard_map/pallas_call | solution.py:509
  193.4 0.7 slice_bitcast_fusion
  194.1 0.7 copy.14
  194.8 1.3 copy.18
  196.1 1.7 copy.19
  197.8 1.7 copy.20
  (3 shorter events, 0.0 us)
Async XLA Ops:
  0.6 5.2 %copy-start.2 = (bf16[1024,128]{1,0:T(8,128)(2,1)S(1)}, bf16[1024,128]{1,0:T(8,128)(2,1)}, u32[]{:S(2)}) copy-start(bf16[1024,128]{1,0:T(8,128)(2,1)} %latents_ref.1) | copy-start | bytes 786436
  0.6 6.0 %copy-start.3 = (bf16[1024,128]{1,0:T(8,128)(2,1)S(1)}, bf16[1024,128]{1,0:T(8,128)(2,1)}, u32[]{:S(2)}) copy-start(bf16[1024,128]{1,0:T(8,128)(2,1)} %grad_out_ref.1) | copy-start | bytes 786436
  0.7 6.8 %copy-start.1 = (bf16[4096,128]{1,0:T(8,128)(2,1)S(1)}, bf16[4096,128]{1,0:T(8,128)(2,1)}, u32[]{:S(2)}) copy-start(bf16[4096,128]{1,0:T(8,128)(2,1)} %values_ref.1) | copy-start | bytes 3145732
  5.8 2.2 %copy-start.4 = (bf16[4,16,4096]{2,1,0:T(8,128)(2,1)S(1)}, bf16[4,16,4096]{2,1,0:T(8,128)(2,1)}, u32[]{:S(2)}) copy-start(bf16[4,16,4096]{2,1,0:T(8,128)(2,1)} %constant.44.clone.1) | copy-start | bytes 1572868
  9.3 87.0 %copy-start = (bf16[4096,128]{1,0:T(8,128)(2,1)S(1)}, bf16[4096,128]{1,0:T(8,128)(2,1)}, u32[]{:S(2)}) copy-start(bf16[4096,128]{1,0:T(8,128)(2,1)} %keys_ref.3) | copy-start | bytes 3145732
  73.7 23.9 %copy-start.5 = (s32[4096]{0:T(1024)S(1)}, s32[4096]{0:T(1024)}, u32[]{:S(2)}) copy-start(s32[4096]{0:T(1024)} %param.11) | copy-start | bytes 49156

commit v2 on v0

v2 whole, which is shorter than its diff:
```python
import functools
import math

import jax
import jax.numpy as jnp
from jax import lax
from jax.experimental import pallas as pl
from jax.experimental.pallas import tpu as pltpu
from jax.sharding import PartitionSpec as P

HEADS = 4
HEAD_DIM = 32
WIDTH = HEADS * HEAD_DIM
SWEEPS = 16
SCALE = HEAD_DIM**-0.5
LOG2E = math.log2(math.e)
TO_LOG2 = SCALE * LOG2E
YS = 4
ONES_ROW = 3 * SWEEPS
BF = jnp.bfloat16
F32 = jnp.float32
MESH = pl.DeviceIdType.MESH
VMEM_BYTES = 56 * 1024 * 1024


def dot(a, b):
    return jnp.dot(a, b, preferred_element_type=F32)


def three_pieces(x):
    hi = x.astype(BF)
    rest = x - hi.astype(F32)
    mid = rest.astype(BF)
    low = (rest - mid.astype(F32)).astype(BF)
    return hi, mid, low


def vmem_specs(count):
    return [pl.BlockSpec(memory_space=pltpu.VMEM)] * count


def whole_kernel(
    count,
    lats,
    latents_ref,
    keys_ref,
    values_ref,
    sweep_ref,
    sweep_bias_ref,
    grad_out_ref,
    grad_k_ref,
    grad_v_ref,
    small_ref,
    k_aux,
    value_rows,
    onehot_t,
    g_t,
    q_feat,
    g_feat,
    q_stack,
    g_stack,
    scores_0,
    scores_1,
    stats,
    arrived,
    mine,
    final,
    k_stage,
    v_stage,
    probs,
    scaled,
    part_sum,
    from_ring,
    from_z,
    grad_q_t,
    bias_sum,
    q_parts,
    from_core,
    by_lat,
    q_mine,
    by_chip,
    sent_1,
    got_1,
    sent_2,
    got_2,
    sent_ring,
    got_ring,
    sent_z,
    got_z,
    sent_core,
    got_core,
    sent_bias,
    got_bias,
    sent_chip,
    got_chip,
):
    points, latents = keys_ref.shape[0], latents_ref.shape[0]
    span = latents // 2
    cols = min(256, span)
    per_span = span // cols
    tiles = HEADS * 2 * per_span
    pairs = tiles // 2
    chunk = min(512, points)
    chunks = points // chunk
    block = points // (2 * YS)
    half = block // 2
    chips = count // 2
    share = stats.shape[0] // count
    rows_out = latents // count

    me = lax.axis_index("pts")
    lat = lax.axis_index("lat")
    core = lax.rem(me, 2)
    chip = me // 2
    z, y = lat // YS, lax.rem(lat, YS)
    up = z * YS + lax.rem(y + 1, YS)
    down = z * YS + lax.rem(y + YS - 1, YS)
    across = (1 - z) * YS + y

    def every(start, stop, action):
        def step(k, unused):
            action(k)
            return unused

        lax.fori_loop(start, stop, step, 0)

    def others(start, stop, action):
        def guarded(k):
            @pl.when(k != me)
            def _():
                action(k)

        every(start, stop, guarded)

    barrier = pltpu.get_barrier_semaphore()

    def bias_peer(k):
        there = lax.rem(lat * 2 + core + k, 2 * lats)
        return {"pts": chip * 2 + lax.rem(there, 2), "lat": there // 2}

    def greet_pts(k):
        pl.semaphore_signal(
            barrier, inc=1, device_id={"pts": lax.rem(me + k, count)}, device_id_type=MESH
        )

    def greet_lat(k):
        pl.semaphore_signal(barrier, inc=1, device_id=bias_peer(k), device_id_type=MESH)

    every(1, count, greet_pts)
    every(1, 2 * lats, greet_lat)

    k_aux[:, :WIDTH] = keys_ref[...]

    def build(c):
        rows = pl.ds(pl.multiple_of(c * chunk, chunk), chunk)
        swept = sweep_ref[:, rows]
        row = lax.broadcasted_iota(jnp.int32, (WIDTH, chunk), 0)
        marked = (row < ONES_ROW) & (lax.rem(row, SWEEPS) == swept)
        ones = (row >= ONES_ROW) & (row < ONES_ROW + 3)
        aux_t = jnp.where(marked | ones, 1.0, 0.0)
        onehot_t[:, rows] = aux_t[:SWEEPS].astype(BF)
        k_aux[rows, WIDTH:] = aux_t.T.astype(BF)
        value_t = values_ref[rows, :].T
        for h in range(HEADS):
            value_rows[h, :HEAD_DIM, rows] = value_t[h * HEAD_DIM : (h + 1) * HEAD_DIM, :]
            value_rows[h, HEAD_DIM:, rows] = jnp.where(row[:16] == 0, 1.0, 0.0).astype(BF)

    every(0, chunks, build)
    q_t = latents_ref[...].T
    g_t[...] = grad_out_ref[...].T
    lane = lax.broadcasted_iota(jnp.int32, (span, WIDTH), 1)
    eye = lax.broadcasted_iota(jnp.int32, (SWEEPS, SWEEPS), 0) == lax.broadcasted_iota(
        jnp.int32, (SWEEPS, SWEEPS), 1
    )
    for h in range(HEADS):
        rows = slice(h * HEAD_DIM, (h + 1) * HEAD_DIM)
        column = jnp.sum(
            jnp.where(eye, sweep_bias_ref[h : h + 1, :], 0.0), axis=1, keepdims=True
        ) * (1.0 / SCALE)
        bias_pieces = three_pieces(jnp.broadcast_to(column, (SWEEPS, span)))
        mine_lanes = (lane >= h * HEAD_DIM) & (lane < (h + 1) * HEAD_DIM)
        for s in range(2):
            n = s * HEADS + h
            here = slice(s * span, (s + 1) * span)
            for source, stack in ((latents_ref, q_stack), (grad_out_ref, g_stack)):
                stack[n] = jnp.where(mine_lanes, source[here, :].astype(F32), 0.0).astype(BF)
            q_feat[n] = jnp.zeros((2 * WIDTH, span), BF)
            g_feat[n] = jnp.zeros((2 * WIDTH, span), BF)
            q_feat[n, rows, :] = q_t[rows, here]
            g_feat[n, rows, :] = g_t[rows, here]
            for index, piece in enumerate(bias_pieces):
                q_feat[n, WIDTH + index * SWEEPS : WIDTH + (index + 1) * SWEEPS, :] = piece
    grad_q_t[...] = jnp.zeros_like(grad_q_t)
    bias_sum[...] = jnp.zeros_like(bias_sum)
    pl.semaphore_wait(barrier, count - 1 + 2 * lats - 1)

    def piece(owner):
        return pltpu.make_async_remote_copy(
            src_ref=stats.at[pl.ds(owner * share, share)],
            dst_ref=arrived.at[me],
            send_sem=sent_1.at[owner],
            recv_sem=got_1.at[me],
            device_id={"pts": owner},
            device_id_type=MESH,
        )

    def piece_from(source):
        return pltpu.make_async_remote_copy(
            src_ref=mine,
            dst_ref=arrived.at[source],
            send_sem=sent_1.at[source],
            recv_sem=got_1.at[source],
            device_id={"pts": source},
            device_id_type=MESH,
        )

    def result(there):
        return pltpu.make_async_remote_copy(
            src_ref=mine,
            dst_ref=final.at[me],
            send_sem=sent_2.at[there],
            recv_sem=got_2.at[me],
            device_id={"pts": there},
            device_id_type=MESH,
        )

    def result_from(owner):
        return pltpu.make_async_remote_copy(
            src_ref=mine,
            dst_ref=final.at[owner],
            send_sem=sent_2.at[owner],
            recv_sem=got_2.at[owner],
            device_id={"pts": owner},
            device_id_type=MESH,
        )

    def owners(s):
        return s * (count // 2), (s + 1) * (count // 2)

    def send_pieces(s):
        others(*owners(s), lambda k: piece(k).start())

    def combine(s):
        first, last = owners(s)

        @pl.when((me >= first) & (me < last))
        def _():
            arrived[me] = stats[pl.ds(me * share, share)]
            others(0, count, lambda k: piece_from(k).wait_recv())
            for part in range(share):
                top = arrived[:, part, 0, :]
                best = jnp.max(top, axis=0, keepdims=True)
                weight = jnp.exp2(top - best)
                total = jnp.sum(weight * arrived[:, part, 1, :], axis=0, keepdims=True)
                weighted = jnp.sum(weight * arrived[:, part, 2, :], axis=0, keepdims=True)
                rounded_total = jnp.sum(weight * arrived[:, part, 3, :], axis=0, keepdims=True)
                offset = (best + jnp.log(total) * LOG2E) * (-1.0 / TO_LOG2)
                row = lax.broadcasted_iota(jnp.int32, (8, 128), 0)
                mine[part] = jnp.where(row == 0, offset, -(weighted / rounded_total))
            others(0, count, lambda k: result(k).start())
            final[me] = mine[...]

    def take_results(s):
        others(*owners(s), lambda k: result_from(k).wait_recv())
        row16 = lax.broadcasted_iota(jnp.int32, (16, 128), 0)
        per_tile = cols // 128
        for n in range(tiles // 2):
            it, h = n // HEADS, n % HEADS
            for part in range(per_tile):
                number = s * (tiles // 2) * per_tile + n * per_tile + part
                tile = final[number // share, number % share]
                left = it * cols + part * 128
                for index, feat in ((0, q_feat), (1, g_feat)):
                    hi, mid, low = three_pieces(tile[index : index + 1, :])
                    feat[
                        s * HEADS + h,
                        WIDTH + ONES_ROW : WIDTH + ONES_ROW + 16,
                        left : left + 128,
                    ] = jnp.where(
                        row16 == 0,
                        hi.astype(F32),
                        jnp.where(
                            row16 == 1, mid.astype(F32), jnp.where(row16 == 2, low.astype(F32), 0.0)
                        ),
                    ).astype(BF)

    lowest = jnp.full((32, cols), -jnp.inf, F32)

    def feature_of(n):
        it = n // HEADS
        return (
            (it // per_span) * HEADS + lax.rem(n, HEADS),
            pl.ds(pl.multiple_of(lax.rem(it, per_span) * cols, cols), cols),
        )

    def score_chunk(n, into, c, top):
        index, lanes = feature_of(n)
        rows = pl.ds(c * chunk, chunk)
        s = dot(k_aux[rows, :], q_feat[index, :, lanes]) * TO_LOG2
        into[rows, :] = s
        return jnp.maximum(top, jnp.max(s.reshape(chunk // 32, 32, cols), axis=0))

    def tile_sums(n, scores, top_rows, following, into):
        top = jnp.max(top_rows, axis=0, keepdims=True)
        head = lax.rem(n, HEADS)
        next_top = lowest
        total = jnp.zeros((32, cols), F32)
        out = jnp.zeros((48, cols), F32)
        for c in range(chunks):
            rows = pl.ds(c * chunk, chunk)
            e = jnp.exp2(scores[rows, :] - top)
            total = total + jnp.sum(e.reshape(chunk // 32, 32, cols), axis=0)
            out = out + dot(value_rows[head, :, rows], e.astype(BF))
            next_top = score_chunk(following, into, c, next_top)
        total = jnp.sum(total, axis=0, keepdims=True)
        g = g_t[
            pl.ds(pl.multiple_of(head * HEAD_DIM, HEAD_DIM), HEAD_DIM),
            pl.ds(pl.multiple_of((n // HEADS) * cols, cols), cols),
        ].astype(F32)
        weighted = jnp.sum(out[:HEAD_DIM] * g, axis=0, keepdims=True)
        rounded_total = out[HEAD_DIM : HEAD_DIM + 1]
        row = lax.broadcasted_iota(jnp.int32, (8, cols), 0)
        tile = jnp.where(
            row == 0, top, jnp.where(row == 1, total, jnp.where(row == 2, weighted, rounded_total))
        )
        for part in range(cols // 128):
            stats[n * (cols // 128) + part] = tile[:, part * 128 : (part + 1) * 128]
        return next_top

    first_top = lowest
    for c in range(chunks):
        first_top = score_chunk(0, scores_0, c, first_top)

    def per_pair(pair, top_rows):
        n = pair * 2
        top_rows = tile_sums(n, scores_0, top_rows, n + 1, scores_1)
        top_rows = tile_sums(n + 1, scores_1, top_rows, lax.rem(n + 2, tiles), scores_0)

        @pl.when(pair == pairs // 2 - 1)
        def _():
            send_pieces(0)

        @pl.when(pair == pairs - 2)
        def _():
            combine(0)

        return top_rows

    lax.fori_loop(0, pairs, per_pair, first_top)
    send_pieces(1)
    take_results(0)

    lane_row = lax.broadcasted_iota(jnp.int32, (block, 128), 1)

    def compute(step, s):
        turn = lax.rem(step, YS)
        owner_z = jnp.where(step < YS, 1 - z, z)
        at_up = (owner_z * YS + lax.rem(y + 2 * YS - 1 - turn, YS)) * block
        at_down = (owner_z * YS + lax.rem(y + 1 + turn, YS)) * block + half
        marks = []
        for row, at in ((0, at_up), (half, at_down)):
            source = pl.ds(pl.multiple_of(at, half), half)
            rows = pl.ds(row, half)
            k_stage[rows, :] = k_aux[source, :]
            v_stage[rows, :WIDTH] = values_ref[source, :]
            v_stage[rows, WIDTH:] = k_aux[source, WIDTH:]
            marks.append(onehot_t[:, source])
        k_t = k_stage[:, :WIDTH].T
        row_sums = jnp.zeros((block, 128), F32)
        grad_k = jnp.zeros((block, WIDTH), F32)
        grad_v = jnp.zeros((block, WIDTH), F32)
        lanes = pl.ds(pl.multiple_of(s * span, span), span)
        for h in range(HEADS):
            n = s * HEADS + h
            rows = slice(h * HEAD_DIM, (h + 1) * HEAD_DIM)
            p = jnp.exp2(dot(k_stage[...], q_feat[n]) * TO_LOG2)
            score_grad = p * dot(v_stage[...], g_feat[n])
            probs[h] = p.astype(BF)
            scaled[h] = (score_grad * SCALE).astype(BF)
            folded = score_grad[:, :128]
            for part in range(1, span // 128):
                folded = folded + score_grad[:, part * 128 : (part + 1) * 128]
            row_sums = row_sums + jnp.where(
                lane_row == h, jnp.sum(folded, axis=1, keepdims=True), 0.0
            )
            grad_v = grad_v + dot(probs[h], g_stack[n])
            grad_k = grad_k + dot(scaled[h], q_stack[n])
            grad_q_t[rows, lanes] += dot(k_t[rows, :], scaled[h])

        @pl.when(s == 0)
        def _():
            part_sum[step, :, :WIDTH] = grad_k
            part_sum[step, :, WIDTH:] = grad_v

        @pl.when(s == 1)
        def _():
            part_sum[step, :, :WIDTH] += grad_k
            part_sum[step, :, WIDTH:] += grad_v

        for piece in three_pieces(row_sums):
            for part in range(2):
                bias_sum[:SWEEPS, :] += dot(marks[part], piece[part * half : (part + 1) * half])

    def ring(step, upwards):
        rows = pl.ds(0, half) if upwards else pl.ds(half, half)
        return pltpu.make_async_remote_copy(
            src_ref=part_sum.at[step, rows],
            dst_ref=from_ring.at[step, rows],
            send_sem=sent_ring.at[step, 0 if upwards else 1],
            recv_sem=got_ring.at[step, 0 if upwards else 1],
            device_id={"lat": up if upwards else down},
            device_id_type=MESH,
        )

    over = pltpu.make_async_remote_copy(
        src_ref=part_sum.at[YS - 1],
        dst_ref=from_z,
        send_sem=sent_z,
        recv_sem=got_z,
        device_id={"lat": across},
        device_id_type=MESH,
    )

    def finish(step):
        turn = lax.rem(step, YS)

        @pl.when(turn > 0)
        def _():
            for upwards in (True, False):
                ring(step - 1, upwards).wait_recv()
            part_sum[step] += from_ring[step - 1]

        @pl.when(turn < YS - 1)
        def _():
            for upwards in (True, False):
                ring(step, upwards).start()

        @pl.when(step == YS - 1)
        def _():
            over.start()

    def per_item(t, unused):
        odd = lax.rem(t, 2)
        second = (t >= 14) | ((t >= 3) & (odd == 1))
        step = jnp.where(
            t < 3, t, jnp.where(t >= 14, t - 8, jnp.where(odd == 1, (t - 3) // 2, t // 2 + 1))
        )

        @pl.when(t == 3)
        def _():
            take_results(1)

        compute(step, jnp.where(second, 1, 0))

        @pl.when(t == 1)
        def _():
            combine(1)

        @pl.when(second & (step < 2 * YS - 1))
        def _():
            finish(step)

        return unused

    lax.fori_loop(0, 4 * YS, per_item, 0)

    swap = pltpu.make_async_remote_copy(
        src_ref=q_parts.at[1 - core],
        dst_ref=from_core,
        send_sem=sent_core,
        recv_sem=got_core,
        device_id={"pts": chip * 2 + 1 - core},
        device_id_type=MESH,
    )

    def bias_copy(k):
        return pltpu.make_async_remote_copy(
            src_ref=bias_sum.at[pl.ds(0, SWEEPS)],
            dst_ref=by_lat.at[lat * 2 + core],
            send_sem=sent_bias.at[k],
            recv_sem=got_bias.at[k],
            device_id=bias_peer(k),
            device_id_type=MESH,
        )

    def chip_copy(k):
        there = lax.rem(chip + k, chips)
        return pltpu.make_async_remote_copy(
            src_ref=q_mine.at[there],
            dst_ref=by_chip.at[chip],
            send_sem=sent_chip.at[k],
            recv_sem=got_chip.at[k],
            device_id={"pts": there * 2 + core},
            device_id_type=MESH,
        )

    every(1, 2 * lats, lambda k: bias_copy(k).start())
    grad_q = grad_q_t[...].T
    for p in range(count):
        q_parts[p % 2, p // 2] = grad_q[p * rows_out : (p + 1) * rows_out]
    swap.start()
    by_lat[lat * 2 + core] = bias_sum[:SWEEPS, :]
    every(1, 2 * lats, lambda k: bias_copy(k).wait_recv())
    bias = jnp.sum(by_lat[...], axis=0)
    swap.wait_recv()
    q_mine[:, :rows_out, :] = q_parts[core] + from_core[...]
    q_mine[:, rows_out:, :] = jnp.broadcast_to(bias, (chips, SWEEPS, 128))
    every(1, chips, lambda k: chip_copy(k).start())
    by_chip[chip] = q_mine[chip]
    finish(2 * YS - 1)
    over.wait_recv()
    done = part_sum[2 * YS - 1] + from_z[...]
    grad_k_ref[...] = done[:, :WIDTH]
    grad_v_ref[...] = done[:, WIDTH:]
    every(1, chips, lambda k: chip_copy(k).wait_recv())
    small_ref[...] = jnp.sum(by_chip[...], axis=0)

    others(0, count, lambda k: piece(k).wait_send())
    others(0, count, lambda k: result(k).wait_send())
    for step in range(2 * YS):
        if step % YS < YS - 1:
            for upwards in (True, False):
                ring(step, upwards).wait_send()
    over.wait_send()
    swap.wait_send()
    every(1, 2 * lats, lambda k: bias_copy(k).wait_send())
    every(1, chips, lambda k: chip_copy(k).wait_send())


def whole(latents, keys, values, sweep, sweep_bias, grad_out, count, lats):
    rows, points = latents.shape[0], keys.shape[0]
    block, span, chips = points // (2 * YS), rows // 2, count // 2
    cols = min(256, span)
    stat_tiles = HEADS * rows // 128
    share = stat_tiles // count
    rows_out = rows // count
    dma = pltpu.SemaphoreType.DMA
    return pl.pallas_call(
        functools.partial(whole_kernel, count, lats),
        out_shape=[
            jax.ShapeDtypeStruct((block, WIDTH), F32),
            jax.ShapeDtypeStruct((block, WIDTH), F32),
            jax.ShapeDtypeStruct((rows_out + SWEEPS, WIDTH), F32),
        ],
        in_specs=vmem_specs(6),
        out_specs=vmem_specs(3),
        scratch_shapes=[
            pltpu.VMEM((points, 2 * WIDTH), BF),
            pltpu.VMEM((HEADS, 48, points), BF),
            pltpu.VMEM((SWEEPS, points), BF),
            pltpu.VMEM((WIDTH, rows), BF),
            pltpu.VMEM((2 * HEADS, 2 * WIDTH, span), BF),
            pltpu.VMEM((2 * HEADS, 2 * WIDTH, span), BF),
            pltpu.VMEM((2 * HEADS, span, WIDTH), BF),
            pltpu.VMEM((2 * HEADS, span, WIDTH), BF),
            pltpu.VMEM((points, cols), F32),
            pltpu.VMEM((points, cols), F32),
            pltpu.VMEM((stat_tiles, 8, 128), F32),
            pltpu.VMEM((count, share, 8, 128), F32),
            pltpu.VMEM((share, 8, 128), F32),
            pltpu.VMEM((count, share, 8, 128), F32),
            pltpu.VMEM((block, 2 * WIDTH), BF),
            pltpu.VMEM((block, 2 * WIDTH), BF),
            pltpu.VMEM((HEADS, block, span), BF),
            pltpu.VMEM((HEADS, block, span), BF),
            pltpu.VMEM((2 * YS, block, 2 * WIDTH), F32),
            pltpu.VMEM((2 * YS, block, 2 * WIDTH), F32),
            pltpu.VMEM((block, 2 * WIDTH), F32),
            pltpu.VMEM((WIDTH, rows), F32),
            pltpu.VMEM((128, 128), F32),
            pltpu.VMEM((2, chips, rows_out, WIDTH), F32),
            pltpu.VMEM((chips, rows_out, WIDTH), F32),
            pltpu.VMEM((2 * lats, SWEEPS, 128), F32),
            pltpu.VMEM((chips, rows_out + SWEEPS, WIDTH), F32),
            pltpu.VMEM((chips, rows_out + SWEEPS, WIDTH), F32),
            dma((count,)),
            dma((count,)),
            dma((count,)),
            dma((count,)),
            dma((2 * YS, 2)),
            dma((2 * YS, 2)),
            dma,
            dma,
            dma,
            dma,
            dma((2 * lats,)),
            dma((2 * lats,)),
            dma((chips,)),
            dma((chips,)),
        ],
        compiler_params=pltpu.CompilerParams(
            collective_id=0, has_side_effects=True, vmem_limit_bytes=VMEM_BYTES
        ),
    )(latents, keys, values, sweep, sweep_bias, grad_out)


def deliver_kernel(small_ref, grad_k_ref, grad_v_ref, q_out, k_out, v_out, bias_out, square):
    rows_out = q_out.shape[0]
    q_out[...] = small_ref[:rows_out, :]
    k_out[...] = grad_k_ref[...]
    v_out[...] = grad_v_ref[...]
    square[...] = jnp.zeros_like(square)
    square[:SWEEPS, :] = small_ref[rows_out:, :]
    bias_out[...] = square[...].T[:HEADS, :SWEEPS]


def deliver(small, grad_k, grad_v):
    return pl.pallas_call(
        deliver_kernel,
        out_shape=[
            jax.ShapeDtypeStruct((small.shape[0] - SWEEPS, WIDTH), F32),
            jax.ShapeDtypeStruct(grad_k.shape, F32),
            jax.ShapeDtypeStruct(grad_v.shape, F32),
            jax.ShapeDtypeStruct((HEADS, SWEEPS), F32),
        ],
        in_specs=vmem_specs(3),
        out_specs=vmem_specs(4),
        scratch_shapes=[pltpu.VMEM((128, 128), F32)],
    )(small, grad_k, grad_v)


def per_device(count, lats, latents, keys, values, sweep, sweep_bias, grad_out):
    grad_k, grad_v, small = whole(
        latents, keys, values, sweep.reshape(1, -1), sweep_bias, grad_out, count, lats
    )
    return tuple(deliver(small, grad_k, grad_v))


def solution(mesh):
    return jax.shard_map(
        functools.partial(per_device, mesh.shape["pts"], mesh.shape["lat"]),
        mesh=mesh,
        in_specs=(P("lat", None), P("pts", None), P("pts", None), P("pts"), P(), P("lat", None)),
        out_specs=(P(("lat", "pts"), None), P(("pts", "lat"), None), P(("pts", "lat"), None), P()),
        check_vma=False,
    )
```

time: 815 us -> 120 us (0.15)
  blocking collectives: 374 us -> 0 us
  matrix products: 185 us -> 0 us
  waiting for transfers between devices: 162 us -> 0 us
  Pallas kernels: 0 us -> 119 us
  local copies, waits for them, and re-layouts: 57.3 us -> 0 us
  between operations: 14.1 us -> 0.64 us
  other arithmetic: 13.1 us -> 0 us
    psum x2 -> x0, blocking collectives: 239 us -> none  [the longest x1 133 us: per_device(): totals, weighted = lax.psum((local_totals, local_weighted), 'pts')]
    dot_general x192 -> x0, matrix products: 185 us -> none  [the longest x48 65.5 us: score_tile(): jnp.einsum('rhd,chd->hrc', heads_of(query_block), heads_of(key_block), pr...]
    reduce_scatter x2 -> x0, waiting for transfers between devices: 162 us -> none  [the longest x1 137 us: per_device(): lax.psum_scatter(grad_blocks.reshape(query_count, feature_width), 'pts',...]
    pmax x1 -> x0, blocking collectives: 135 us -> none  [per_device(): row_top = lax.pmax(local_top, 'pts')]
    pallas_call x0 -> x2, Pallas kernels: none -> 119 us  [the longest x1 118 us: whole(): pl.pallas_call(functools.partial(whole_kernel, count, lats), out_shape=[j...]
    dynamic_slice x112 -> x0, local copies, waits for them, and re-layouts: 30.9 us -> none  [block_max(): running, unused = lax.scan(inner, lowest, key_data)]
    dynamic_update_slice x42 -> x0, local copies, waits for them, and re-layouts: 17 us -> none  [the longest x32 16.7 us: per_query(): grad_q, (kv_parts, bias_parts) = lax.scan(per_key, start_q, key_data)]
    add x36 -> x0, other arithmetic: 12.2 us -> none  [the longest x2 10.7 us: per_query(): carried[0] + kv_parts.reshape(key_count, 2 * feature_width)]
  transfers between devices with their start and end apart: 2 -> 0, of which waited for: 2 -> 0; matrix products, arithmetic and copies ran while one was open for 0% -> 0% of each run, Pallas kernels for 0% -> 0%
where the time goes in v2:
time: 120 us
  Pallas kernels  119 us (99%)
    pallas_call x1, Pallas kernels, whole(): pl.pallas_call(functools.partial(whole_kernel, count, lats), out_shape=[j...  118 us

profile of v2, /device:TPU:1, one launch (start us, length us, event | category | flops | bytes accessed | tf_op | source)
XLA Modules:
  0.0 120.1 jit_solution(12172171112079552577)
XLA Ops:
  0.6 117.6 %shard_map.93 = (f32[512,128]{1,0:T(8,128)}, f32[512,128]{1,0:T(8,128)}, f32[48,128]{1,0:T(8,128)}) custom-call(bf16[1024,128]{1,0:T(8,128)(2,1)} %latents_ref.1, bf16[4096,128]{1,0:T(8,128)(2,1)} %keys_ref.1, bf16[4096,128]{1,0:T(8,128)(2,1)} %values_ref.1, s32[1,4096]{1,0:T(1,128)} %bitcast.1, f32[4,16]{1,0:T(4,128)} %sweep_bias_ref.1, ...), custom_call_target="tpu_custom_call" | custom-call | tf_op jit(solution)/shard_map/pallas_call | solution.py:538
  118.2 1.9 %shard_map.94 = (f32[32,128]{1,0:T(8,128)}, f32[512,128]{1,0:T(8,128)}, f32[512,128]{1,0:T(8,128)}, f32[4,16]{1,0:T(4,128)}) custom-call(f32[48,128]{1,0:T(8,128)} %get-tuple-element.7.small_ref, f32[512,128]{1,0:T(8,128)} %get-tuple-element.8.grad_k_ref, f32[512,128]{1,0:T(8,128)} %get-tuple-element.9.grad_v_ref), custom_call_target="tpu_custom_call" | custom-call | tf_op jit(solution)/shard_map/pallas_call | solution.py:608

commit v3 on v2

--- a/solution.py
+++ b/solution.py
@@ -54,6 +54,8 @@
     k_aux,
     value_rows,
     onehot_t,
+    lat_rows,
+    out_rows,
     g_t,
     q_feat,
     g_feat,
@@ -69,14 +71,18 @@
     v_stage,
     probs,
     scaled,
+    mark_stage,
     part_sum,
     from_ring,
+    relay,
     from_z,
     grad_q_t,
     bias_sum,
     q_parts,
     from_core,
     by_lat,
+    bias_mine,
+    by_bias,
     q_mine,
     by_chip,
     sent_1,
@@ -85,12 +91,16 @@
     got_2,
     sent_ring,
     got_ring,
-    sent_z,
-    got_z,
+    sent_near,
+    got_near,
+    sent_far,
+    got_far,
     sent_core,
     got_core,
     sent_bias,
     got_bias,
+    sent_all,
+    got_all,
     sent_chip,
     got_chip,
 ):
@@ -104,7 +114,9 @@
     chunks = points // chunk
     block = points // (2 * YS)
     half = block // 2
+    quarter = block // 4
     chips = count // 2
+    near_z = 4 if chips % 4 == 0 else chips
     share = stats.shape[0] // count
     rows_out = latents // count
 
@@ -115,7 +127,14 @@
     z, y = lat // YS, lax.rem(lat, YS)
     up = z * YS + lax.rem(y + 1, YS)
     down = z * YS + lax.rem(y + YS - 1, YS)
-    across = (1 - z) * YS + y
+    height = z * near_z + lax.rem(chip, near_z)
+
+    def at_height(shift):
+        there = lax.rem(height + shift + 2 * near_z, 2 * near_z)
+        return {
+            "pts": ((chip // near_z) * near_z + lax.rem(there, near_z)) * 2 + core,
+            "lat": (there // near_z) * YS + y,
+        }
 
     def every(start, stop, action):
         def step(k, unused):
@@ -148,6 +167,8 @@
 
     every(1, count, greet_pts)
     every(1, 2 * lats, greet_lat)
+    for shift in (1, -1, near_z - 1, 1 - near_z):
+        pl.semaphore_signal(barrier, inc=1, device_id=at_height(shift), device_id_type=MESH)
 
     k_aux[:, :WIDTH] = keys_ref[...]
 
@@ -166,8 +187,13 @@
             value_rows[h, HEAD_DIM:, rows] = jnp.where(row[:16] == 0, 1.0, 0.0).astype(BF)
 
     every(0, chunks, build)
-    q_t = latents_ref[...].T
-    g_t[...] = grad_out_ref[...].T
+    order = [p for parity in range(2) for p in range(count) if (p // 2) % 2 == parity]
+    for at, p in enumerate(order):
+        to, of = slice(at * rows_out, (at + 1) * rows_out), slice(p * rows_out, (p + 1) * rows_out)
+        lat_rows[to, :] = latents_ref[of, :]
+        out_rows[to, :] = grad_out_ref[of, :]
+    q_t = lat_rows[...].T
+    g_t[...] = out_rows[...].T
     lane = lax.broadcasted_iota(jnp.int32, (span, WIDTH), 1)
     eye = lax.broadcasted_iota(jnp.int32, (SWEEPS, SWEEPS), 0) == lax.broadcasted_iota(
         jnp.int32, (SWEEPS, SWEEPS), 1
@@ -182,7 +208,7 @@
         for s in range(2):
             n = s * HEADS + h
             here = slice(s * span, (s + 1) * span)
-            for source, stack in ((latents_ref, q_stack), (grad_out_ref, g_stack)):
+            for source, stack in ((lat_rows, q_stack), (out_rows, g_stack)):
                 stack[n] = jnp.where(mine_lanes, source[here, :].astype(F32), 0.0).astype(BF)
             q_feat[n] = jnp.zeros((2 * WIDTH, span), BF)
             g_feat[n] = jnp.zeros((2 * WIDTH, span), BF)
@@ -192,7 +218,6 @@
                 q_feat[n, WIDTH + index * SWEEPS : WIDTH + (index + 1) * SWEEPS, :] = piece
     grad_q_t[...] = jnp.zeros_like(grad_q_t)
     bias_sum[...] = jnp.zeros_like(bias_sum)
-    pl.semaphore_wait(barrier, count - 1 + 2 * lats - 1)
 
     def piece(owner):
         return pltpu.make_async_remote_copy(
@@ -338,6 +363,7 @@
 
         @pl.when(pair == pairs // 2 - 1)
         def _():
+            pl.semaphore_wait(barrier, count - 1 + 2 * lats - 1 + 4)
             send_pieces(0)
 
         @pl.when(pair == pairs - 2)
@@ -352,19 +378,24 @@
 
     lane_row = lax.broadcasted_iota(jnp.int32, (block, 128), 1)
 
-    def compute(step, s):
-        turn = lax.rem(step, YS)
-        owner_z = jnp.where(step < YS, 1 - z, z)
-        at_up = (owner_z * YS + lax.rem(y + 2 * YS - 1 - turn, YS)) * block
-        at_down = (owner_z * YS + lax.rem(y + 1 + turn, YS)) * block + half
-        marks = []
-        for row, at in ((0, at_up), (half, at_down)):
-            source = pl.ds(pl.multiple_of(at, half), half)
-            rows = pl.ds(row, half)
-            k_stage[rows, :] = k_aux[source, :]
-            v_stage[rows, :WIDTH] = values_ref[source, :]
-            v_stage[rows, WIDTH:] = k_aux[source, WIDTH:]
-            marks.append(onehot_t[:, source])
+    def compute(item, s):
+        owner_z = jnp.where(item < YS, 1 - z, z)
+        sub = lax.rem(item // 2, 2)
+        for part in range(2):
+            turn = lax.rem(item, 2) * 2 + part
+            y_up = lax.rem(y + 2 * YS - 1 - turn, YS)
+            y_down = lax.rem(y + 1 + turn, YS)
+            for place, at in (
+                (0, (owner_z * YS + y_up) * block + sub * quarter),
+                (1, (owner_z * YS + y_down) * block + half + sub * quarter),
+            ):
+                source = pl.ds(pl.multiple_of(at, quarter), quarter)
+                row = (part * 2 + place) * quarter
+                rows = pl.ds(row, quarter)
+                k_stage[rows, :] = k_aux[source, :]
+                v_stage[rows, :WIDTH] = values_ref[source, :]
+                v_stage[rows, WIDTH:] = k_aux[source, WIDTH:]
+                mark_stage[:, row : row + quarter] = onehot_t[:, source]
         k_t = k_stage[:, :WIDTH].T
         row_sums = jnp.zeros((block, 128), F32)
         grad_k = jnp.zeros((block, WIDTH), F32)
@@ -387,91 +418,127 @@
             grad_k = grad_k + dot(scaled[h], q_stack[n])
             grad_q_t[rows, lanes] += dot(k_t[rows, :], scaled[h])
 
-        @pl.when(s == 0)
-        def _():
-            part_sum[step, :, :WIDTH] = grad_k
-            part_sum[step, :, WIDTH:] = grad_v
-
-        @pl.when(s == 1)
-        def _():
-            part_sum[step, :, :WIDTH] += grad_k
-            part_sum[step, :, WIDTH:] += grad_v
+        for part in range(2):
+            rows = slice(part * half, (part + 1) * half)
+            unit = item * 2 + part
+
+            @pl.when(s == 0)
+            def _():
+                part_sum[unit, :, :WIDTH] = grad_k[rows]
+                part_sum[unit, :, WIDTH:] = grad_v[rows]
+
+            @pl.when(s == 1)
+            def _():
+                part_sum[unit, :, :WIDTH] += grad_k[rows]
+                part_sum[unit, :, WIDTH:] += grad_v[rows]
 
         for piece in three_pieces(row_sums):
-            for part in range(2):
-                bias_sum[:SWEEPS, :] += dot(marks[part], piece[part * half : (part + 1) * half])
-
-    def ring(step, upwards):
-        rows = pl.ds(0, half) if upwards else pl.ds(half, half)
-        return pltpu.make_async_remote_copy(
-            src_ref=part_sum.at[step, rows],
-            dst_ref=from_ring.at[step, rows],
-            send_sem=sent_ring.at[step, 0 if upwards else 1],
-            recv_sem=got_ring.at[step, 0 if upwards else 1],
-            device_id={"lat": up if upwards else down},
-            device_id_type=MESH,
-        )
-
-    over = pltpu.make_async_remote_copy(
-        src_ref=part_sum.at[YS - 1],
-        dst_ref=from_z,
-        send_sem=sent_z,
-        recv_sem=got_z,
-        device_id={"lat": across},
-        device_id_type=MESH,
-    )
-
-    def finish(step):
-        turn = lax.rem(step, YS)
+            bias_sum[:SWEEPS, :] += dot(mark_stage[...], piece)
+
+    def ring(unit, way):
+        rows = pl.ds(way * quarter, quarter)
+        return pltpu.make_async_remote_copy(
+            src_ref=part_sum.at[unit, rows],
+            dst_ref=from_ring.at[unit, rows],
+            send_sem=sent_ring.at[unit, way],
+            recv_sem=got_ring.at[unit, way],
+            device_id={"lat": down if way else up},
+            device_id_type=MESH,
+        )
+
+    def near(sub, way):
+        return pltpu.make_async_remote_copy(
+            src_ref=part_sum.at[sub * YS + YS - 1, pl.ds(way * quarter, quarter)],
+            dst_ref=relay.at[sub, way],
+            send_sem=sent_near.at[sub, way],
+            recv_sem=got_near.at[sub, way],
+            device_id=at_height(-1 if way else 1),
+            device_id_type=MESH,
+        )
+
+    def far(sub, way):
+        return pltpu.make_async_remote_copy(
+            src_ref=relay.at[sub, way],
+            dst_ref=from_z.at[sub, pl.ds(way * quarter, quarter)],
+            send_sem=sent_far.at[sub, way],
+            recv_sem=got_far.at[sub, way],
+            device_id=at_height(1 - near_z if way else near_z - 1),
+            device_id_type=MESH,
+        )
+
+    def finish(unit):
+        turn = lax.rem(unit, YS)
 
         @pl.when(turn > 0)
         def _():
-            for upwards in (True, False):
-                ring(step - 1, upwards).wait_recv()
-            part_sum[step] += from_ring[step - 1]
+            for way in range(2):
+                ring(unit - 1, way).wait_recv()
+            part_sum[unit] += from_ring[unit - 1]
 
         @pl.when(turn < YS - 1)
         def _():
-            for upwards in (True, False):
-                ring(step, upwards).start()
-
-        @pl.when(step == YS - 1)
-        def _():
-            over.start()
+            for way in range(2):
+                ring(unit, way).start()
+
+        @pl.when((turn == YS - 1) & (unit < 2 * YS))
+        def _():
+            for way in range(2):
+                near(unit // YS, way).start()
+
+    def swap(s):
+        return pltpu.make_async_remote_copy(
+            src_ref=q_parts.at[s, 1 - core],
+            dst_ref=from_core.at[s],
+            send_sem=sent_core.at[s],
+            recv_sem=got_core.at[s],
+            device_id={"pts": chip * 2 + 1 - core},
+            device_id_type=MESH,
+        )
+
+    def start_swap(s):
+        grad_q = grad_q_t[:, s * span : (s + 1) * span].T
+        for part in range(chips):
+            q_parts[s, part % 2, part // 2] = grad_q[part * rows_out : (part + 1) * rows_out]
+        swap(s).start()
 
     def per_item(t, unused):
-        odd = lax.rem(t, 2)
-        second = (t >= 14) | ((t >= 3) & (odd == 1))
-        step = jnp.where(
-            t < 3, t, jnp.where(t >= 14, t - 8, jnp.where(odd == 1, (t - 3) // 2, t // 2 + 1))
-        )
-
-        @pl.when(t == 3)
+        swapped = (t == 1) | (t == 2)
+        item = jnp.where(swapped, 2 - t, t // 2)
+        s = jnp.where(swapped, t - 1, lax.rem(t, 2))
+
+        @pl.when(t == 2)
         def _():
             take_results(1)
 
-        compute(step, jnp.where(second, 1, 0))
-
-        @pl.when(t == 1)
+        compute(item, s)
+
+        @pl.when(t == 0)
         def _():
             combine(1)
 
-        @pl.when(second & (step < 2 * YS - 1))
-        def _():
-            finish(step)
+        @pl.when(t >= 2)
+        def _():
+            finish(jnp.where(t < 6, t - 2, t - 1))
+
+        @pl.when(t == 5)
+        def _():
+            finish(4)
+
+        for sub, when in ((0, 7), (1, 10)):
+
+            @pl.when(t == when)
+            def _():
+                for way in range(2):
+                    near(sub, way).wait_recv()
+                    far(sub, way).start()
+
+        @pl.when(t == 4 * YS - 2)
+        def _():
+            start_swap(0)
 
         return unused
 
     lax.fori_loop(0, 4 * YS, per_item, 0)
-
-    swap = pltpu.make_async_remote_copy(
-        src_ref=q_parts.at[1 - core],
-        dst_ref=from_core,
-        send_sem=sent_core,
-        recv_sem=got_core,
-        device_id={"pts": chip * 2 + 1 - core},
-        device_id_type=MESH,
-    )
 
     def bias_copy(k):
         return pltpu.make_async_remote_copy(
@@ -483,48 +550,95 @@
             device_id_type=MESH,
         )
 
-    def chip_copy(k):
-        there = lax.rem(chip + k, chips)
-        return pltpu.make_async_remote_copy(
-            src_ref=q_mine.at[there],
+    def bias_all(k):
+        return pltpu.make_async_remote_copy(
+            src_ref=bias_mine,
+            dst_ref=by_bias.at[chip],
+            send_sem=sent_all.at[k],
+            recv_sem=got_all.at[k],
+            device_id={"pts": lax.rem(chip + k, chips) * 2 + core},
+            device_id_type=MESH,
+        )
+
+    def chip_copy(s, m):
+        there = 2 * m + s
+        return pltpu.make_async_remote_copy(
+            src_ref=q_mine.at[s, m],
             dst_ref=by_chip.at[chip],
-            send_sem=sent_chip.at[k],
-            recv_sem=got_chip.at[k],
+            send_sem=sent_chip.at[there],
+            recv_sem=got_chip.at[chip],
             device_id={"pts": there * 2 + core},
             device_id_type=MESH,
         )
 
+    def chip_from(source):
+        return pltpu.make_async_remote_copy(
+            src_ref=q_mine.at[0, 0],
+            dst_ref=by_chip.at[source],
+            send_sem=sent_chip.at[source],
+            recv_sem=got_chip.at[source],
+            device_id={"pts": source * 2 + core},
+            device_id_type=MESH,
+        )
+
+    def chips_of(s, action):
+        def guarded(m):
+            @pl.when(2 * m + s != chip)
+            def _():
+                action(m)
+
+        every(0, chips // 2, guarded)
+
+    def send_chips(s):
+        swap(s).wait_recv()
+        q_mine[s] = q_parts[s, core] + from_core[s]
+        chips_of(s, lambda m: chip_copy(s, m).start())
+
     every(1, 2 * lats, lambda k: bias_copy(k).start())
-    grad_q = grad_q_t[...].T
-    for p in range(count):
-        q_parts[p % 2, p // 2] = grad_q[p * rows_out : (p + 1) * rows_out]
-    swap.start()
+    start_swap(1)
+    send_chips(0)
     by_lat[lat * 2 + core] = bias_sum[:SWEEPS, :]
     every(1, 2 * lats, lambda k: bias_copy(k).wait_recv())
-    bias = jnp.sum(by_lat[...], axis=0)
-    swap.wait_recv()
-    q_mine[:, :rows_out, :] = q_parts[core] + from_core[...]
-    q_mine[:, rows_out:, :] = jnp.broadcast_to(bias, (chips, SWEEPS, 128))
-    every(1, chips, lambda k: chip_copy(k).start())
-    by_chip[chip] = q_mine[chip]
-    finish(2 * YS - 1)
-    over.wait_recv()
-    done = part_sum[2 * YS - 1] + from_z[...]
-    grad_k_ref[...] = done[:, :WIDTH]
-    grad_v_ref[...] = done[:, WIDTH:]
-    every(1, chips, lambda k: chip_copy(k).wait_recv())
-    small_ref[...] = jnp.sum(by_chip[...], axis=0)
+    bias_mine[...] = jnp.sum(by_lat[...], axis=0)
+    every(1, chips, lambda k: bias_all(k).start())
+    send_chips(1)
+    by_bias[chip] = bias_mine[...]
+    by_chip[chip] = q_mine[lax.rem(chip, 2), chip // 2]
+    finish(4 * YS - 1)
+    for sub in range(2):
+        for way in range(2):
+            far(sub, way).wait_recv()
+        done = part_sum[(2 + sub) * YS + YS - 1] + from_z[sub]
+        for way in range(2):
+            source = slice(way * quarter, (way + 1) * quarter)
+            rows = slice(way * half + sub * quarter, way * half + (sub + 1) * quarter)
+            grad_k_ref[rows, :] = done[source, :WIDTH]
+            grad_v_ref[rows, :] = done[source, WIDTH:]
+
+    def got_from(c):
+        @pl.when(c != chip)
+        def _():
+            chip_from(c).wait_recv()
+
+    every(0, chips, got_from)
+    small_ref[:rows_out, :] = jnp.sum(by_chip[...], axis=0)
+    every(1, chips, lambda k: bias_all(k).wait_recv())
+    small_ref[rows_out:, :] = jnp.sum(by_bias[...], axis=0)
 
     others(0, count, lambda k: piece(k).wait_send())
     others(0, count, lambda k: result(k).wait_send())
-    for step in range(2 * YS):
-        if step % YS < YS - 1:
-            for upwards in (True, False):
-                ring(step, upwards).wait_send()
-    over.wait_send()
-    swap.wait_send()
+    for unit in range(4 * YS):
+        if unit % YS < YS - 1:
+            for way in range(2):
+                ring(unit, way).wait_send()
+    for sub in range(2):
+        for way in range(2):
+            near(sub, way).wait_send()
+            far(sub, way).wait_send()
+        swap(sub).wait_send()
+        chips_of(sub, lambda m: chip_copy(sub, m).wait_send())
     every(1, 2 * lats, lambda k: bias_copy(k).wait_send())
-    every(1, chips, lambda k: chip_copy(k).wait_send())
+    every(1, chips, lambda k: bias_all(k).wait_send())
 
 
 def whole(latents, keys, values, sweep, sweep_bias, grad_out, count, lats):
@@ -548,6 +662,8 @@
             pltpu.VMEM((points, 2 * WIDTH), BF),
             pltpu.VMEM((HEADS, 48, points), BF),
             pltpu.VMEM((SWEEPS, points), BF),
+            pltpu.VMEM((rows, WIDTH), BF),
+            pltpu.VMEM((rows, WIDTH), BF),
             pltpu.VMEM((WIDTH, rows), BF),
             pltpu.VMEM((2 * HEADS, 2 * WIDTH, span), BF),
             pltpu.VMEM((2 * HEADS, 2 * WIDTH, span), BF),
@@ -563,28 +679,36 @@
             pltpu.VMEM((block, 2 * WIDTH), BF),
             pltpu.VMEM((HEADS, block, span), BF),
             pltpu.VMEM((HEADS, block, span), BF),
-            pltpu.VMEM((2 * YS, block, 2 * WIDTH), F32),
-            pltpu.VMEM((2 * YS, block, 2 * WIDTH), F32),
-            pltpu.VMEM((block, 2 * WIDTH), F32),
+            pltpu.VMEM((SWEEPS, block), BF),
+            pltpu.VMEM((4 * YS, block // 2, 2 * WIDTH), F32),
+            pltpu.VMEM((4 * YS, block // 2, 2 * WIDTH), F32),
+            pltpu.VMEM((2, 2, block // 4, 2 * WIDTH), F32),
+            pltpu.VMEM((2, block // 2, 2 * WIDTH), F32),
             pltpu.VMEM((WIDTH, rows), F32),
             pltpu.VMEM((128, 128), F32),
-            pltpu.VMEM((2, chips, rows_out, WIDTH), F32),
+            pltpu.VMEM((2, 2, chips // 2, rows_out, WIDTH), F32),
+            pltpu.VMEM((2, chips // 2, rows_out, WIDTH), F32),
+            pltpu.VMEM((2 * lats, SWEEPS, 128), F32),
+            pltpu.VMEM((SWEEPS, 128), F32),
+            pltpu.VMEM((chips, SWEEPS, 128), F32),
+            pltpu.VMEM((2, chips // 2, rows_out, WIDTH), F32),
             pltpu.VMEM((chips, rows_out, WIDTH), F32),
-            pltpu.VMEM((2 * lats, SWEEPS, 128), F32),
-            pltpu.VMEM((chips, rows_out + SWEEPS, WIDTH), F32),
-            pltpu.VMEM((chips, rows_out + SWEEPS, WIDTH), F32),
             dma((count,)),
             dma((count,)),
             dma((count,)),
             dma((count,)),
-            dma((2 * YS, 2)),
-            dma((2 * YS, 2)),
-            dma,
-            dma,
-            dma,
-            dma,
+            dma((4 * YS, 2)),
+            dma((4 * YS, 2)),
+            dma((2, 2)),
+            dma((2, 2)),
+            dma((2, 2)),
+            dma((2, 2)),
+            dma((2,)),
+            dma((2,)),
             dma((2 * lats,)),
             dma((2 * lats,)),
+            dma((chips,)),
+            dma((chips,)),
             dma((chips,)),
             dma((chips,)),
         ],

time: 120 us -> 132 us (1.10); the launches traced: 120 us -> 130 us
  Pallas kernels: 119 us -> 129 us
    pallas_call x1, Pallas kernels: 118 us -> 127 us  [whole(): pl.pallas_call(functools.partial(whole_kernel, count, lats), out_shape=[j...]
where the time goes in v3:
time: 132 us; the launch traced here: 130 us
  Pallas kernels  129 us (98%)
    pallas_call x1, Pallas kernels, whole(): pl.pallas_call(functools.partial(whole_kernel, count, lats), out_shape=[j...  127 us

profile of v3, /device:TPU:1, one launch (start us, length us, event | category | flops | bytes accessed | tf_op | source)
XLA Modules:
  0.0 130.0 jit_solution(7518589748003038467)
XLA Ops:
  0.6 127.4 %shard_map.93 = (f32[512,128]{1,0:T(8,128)}, f32[512,128]{1,0:T(8,128)}, f32[48,128]{1,0:T(8,128)}) custom-call(bf16[1024,128]{1,0:T(8,128)(2,1)} %latents_ref.1, bf16[4096,128]{1,0:T(8,128)(2,1)} %keys_ref.1, bf16[4096,128]{1,0:T(8,128)(2,1)} %values_ref.1, s32[1,4096]{1,0:T(1,128)} %bitcast.1, f32[4,16]{1,0:T(4,128)} %sweep_bias_ref.1, ...), custom_call_target="tpu_custom_call" | custom-call | tf_op jit(solution)/shard_map/pallas_call | solution.py:652
  128.1 1.9 %shard_map.94 = (f32[32,128]{1,0:T(8,128)}, f32[512,128]{1,0:T(8,128)}, f32[512,128]{1,0:T(8,128)}, f32[4,16]{1,0:T(4,128)}) custom-call(f32[48,128]{1,0:T(8,128)} %get-tuple-element.7.small_ref, f32[512,128]{1,0:T(8,128)} %get-tuple-element.8.grad_k_ref, f32[512,128]{1,0:T(8,128)} %get-tuple-element.9.grad_v_ref), custom_call_target="tpu_custom_call" | custom-call | tf_op jit(solution)/shard_map/pallas_call | solution.py:732

commit v4 on v2

v4 whole, which is shorter than its diff:
```python
import functools
import math

import jax
import jax.numpy as jnp
from jax import lax
from jax.experimental import pallas as pl
from jax.experimental.pallas import tpu as pltpu
from jax.sharding import PartitionSpec as P

HEADS = 4
HEAD_DIM = 32
WIDTH = HEADS * HEAD_DIM
SWEEPS = 16
SCALE = HEAD_DIM**-0.5
LOG2E = math.log2(math.e)
TO_LOG2 = SCALE * LOG2E
YS = 4
ONES_ROW = 3 * SWEEPS
BF = jnp.bfloat16
F32 = jnp.float32
MESH = pl.DeviceIdType.MESH
VMEM_BYTES = 56 * 1024 * 1024


def dot(a, b):
    return jnp.dot(a, b, preferred_element_type=F32)


def three_pieces(x):
    hi = x.astype(BF)
    rest = x - hi.astype(F32)
    mid = rest.astype(BF)
    low = (rest - mid.astype(F32)).astype(BF)
    return hi, mid, low


def vmem_specs(count):
    return [pl.BlockSpec(memory_space=pltpu.VMEM)] * count


def whole_kernel(
    count,
    lats,
    latents_ref,
    keys_ref,
    values_ref,
    sweep_ref,
    sweep_bias_ref,
    grad_out_ref,
    grad_k_ref,
    grad_v_ref,
    small_ref,
    k_aux,
    value_rows,
    onehot_t,
    g_t,
    q_feat,
    g_feat,
    q_stack,
    g_stack,
    scores_0,
    scores_1,
    stats,
    from_sibling,
    stats_1,
    stats_x,
    stats_2,
    stats_z,
    k_stage,
    v_stage,
    mark_stage,
    probs,
    scaled,
    part_sum,
    from_ring,
    relay,
    from_z,
    grad_q_t,
    bias_sum,
    q_parts,
    from_core,
    bias_1,
    q_x,
    got_q_x,
    q_z,
    got_q_z,
    bias_2,
    bias_z,
    sent_s1,
    got_s1,
    sent_sx,
    got_sx,
    sent_sz,
    got_sz,
    sent_ring,
    got_ring,
    sent_near,
    got_near,
    sent_far,
    got_far,
    sent_core,
    got_core,
    sent_b1,
    got_b1,
    sent_qx,
    got_qx,
    sent_qz,
    got_qz,
    sent_b2,
    got_b2,
):
    points, latents = keys_ref.shape[0], latents_ref.shape[0]
    span = latents // 2
    cols = min(256, span)
    per_span = span // cols
    tiles = HEADS * 2 * per_span
    pairs = tiles // 2
    chunk = min(512, points)
    chunks = points // chunk
    block = points // (2 * YS)
    half = block // 2
    quarter = block // 4
    chips = count // 2
    nz = 4 if chips % 4 == 0 else chips
    nx = chips // nz
    heights = 2 * nz
    rows_out = latents // count

    me = lax.axis_index("pts")
    lat = lax.axis_index("lat")
    core = lax.rem(me, 2)
    chip = me // 2
    z, y = lat // YS, lax.rem(lat, YS)
    up = z * YS + lax.rem(y + 1, YS)
    down = z * YS + lax.rem(y + YS - 1, YS)
    x, zl = chip // nz, lax.rem(chip, nz)
    height = z * nz + zl

    def x_peer(k):
        return {"pts": (lax.rem(x + k, nx) * nz + zl) * 2 + core}

    def z_peer(k):
        return {"pts": (x * nz + lax.rem(zl + k, nz)) * 2 + core}

    def y_peer(k):
        there = lax.rem(y * 2 + core + k, 2 * YS)
        return {"pts": chip * 2 + lax.rem(there, 2), "lat": z * YS + there // 2}

    def at_height(shift):
        there = lax.rem(height + shift + heights, heights)
        return {"pts": (x * nz + lax.rem(there, nz)) * 2 + core, "lat": (there // nz) * YS + y}

    def remote(src, dst, sent, got, device):
        return pltpu.make_async_remote_copy(
            src_ref=src,
            dst_ref=dst,
            send_sem=sent,
            recv_sem=got,
            device_id=device,
            device_id_type=MESH,
        )

    def every(start, stop, action):
        def step(k, unused):
            action(k)
            return unused

        lax.fori_loop(start, stop, step, 0)

    barrier = pltpu.get_barrier_semaphore()
    greeted = (
        [x_peer(k) for k in range(1, nx)]
        + [at_height(k) for k in range(1, heights)]
        + [y_peer(k) for k in range(1, 2 * YS)]
    )
    for device in greeted:
        pl.semaphore_signal(barrier, inc=1, device_id=device, device_id_type=MESH)

    k_aux[:, :WIDTH] = keys_ref[...]

    def build(c):
        rows = pl.ds(pl.multiple_of(c * chunk, chunk), chunk)
        swept = sweep_ref[:, rows]
        row = lax.broadcasted_iota(jnp.int32, (WIDTH, chunk), 0)
        marked = (row < ONES_ROW) & (lax.rem(row, SWEEPS) == swept)
        ones = (row >= ONES_ROW) & (row < ONES_ROW + 3)
        aux_t = jnp.where(marked | ones, 1.0, 0.0)
        onehot_t[:, rows] = aux_t[:SWEEPS].astype(BF)
        k_aux[rows, WIDTH:] = aux_t.T.astype(BF)
        value_t = values_ref[rows, :].T
        for h in range(HEADS):
            value_rows[h, :HEAD_DIM, rows] = value_t[h * HEAD_DIM : (h + 1) * HEAD_DIM, :]
            value_rows[h, HEAD_DIM:, rows] = jnp.where(row[:16] == 0, 1.0, 0.0).astype(BF)

    every(0, chunks, build)
    q_t = latents_ref[...].T
    g_t[...] = grad_out_ref[...].T
    lane = lax.broadcasted_iota(jnp.int32, (span, WIDTH), 1)
    eye = lax.broadcasted_iota(jnp.int32, (SWEEPS, SWEEPS), 0) == lax.broadcasted_iota(
        jnp.int32, (SWEEPS, SWEEPS), 1
    )
    for h in range(HEADS):
        rows = slice(h * HEAD_DIM, (h + 1) * HEAD_DIM)
        column = jnp.sum(
            jnp.where(eye, sweep_bias_ref[h : h + 1, :], 0.0), axis=1, keepdims=True
        ) * (1.0 / SCALE)
        bias_pieces = three_pieces(jnp.broadcast_to(column, (SWEEPS, span)))
        mine_lanes = (lane >= h * HEAD_DIM) & (lane < (h + 1) * HEAD_DIM)
        for s in range(2):
            n = s * HEADS + h
            here = slice(s * span, (s + 1) * span)
            for source, stack in ((latents_ref, q_stack), (grad_out_ref, g_stack)):
                stack[n] = jnp.where(mine_lanes, source[here, :].astype(F32), 0.0).astype(BF)
            q_feat[n] = jnp.zeros((2 * WIDTH, span), BF)
            g_feat[n] = jnp.zeros((2 * WIDTH, span), BF)
            q_feat[n, rows, :] = q_t[rows, here]
            g_feat[n, rows, :] = g_t[rows, here]
            for index, piece in enumerate(bias_pieces):
                q_feat[n, WIDTH + index * SWEEPS : WIDTH + (index + 1) * SWEEPS, :] = piece
    grad_q_t[...] = jnp.zeros_like(grad_q_t)
    bias_sum[...] = jnp.zeros_like(bias_sum)

    def merge(parts):
        best = functools.reduce(jnp.maximum, [part[0] for part in parts])
        weights = [jnp.exp2(part[0] - best) for part in parts]
        sums = [sum(w * part[kind] for w, part in zip(weights, parts)) for kind in (1, 2, 3)]
        return [best] + sums

    def keep(ref, merged):
        for kind, value in enumerate(merged):
            ref[kind] = value

    def to_sibling(s):
        return remote(
            stats.at[s], from_sibling.at[s], sent_s1.at[s], got_s1.at[s], {"pts": me + 1 - 2 * core}
        )

    def along_x(s, k):
        return remote(
            stats_1.at[s], stats_x.at[s, x], sent_sx.at[s, k], got_sx.at[s, k], x_peer(k)
        )

    def along_z(s, k):
        return remote(
            stats_2.at[s], stats_z.at[s, zl], sent_sz.at[s, k], got_sz.at[s, k], z_peer(k)
        )

    def exchange_x(s):
        to_sibling(s).wait_recv()
        merged = merge([stats[s], from_sibling[s]])
        keep(stats_1.at[s], merged)
        for k in range(1, nx):
            along_x(s, k).start()
        keep(stats_x.at[s, x], merged)

    def exchange_z(s):
        for k in range(1, nx):
            along_x(s, k).wait_recv()
        merged = merge([stats_x[s, i] for i in range(nx)])
        keep(stats_2.at[s], merged)
        for k in range(1, nz):
            along_z(s, k).start()
        keep(stats_z.at[s, zl], merged)

    def take_results(s):
        for k in range(1, nz):
            along_z(s, k).wait_recv()
        best, total, weighted, rounded_total = merge([stats_z[s, i] for i in range(nz)])
        offset = (best + jnp.log(total) * LOG2E) * (-1.0 / TO_LOG2)
        delta = -(weighted / rounded_total)
        row16 = lax.broadcasted_iota(jnp.int32, (16, 128), 0)
        per_tile = cols // 128
        for n in range(tiles // 2):
            it, h = n // HEADS, n % HEADS
            for part in range(per_tile):
                line = n * per_tile + part
                left = it * cols + part * 128
                for value, feat in ((offset, q_feat), (delta, g_feat)):
                    hi, mid, low = three_pieces(value[line : line + 1, :])
                    feat[
                        s * HEADS + h,
                        WIDTH + ONES_ROW : WIDTH + ONES_ROW + 16,
                        left : left + 128,
                    ] = jnp.where(
                        row16 == 0,
                        hi.astype(F32),
                        jnp.where(
                            row16 == 1, mid.astype(F32), jnp.where(row16 == 2, low.astype(F32), 0.0)
                        ),
                    ).astype(BF)

    lowest = jnp.full((32, cols), -jnp.inf, F32)

    def feature_of(n):
        it = n // HEADS
        return (
            (it // per_span) * HEADS + lax.rem(n, HEADS),
            pl.ds(pl.multiple_of(lax.rem(it, per_span) * cols, cols), cols),
        )

    def score_chunk(n, into, c, top):
        index, lanes = feature_of(n)
        rows = pl.ds(c * chunk, chunk)
        s = dot(k_aux[rows, :], q_feat[index, :, lanes]) * TO_LOG2
        into[rows, :] = s
        return jnp.maximum(top, jnp.max(s.reshape(chunk // 32, 32, cols), axis=0))

    def tile_sums(n, scores, top_rows, following, into):
        top = jnp.max(top_rows, axis=0, keepdims=True)
        head = lax.rem(n, HEADS)
        next_top = lowest
        total = jnp.zeros((32, cols), F32)
        out = jnp.zeros((48, cols), F32)
        for c in range(chunks):
            rows = pl.ds(c * chunk, chunk)
            e = jnp.exp2(scores[rows, :] - top)
            total = total + jnp.sum(e.reshape(chunk // 32, 32, cols), axis=0)
            out = out + dot(value_rows[head, :, rows], e.astype(BF))
            next_top = score_chunk(following, into, c, next_top)
        total = jnp.sum(total, axis=0, keepdims=True)
        g = g_t[
            pl.ds(pl.multiple_of(head * HEAD_DIM, HEAD_DIM), HEAD_DIM),
            pl.ds(pl.multiple_of((n // HEADS) * cols, cols), cols),
        ].astype(F32)
        weighted = jnp.sum(out[:HEAD_DIM] * g, axis=0, keepdims=True)
        rounded_total = out[HEAD_DIM : HEAD_DIM + 1]
        per_tile = cols // 128
        for kind, value in enumerate((top, total, weighted, rounded_total)):
            for part in range(per_tile):
                line = lax.rem(n, tiles // 2) * per_tile + part
                stats[n // (tiles // 2), kind, pl.ds(line, 1), :] = value[
                    :, part * 128 : (part + 1) * 128
                ]
        return next_top

    first_top = lowest
    for c in range(chunks):
        first_top = score_chunk(0, scores_0, c, first_top)

    def per_pair(pair, top_rows):
        n = pair * 2
        top_rows = tile_sums(n, scores_0, top_rows, n + 1, scores_1)
        top_rows = tile_sums(n + 1, scores_1, top_rows, lax.rem(n + 2, tiles), scores_0)

        @pl.when(pair == pairs // 2 - 1)
        def _():
            pl.semaphore_wait(barrier, len(greeted))
            to_sibling(0).start()

        @pl.when(pair == pairs // 2)
        def _():
            exchange_x(0)

        @pl.when(pair == pairs // 2 + 1)
        def _():
            exchange_z(0)

        return top_rows

    lax.fori_loop(0, pairs, per_pair, first_top)
    to_sibling(1).start()
    take_results(0)

    lane_row = lax.broadcasted_iota(jnp.int32, (block, 128), 1)

    def compute(step, s):
        turn = lax.rem(step, YS)
        owner_z = jnp.where(step < YS, 1 - z, z)
        at_up = (owner_z * YS + lax.rem(y + 2 * YS - 1 - turn, YS)) * block
        at_down = (owner_z * YS + lax.rem(y + 1 + turn, YS)) * block + half
        for row, at in ((0, at_up), (half, at_down)):
            source = pl.ds(pl.multiple_of(at, half), half)
            rows = pl.ds(row, half)
            k_stage[rows, :] = k_aux[source, :]
            v_stage[rows, :WIDTH] = values_ref[source, :]
            v_stage[rows, WIDTH:] = k_aux[source, WIDTH:]
            mark_stage[:, row : row + half] = onehot_t[:, source]
        k_t = k_stage[:, :WIDTH].T
        row_sums = jnp.zeros((block, 128), F32)
        grad_k = jnp.zeros((block, WIDTH), F32)
        grad_v = jnp.zeros((block, WIDTH), F32)
        lanes = pl.ds(pl.multiple_of(s * span, span), span)
        for h in range(HEADS):
            n = s * HEADS + h
            rows = slice(h * HEAD_DIM, (h + 1) * HEAD_DIM)
            p = jnp.exp2(dot(k_stage[...], q_feat[n]) * TO_LOG2)
            score_grad = p * dot(v_stage[...], g_feat[n])
            probs[h] = p.astype(BF)
            scaled[h] = (score_grad * SCALE).astype(BF)
            folded = score_grad[:, :128]
            for part in range(1, span // 128):
                folded = folded + score_grad[:, part * 128 : (part + 1) * 128]
            row_sums = row_sums + jnp.where(
                lane_row == h, jnp.sum(folded, axis=1, keepdims=True), 0.0
            )
            grad_v = grad_v + dot(probs[h], g_stack[n])
            grad_k = grad_k + dot(scaled[h], q_stack[n])
            grad_q_t[rows, lanes] += dot(k_t[rows, :], scaled[h])

        @pl.when(s == 0)
        def _():
            part_sum[step, :, :WIDTH] = grad_k
            part_sum[step, :, WIDTH:] = grad_v

        @pl.when(s == 1)
        def _():
            part_sum[step, :, :WIDTH] += grad_k
            part_sum[step, :, WIDTH:] += grad_v

        for piece in three_pieces(row_sums):
            bias_sum[:SWEEPS, :] += dot(mark_stage[...], piece)

    def rows_of(part, way):
        return pl.ds(way * half + part * quarter, quarter)

    def ring(step, part, way):
        rows = rows_of(part, way)
        return remote(
            part_sum.at[step, rows],
            from_ring.at[step, rows],
            sent_ring.at[step, part, way],
            got_ring.at[step, part, way],
            {"lat": down if way else up},
        )

    def near(part, way):
        return remote(
            part_sum.at[YS - 1, rows_of(part, way)],
            relay.at[part, way],
            sent_near.at[part, way],
            got_near.at[part, way],
            at_height(-1 if way else 1),
        )

    def far(part, way):
        return remote(
            relay.at[part, way],
            from_z.at[rows_of(part, way)],
            sent_far.at[part, way],
            got_far.at[part, way],
            at_height(1 - nz if way else nz - 1),
        )

    def finish(step, part):
        turn = lax.rem(step, YS)

        @pl.when(turn > 0)
        def _():
            for way in range(2):
                ring(step - 1, part, way).wait_recv()
                rows = rows_of(part, way)
                part_sum[step, rows, :] += from_ring[step - 1, rows, :]

        @pl.when(turn < YS - 1)
        def _():
            for way in range(2):
                ring(step, part, way).start()

        @pl.when(step == YS - 1)
        def _():
            for way in range(2):
                near(part, way).start()

    def per_item(t, unused):
        step = t // 2
        for when, value in ((1, 1), (2, 2), (3, 0), (4, 1), (5, 3), (6, 2)):
            step = jnp.where(t == when, value, step)
        s = jnp.where((t < 3) | (t == 5), 0, jnp.where(t < 8, 1, lax.rem(t, 2)))

        @pl.when(t == 3)
        def _():
            take_results(1)

        compute(step, s)

        @pl.when(t == 0)
        def _():
            exchange_x(1)

        @pl.when(t == 1)
        def _():
            exchange_z(1)

        @pl.when(t >= 3)
        def _():
            finish(jnp.where(t < 11, (t - 3) // 2, (t - 1) // 2), lax.rem(t + 1, 2))

        @pl.when((t == 9) | (t == 10))
        def _():
            finish(YS, t - 9)

        for part in range(2):

            @pl.when(t == 11 + part)
            def _():
                for way in range(2):
                    near(part, way).wait_recv()
                    far(part, way).start()

        return unused

    lax.fori_loop(0, 4 * YS, per_item, 0)

    swap = remote(q_parts.at[1 - core], from_core, sent_core, got_core, {"pts": me + 1 - 2 * core})

    def bias_y(k):
        return remote(
            bias_sum.at[pl.ds(0, SWEEPS)],
            bias_1.at[y * 2 + core],
            sent_b1.at[k],
            got_b1.at[k],
            y_peer(k),
        )

    def q_along_x(k):
        return remote(
            q_x.at[lax.rem(x + k, nx)], got_q_x.at[x], sent_qx.at[k], got_qx.at[k], x_peer(k)
        )

    def q_along_z(k):
        return remote(
            q_z.at[lax.rem(zl + k, nz)], got_q_z.at[zl], sent_qz.at[k], got_qz.at[k], z_peer(k)
        )

    def bias_along_z(k):
        return remote(bias_2, bias_z.at[height], sent_b2.at[k], got_b2.at[k], at_height(k))

    bias_copies = [bias_y(k) for k in range(1, 2 * YS)]
    x_copies = [q_along_x(k) for k in range(1, nx)]
    z_copies = [q_along_z(k) for k in range(1, nz)]
    bias_z_copies = [bias_along_z(k) for k in range(1, heights)]

    for copy in bias_copies:
        copy.start()
    grad_q = grad_q_t[...].T
    for p in range(count):
        q_parts[p % 2, p // 2] = grad_q[p * rows_out : (p + 1) * rows_out]
    swap.start()
    bias_1[y * 2 + core] = bias_sum[:SWEEPS, :]
    for copy in bias_copies:
        copy.wait_recv()
    bias = jnp.sum(bias_1[...], axis=0)
    swap.wait_recv()
    for i in range(nx):
        for j in range(nz):
            q_x[i, j * rows_out : (j + 1) * rows_out, :] = (
                q_parts[core, i * nz + j] + from_core[i * nz + j]
            )
        q_x[i, nz * rows_out :, :] = bias
    for copy in x_copies:
        copy.start()
    got_q_x[x] = q_x[x]
    finish(2 * YS - 1, 1)
    for copy in x_copies:
        copy.wait_recv()
    summed = jnp.sum(got_q_x[...], axis=0)
    bias_2[...] = summed[nz * rows_out :]
    for j in range(nz):
        q_z[j] = summed[j * rows_out : (j + 1) * rows_out]
    for copy in bias_z_copies + z_copies:
        copy.start()
    got_q_z[zl] = q_z[zl]
    bias_z[height] = bias_2[...]
    for part in range(2):
        for way in range(2):
            far(part, way).wait_recv()
    done = part_sum[2 * YS - 1] + from_z[...]
    grad_k_ref[...] = done[:, :WIDTH]
    grad_v_ref[...] = done[:, WIDTH:]
    for copy in bias_z_copies + z_copies:
        copy.wait_recv()
    small_ref[:rows_out, :] = jnp.sum(got_q_z[...], axis=0)
    small_ref[rows_out:, :] = jnp.sum(bias_z[...], axis=0)

    for s in range(2):
        to_sibling(s).wait_send()
        for k in range(1, nx):
            along_x(s, k).wait_send()
        for k in range(1, nz):
            along_z(s, k).wait_send()
    for part in range(2):
        for way in range(2):
            for step in range(2 * YS):
                if step % YS < YS - 1:
                    ring(step, part, way).wait_send()
            near(part, way).wait_send()
            far(part, way).wait_send()
    swap.wait_send()
    for copy in bias_copies + x_copies + z_copies + bias_z_copies:
        copy.wait_send()


def whole(latents, keys, values, sweep, sweep_bias, grad_out, count, lats):
    rows, points = latents.shape[0], keys.shape[0]
    block, span, chips = points // (2 * YS), rows // 2, count // 2
    cols = min(256, span)
    lines = HEADS * rows // 256
    nz = 4 if chips % 4 == 0 else chips
    nx = chips // nz
    heights = 2 * nz
    rows_out = rows // count
    dma = pltpu.SemaphoreType.DMA
    return pl.pallas_call(
        functools.partial(whole_kernel, count, lats),
        out_shape=[
            jax.ShapeDtypeStruct((block, WIDTH), F32),
            jax.ShapeDtypeStruct((block, WIDTH), F32),
            jax.ShapeDtypeStruct((rows_out + SWEEPS, WIDTH), F32),
        ],
        in_specs=vmem_specs(6),
        out_specs=vmem_specs(3),
        scratch_shapes=[
            pltpu.VMEM((points, 2 * WIDTH), BF),
            pltpu.VMEM((HEADS, 48, points), BF),
            pltpu.VMEM((SWEEPS, points), BF),
            pltpu.VMEM((WIDTH, rows), BF),
            pltpu.VMEM((2 * HEADS, 2 * WIDTH, span), BF),
            pltpu.VMEM((2 * HEADS, 2 * WIDTH, span), BF),
            pltpu.VMEM((2 * HEADS, span, WIDTH), BF),
            pltpu.VMEM((2 * HEADS, span, WIDTH), BF),
            pltpu.VMEM((points, cols), F32),
            pltpu.VMEM((points, cols), F32),
            pltpu.VMEM((2, 4, lines, 128), F32),
            pltpu.VMEM((2, 4, lines, 128), F32),
            pltpu.VMEM((2, 4, lines, 128), F32),
            pltpu.VMEM((2, nx, 4, lines, 128), F32),
            pltpu.VMEM((2, 4, lines, 128), F32),
            pltpu.VMEM((2, nz, 4, lines, 128), F32),
            pltpu.VMEM((block, 2 * WIDTH), BF),
            pltpu.VMEM((block, 2 * WIDTH), BF),
            pltpu.VMEM((SWEEPS, block), BF),
            pltpu.VMEM((HEADS, block, span), BF),
            pltpu.VMEM((HEADS, block, span), BF),
            pltpu.VMEM((2 * YS, block, 2 * WIDTH), F32),
            pltpu.VMEM((2 * YS, block, 2 * WIDTH), F32),
            pltpu.VMEM((2, 2, block // 4, 2 * WIDTH), F32),
            pltpu.VMEM((block, 2 * WIDTH), F32),
            pltpu.VMEM((WIDTH, rows), F32),
            pltpu.VMEM((128, 128), F32),
            pltpu.VMEM((2, chips, rows_out, WIDTH), F32),
            pltpu.VMEM((chips, rows_out, WIDTH), F32),
            pltpu.VMEM((2 * YS, SWEEPS, 128), F32),
            pltpu.VMEM((nx, nz * rows_out + SWEEPS, WIDTH), F32),
            pltpu.VMEM((nx, nz * rows_out + SWEEPS, WIDTH), F32),
            pltpu.VMEM((nz, rows_out, WIDTH), F32),
            pltpu.VMEM((nz, rows_out, WIDTH), F32),
            pltpu.VMEM((SWEEPS, 128), F32),
            pltpu.VMEM((heights, SWEEPS, 128), F32),
            dma((2,)),
            dma((2,)),
            dma((2, nx)),
            dma((2, nx)),
            dma((2, nz)),
            dma((2, nz)),
            dma((2 * YS, 2, 2)),
            dma((2 * YS, 2, 2)),
            dma((2, 2)),
            dma((2, 2)),
            dma((2, 2)),
            dma((2, 2)),
            dma,
            dma,
            dma((2 * YS,)),
            dma((2 * YS,)),
            dma((nx,)),
            dma((nx,)),
            dma((nz,)),
            dma((nz,)),
            dma((heights,)),
            dma((heights,)),
        ],
        compiler_params=pltpu.CompilerParams(
            collective_id=0, has_side_effects=True, vmem_limit_bytes=VMEM_BYTES
        ),
    )(latents, keys, values, sweep, sweep_bias, grad_out)


def deliver_kernel(small_ref, grad_k_ref, grad_v_ref, q_out, k_out, v_out, bias_out, square):
    rows_out = q_out.shape[0]
    q_out[...] = small_ref[:rows_out, :]
    k_out[...] = grad_k_ref[...]
    v_out[...] = grad_v_ref[...]
    square[...] = jnp.zeros_like(square)
    square[:SWEEPS, :] = small_ref[rows_out:, :]
    bias_out[...] = square[...].T[:HEADS, :SWEEPS]


def deliver(small, grad_k, grad_v):
    return pl.pallas_call(
        deliver_kernel,
        out_shape=[
            jax.ShapeDtypeStruct((small.shape[0] - SWEEPS, WIDTH), F32),
            jax.ShapeDtypeStruct(grad_k.shape, F32),
            jax.ShapeDtypeStruct(grad_v.shape, F32),
            jax.ShapeDtypeStruct((HEADS, SWEEPS), F32),
        ],
        in_specs=vmem_specs(3),
        out_specs=vmem_specs(4),
        scratch_shapes=[pltpu.VMEM((128, 128), F32)],
    )(small, grad_k, grad_v)


def per_device(count, lats, latents, keys, values, sweep, sweep_bias, grad_out):
    grad_k, grad_v, small = whole(
        latents, keys, values, sweep.reshape(1, -1), sweep_bias, grad_out, count, lats
    )
    return tuple(deliver(small, grad_k, grad_v))


def solution(mesh):
    return jax.shard_map(
        functools.partial(per_device, mesh.shape["pts"], mesh.shape["lat"]),
        mesh=mesh,
        in_specs=(P("lat", None), P("pts", None), P("pts", None), P("pts"), P(), P("lat", None)),
        out_specs=(P(("lat", "pts"), None), P(("pts", "lat"), None), P(("pts", "lat"), None), P()),
        check_vma=False,
    )
```

time: 120 us -> 110 us (0.917)
  Pallas kernels: 119 us -> 110 us
    pallas_call x1, Pallas kernels: 118 us -> 108 us  [whole(): pl.pallas_call(functools.partial(whole_kernel, count, lats), out_shape=[j...]
where the time goes in v4:
time: 110 us
  Pallas kernels  110 us (100%)
    pallas_call x1, Pallas kernels, whole(): pl.pallas_call(functools.partial(whole_kernel, count, lats), out_shape=[j...  108 us

profile of v4, /device:TPU:1, one launch (start us, length us, event | category | flops | bytes accessed | tf_op | source)
XLA Modules:
  0.0 110.2 jit_solution(8944036237624053964)
XLA Ops:
  0.6 107.7 %shard_map.93 = (f32[512,128]{1,0:T(8,128)}, f32[512,128]{1,0:T(8,128)}, f32[48,128]{1,0:T(8,128)}) custom-call(bf16[1024,128]{1,0:T(8,128)(2,1)} %latents_ref.1, bf16[4096,128]{1,0:T(8,128)(2,1)} %keys_ref.1, bf16[4096,128]{1,0:T(8,128)(2,1)} %values_ref.1, s32[1,4096]{1,0:T(1,128)} %bitcast.1, f32[4,16]{1,0:T(4,128)} %sweep_bias_ref.1, ...), custom_call_target="tpu_custom_call" | custom-call | tf_op jit(solution)/shard_map/pallas_call | solution.py:604
  108.3 1.9 %shard_map.94 = (f32[32,128]{1,0:T(8,128)}, f32[512,128]{1,0:T(8,128)}, f32[512,128]{1,0:T(8,128)}, f32[4,16]{1,0:T(4,128)}) custom-call(f32[48,128]{1,0:T(8,128)} %get-tuple-element.7.small_ref, f32[512,128]{1,0:T(8,128)} %get-tuple-element.8.grad_k_ref, f32[512,128]{1,0:T(8,128)} %get-tuple-element.9.grad_v_ref), custom_call_target="tpu_custom_call" | custom-call | tf_op jit(solution)/shard_map/pallas_call | solution.py:690

commit v5 on v4

--- a/solution.py
+++ b/solution.py
@@ -27,6 +27,10 @@
     return jnp.dot(a, b, preferred_element_type=F32)
 
 
+def dot_transposed(a, b):
+    return lax.dot_general(a, b, (((1,), (1,)), ((), ())), preferred_element_type=F32)
+
+
 def three_pieces(x):
     hi = x.astype(BF)
     rest = x - hi.astype(F32)
@@ -48,8 +52,7 @@
     sweep_ref,
     sweep_bias_ref,
     grad_out_ref,
-    grad_k_ref,
-    grad_v_ref,
+    grads_ref,
     small_ref,
     k_aux,
     value_rows,
@@ -57,8 +60,6 @@
     g_t,
     q_feat,
     g_feat,
-    q_stack,
-    g_stack,
     scores_0,
     scores_1,
     stats,
@@ -196,7 +197,6 @@
     every(0, chunks, build)
     q_t = latents_ref[...].T
     g_t[...] = grad_out_ref[...].T
-    lane = lax.broadcasted_iota(jnp.int32, (span, WIDTH), 1)
     eye = lax.broadcasted_iota(jnp.int32, (SWEEPS, SWEEPS), 0) == lax.broadcasted_iota(
         jnp.int32, (SWEEPS, SWEEPS), 1
     )
@@ -206,12 +206,9 @@
             jnp.where(eye, sweep_bias_ref[h : h + 1, :], 0.0), axis=1, keepdims=True
         ) * (1.0 / SCALE)
         bias_pieces = three_pieces(jnp.broadcast_to(column, (SWEEPS, span)))
-        mine_lanes = (lane >= h * HEAD_DIM) & (lane < (h + 1) * HEAD_DIM)
         for s in range(2):
             n = s * HEADS + h
             here = slice(s * span, (s + 1) * span)
-            for source, stack in ((latents_ref, q_stack), (grad_out_ref, g_stack)):
-                stack[n] = jnp.where(mine_lanes, source[here, :].astype(F32), 0.0).astype(BF)
             q_feat[n] = jnp.zeros((2 * WIDTH, span), BF)
             g_feat[n] = jnp.zeros((2 * WIDTH, span), BF)
             q_feat[n, rows, :] = q_t[rows, here]
@@ -220,11 +217,12 @@
                 q_feat[n, WIDTH + index * SWEEPS : WIDTH + (index + 1) * SWEEPS, :] = piece
     grad_q_t[...] = jnp.zeros_like(grad_q_t)
     bias_sum[...] = jnp.zeros_like(bias_sum)
+    part_sum[...] = jnp.zeros_like(part_sum)
 
     def merge(parts):
         best = functools.reduce(jnp.maximum, [part[0] for part in parts])
         weights = [jnp.exp2(part[0] - best) for part in parts]
-        sums = [sum(w * part[kind] for w, part in zip(weights, parts)) for kind in (1, 2, 3)]
+        sums = [sum(w * part[kind] for w, part in zip(weights, parts)) for kind in (1, 2)]
         return [best] + sums
 
     def keep(ref, merged):
@@ -266,9 +264,9 @@
     def take_results(s):
         for k in range(1, nz):
             along_z(s, k).wait_recv()
-        best, total, weighted, rounded_total = merge([stats_z[s, i] for i in range(nz)])
+        best, total, weighted = merge([stats_z[s, i] for i in range(nz)])
         offset = (best + jnp.log(total) * LOG2E) * (-1.0 / TO_LOG2)
-        delta = -(weighted / rounded_total)
+        delta = -(weighted / total)
         row16 = lax.broadcasted_iota(jnp.int32, (16, 128), 0)
         per_tile = cols // 128
         for n in range(tiles // 2):
@@ -310,23 +308,20 @@
         top = jnp.max(top_rows, axis=0, keepdims=True)
         head = lax.rem(n, HEADS)
         next_top = lowest
-        total = jnp.zeros((32, cols), F32)
         out = jnp.zeros((48, cols), F32)
         for c in range(chunks):
             rows = pl.ds(c * chunk, chunk)
             e = jnp.exp2(scores[rows, :] - top)
-            total = total + jnp.sum(e.reshape(chunk // 32, 32, cols), axis=0)
             out = out + dot(value_rows[head, :, rows], e.astype(BF))
             next_top = score_chunk(following, into, c, next_top)
-        total = jnp.sum(total, axis=0, keepdims=True)
         g = g_t[
             pl.ds(pl.multiple_of(head * HEAD_DIM, HEAD_DIM), HEAD_DIM),
             pl.ds(pl.multiple_of((n // HEADS) * cols, cols), cols),
         ].astype(F32)
         weighted = jnp.sum(out[:HEAD_DIM] * g, axis=0, keepdims=True)
-        rounded_total = out[HEAD_DIM : HEAD_DIM + 1]
+        total = out[HEAD_DIM : HEAD_DIM + 1]
         per_tile = cols // 128
-        for kind, value in enumerate((top, total, weighted, rounded_total)):
+        for kind, value in enumerate((top, total, weighted)):
             for part in range(per_tile):
                 line = lax.rem(n, tiles // 2) * per_tile + part
                 stats[n // (tiles // 2), kind, pl.ds(line, 1), :] = value[
@@ -378,8 +373,6 @@
             mark_stage[:, row : row + half] = onehot_t[:, source]
         k_t = k_stage[:, :WIDTH].T
         row_sums = jnp.zeros((block, 128), F32)
-        grad_k = jnp.zeros((block, WIDTH), F32)
-        grad_v = jnp.zeros((block, WIDTH), F32)
         lanes = pl.ds(pl.multiple_of(s * span, span), span)
         for h in range(HEADS):
             n = s * HEADS + h
@@ -394,31 +387,23 @@
             row_sums = row_sums + jnp.where(
                 lane_row == h, jnp.sum(folded, axis=1, keepdims=True), 0.0
             )
-            grad_v = grad_v + dot(probs[h], g_stack[n])
-            grad_k = grad_k + dot(scaled[h], q_stack[n])
+            part_sum[step, rows, :] += dot_transposed(q_feat[n, rows, :], scaled[h])
+            part_sum[step, WIDTH + h * HEAD_DIM : WIDTH + (h + 1) * HEAD_DIM, :] += dot_transposed(
+                g_feat[n, rows, :], probs[h]
+            )
             grad_q_t[rows, lanes] += dot(k_t[rows, :], scaled[h])
-
-        @pl.when(s == 0)
-        def _():
-            part_sum[step, :, :WIDTH] = grad_k
-            part_sum[step, :, WIDTH:] = grad_v
-
-        @pl.when(s == 1)
-        def _():
-            part_sum[step, :, :WIDTH] += grad_k
-            part_sum[step, :, WIDTH:] += grad_v
 
         for piece in three_pieces(row_sums):
             bias_sum[:SWEEPS, :] += dot(mark_stage[...], piece)
 
-    def rows_of(part, way):
-        return pl.ds(way * half + part * quarter, quarter)
+    def lanes_of(part, way):
+        return pl.ds(pl.multiple_of(way * half + part * quarter, quarter), quarter)
 
     def ring(step, part, way):
-        rows = rows_of(part, way)
-        return remote(
-            part_sum.at[step, rows],
-            from_ring.at[step, rows],
+        here = lanes_of(part, way)
+        return remote(
+            part_sum.at[step, :, here],
+            from_ring.at[step, :, here],
             sent_ring.at[step, part, way],
             got_ring.at[step, part, way],
             {"lat": down if way else up},
@@ -426,7 +411,7 @@
 
     def near(part, way):
         return remote(
-            part_sum.at[YS - 1, rows_of(part, way)],
+            part_sum.at[YS - 1, :, lanes_of(part, way)],
             relay.at[part, way],
             sent_near.at[part, way],
             got_near.at[part, way],
@@ -436,7 +421,7 @@
     def far(part, way):
         return remote(
             relay.at[part, way],
-            from_z.at[rows_of(part, way)],
+            from_z.at[:, lanes_of(part, way)],
             sent_far.at[part, way],
             got_far.at[part, way],
             at_height(1 - nz if way else nz - 1),
@@ -449,8 +434,8 @@
         def _():
             for way in range(2):
                 ring(step - 1, part, way).wait_recv()
-                rows = rows_of(part, way)
-                part_sum[step, rows, :] += from_ring[step - 1, rows, :]
+                here = lanes_of(part, way)
+                part_sum[step, :, here] += from_ring[step - 1, :, here]
 
         @pl.when(turn < YS - 1)
         def _():
@@ -565,9 +550,7 @@
     for part in range(2):
         for way in range(2):
             far(part, way).wait_recv()
-    done = part_sum[2 * YS - 1] + from_z[...]
-    grad_k_ref[...] = done[:, :WIDTH]
-    grad_v_ref[...] = done[:, WIDTH:]
+    grads_ref[...] = part_sum[2 * YS - 1] + from_z[...]
     for copy in bias_z_copies + z_copies:
         copy.wait_recv()
     small_ref[:rows_out, :] = jnp.sum(got_q_z[...], axis=0)
@@ -604,12 +587,11 @@
     return pl.pallas_call(
         functools.partial(whole_kernel, count, lats),
         out_shape=[
-            jax.ShapeDtypeStruct((block, WIDTH), F32),
-            jax.ShapeDtypeStruct((block, WIDTH), F32),
+            jax.ShapeDtypeStruct((2 * WIDTH, block), F32),
             jax.ShapeDtypeStruct((rows_out + SWEEPS, WIDTH), F32),
         ],
         in_specs=vmem_specs(6),
-        out_specs=vmem_specs(3),
+        out_specs=vmem_specs(2),
         scratch_shapes=[
             pltpu.VMEM((points, 2 * WIDTH), BF),
             pltpu.VMEM((HEADS, 48, points), BF),
@@ -617,25 +599,23 @@
             pltpu.VMEM((WIDTH, rows), BF),
             pltpu.VMEM((2 * HEADS, 2 * WIDTH, span), BF),
             pltpu.VMEM((2 * HEADS, 2 * WIDTH, span), BF),
-            pltpu.VMEM((2 * HEADS, span, WIDTH), BF),
-            pltpu.VMEM((2 * HEADS, span, WIDTH), BF),
             pltpu.VMEM((points, cols), F32),
             pltpu.VMEM((points, cols), F32),
-            pltpu.VMEM((2, 4, lines, 128), F32),
-            pltpu.VMEM((2, 4, lines, 128), F32),
-            pltpu.VMEM((2, 4, lines, 128), F32),
-            pltpu.VMEM((2, nx, 4, lines, 128), F32),
-            pltpu.VMEM((2, 4, lines, 128), F32),
-            pltpu.VMEM((2, nz, 4, lines, 128), F32),
+            pltpu.VMEM((2, 3, lines, 128), F32),
+            pltpu.VMEM((2, 3, lines, 128), F32),
+            pltpu.VMEM((2, 3, lines, 128), F32),
+            pltpu.VMEM((2, nx, 3, lines, 128), F32),
+            pltpu.VMEM((2, 3, lines, 128), F32),
+            pltpu.VMEM((2, nz, 3, lines, 128), F32),
             pltpu.VMEM((block, 2 * WIDTH), BF),
             pltpu.VMEM((block, 2 * WIDTH), BF),
             pltpu.VMEM((SWEEPS, block), BF),
             pltpu.VMEM((HEADS, block, span), BF),
             pltpu.VMEM((HEADS, block, span), BF),
-            pltpu.VMEM((2 * YS, block, 2 * WIDTH), F32),
-            pltpu.VMEM((2 * YS, block, 2 * WIDTH), F32),
-            pltpu.VMEM((2, 2, block // 4, 2 * WIDTH), F32),
-            pltpu.VMEM((block, 2 * WIDTH), F32),
+            pltpu.VMEM((2 * YS, 2 * WIDTH, block), F32),
+            pltpu.VMEM((2 * YS, 2 * WIDTH, block), F32),
+            pltpu.VMEM((2, 2, 2 * WIDTH, block // 4), F32),
+            pltpu.VMEM((2 * WIDTH, block), F32),
             pltpu.VMEM((WIDTH, rows), F32),
             pltpu.VMEM((128, 128), F32),
             pltpu.VMEM((2, chips, rows_out, WIDTH), F32),
@@ -676,36 +656,37 @@
     )(latents, keys, values, sweep, sweep_bias, grad_out)
 
 
-def deliver_kernel(small_ref, grad_k_ref, grad_v_ref, q_out, k_out, v_out, bias_out, square):
+def deliver_kernel(small_ref, grads_ref, q_out, k_out, v_out, bias_out, square):
     rows_out = q_out.shape[0]
     q_out[...] = small_ref[:rows_out, :]
-    k_out[...] = grad_k_ref[...]
-    v_out[...] = grad_v_ref[...]
+    k_out[...] = grads_ref[:WIDTH, :].T
+    v_out[...] = grads_ref[WIDTH:, :].T
     square[...] = jnp.zeros_like(square)
     square[:SWEEPS, :] = small_ref[rows_out:, :]
     bias_out[...] = square[...].T[:HEADS, :SWEEPS]
 
 
-def deliver(small, grad_k, grad_v):
+def deliver(small, grads):
+    block = grads.shape[1]
     return pl.pallas_call(
         deliver_kernel,
         out_shape=[
             jax.ShapeDtypeStruct((small.shape[0] - SWEEPS, WIDTH), F32),
-            jax.ShapeDtypeStruct(grad_k.shape, F32),
-            jax.ShapeDtypeStruct(grad_v.shape, F32),
+            jax.ShapeDtypeStruct((block, WIDTH), F32),
+            jax.ShapeDtypeStruct((block, WIDTH), F32),
             jax.ShapeDtypeStruct((HEADS, SWEEPS), F32),
         ],
-        in_specs=vmem_specs(3),
+        in_specs=vmem_specs(2),
         out_specs=vmem_specs(4),
         scratch_shapes=[pltpu.VMEM((128, 128), F32)],
-    )(small, grad_k, grad_v)
+    )(small, grads)
 
 
 def per_device(count, lats, latents, keys, values, sweep, sweep_bias, grad_out):
-    grad_k, grad_v, small = whole(
+    grads, small = whole(
         latents, keys, values, sweep.reshape(1, -1), sweep_bias, grad_out, count, lats
     )
-    return tuple(deliver(small, grad_k, grad_v))
+    return tuple(deliver(small, grads))
 
 
 def solution(mesh):

time: 110 us -> 108 us (0.982)
  Pallas kernels: 110 us -> 107 us
    pallas_call x1, Pallas kernels: 108 us -> 105 us  [whole(): pl.pallas_call(functools.partial(whole_kernel, count, lats), out_shape=[j...]
where the time goes in v5:
time: 108 us; the launch traced here: 107 us
  Pallas kernels  107 us (99%)
    pallas_call x1, Pallas kernels, whole(): pl.pallas_call(functools.partial(whole_kernel, count, lats), out_shape=[j...  105 us

profile of v5, /device:TPU:1, one launch (start us, length us, event | category | flops | bytes accessed | tf_op | source)
XLA Modules:
  0.0 107.2 jit_solution(17071298105623369902)
XLA Ops:
  0.6 104.6 %shard_map.93 = (f32[256,512]{1,0:T(8,128)}, f32[48,128]{1,0:T(8,128)}) custom-call(bf16[1024,128]{1,0:T(8,128)(2,1)} %latents_ref.1, bf16[4096,128]{1,0:T(8,128)(2,1)} %keys_ref.1, bf16[4096,128]{1,0:T(8,128)(2,1)} %values_ref.1, s32[1,4096]{1,0:T(1,128)} %bitcast.1, f32[4,16]{1,0:T(4,128)} %sweep_bias_ref.1, bf16[1024,128]{1,0:T(8,128)(2,1)} %grad_out_ref.1), custom_call_target="tpu_custom_call" | custom-call | tf_op jit(solution)/shard_map/pallas_call | solution.py:587
  105.2 2.0 %shard_map.94 = (f32[32,128]{1,0:T(8,128)}, f32[512,128]{1,0:T(8,128)}, f32[512,128]{1,0:T(8,128)}, f32[4,16]{1,0:T(4,128)}) custom-call(f32[48,128]{1,0:T(8,128)} %get-tuple-element.6.small_ref, f32[256,512]{1,0:T(8,128)} %get-tuple-element.7.grads_ref), custom_call_target="tpu_custom_call" | custom-call | tf_op jit(solution)/shard_map/pallas_call | solution.py:671

commit v6 on v5

v6 whole, which is shorter than its diff:
```python
import functools
import math

import jax
import jax.numpy as jnp
from jax import lax
from jax.experimental import pallas as pl
from jax.experimental.pallas import tpu as pltpu
from jax.sharding import PartitionSpec as P

HEADS = 4
HEAD_DIM = 32
WIDTH = HEADS * HEAD_DIM
SWEEPS = 16
SCALE = HEAD_DIM**-0.5
LOG2E = math.log2(math.e)
TO_LOG2 = SCALE * LOG2E
YS = 4
ONES_ROW = 3 * SWEEPS
BF = jnp.bfloat16
F32 = jnp.float32
MESH = pl.DeviceIdType.MESH
VMEM_BYTES = 56 * 1024 * 1024


def dot(a, b):
    return jnp.dot(a, b, preferred_element_type=F32)


def dot_transposed(a, b):
    return lax.dot_general(a, b, (((1,), (1,)), ((), ())), preferred_element_type=F32)


def three_pieces(x):
    hi = x.astype(BF)
    rest = x - hi.astype(F32)
    mid = rest.astype(BF)
    low = (rest - mid.astype(F32)).astype(BF)
    return hi, mid, low


def vmem_specs(count):
    return [pl.BlockSpec(memory_space=pltpu.VMEM)] * count


def whole_kernel(
    count,
    lats,
    latents_ref,
    keys_ref,
    values_ref,
    sweep_ref,
    sweep_bias_ref,
    grad_out_ref,
    grads_ref,
    small_ref,
    k_aux,
    value_rows,
    onehot_t,
    own_rows,
    other_rows,
    g_t,
    q_feat,
    g_feat,
    scores_0,
    scores_1,
    stats,
    from_sibling,
    stats_1,
    stats_x,
    stats_2,
    stats_z,
    result,
    results,
    k_stage,
    v_stage,
    mark_stage,
    probs,
    scaled,
    part_sum,
    from_ring,
    grad_q_t,
    bias_sum,
    q_parts,
    from_core,
    bias_1,
    q_x,
    got_q_x,
    q_z,
    got_q_z,
    bias_2,
    bias_z,
    sent_lz,
    got_lz,
    sent_lx,
    got_lx,
    sent_lc,
    got_lc,
    sent_s1,
    got_s1,
    sent_sx,
    got_sx,
    sent_sz,
    got_sz,
    sent_sr,
    got_sr,
    sent_ring,
    got_ring,
    sent_core,
    got_core,
    sent_b1,
    got_b1,
    sent_qx,
    got_qx,
    sent_qz,
    got_qz,
    sent_b2,
    got_b2,
):
    latents = latents_ref.shape[0]
    points = keys_ref.shape[0] // 2
    span = latents // 2
    cols = min(256, span)
    per_span = span // cols
    per_tile = cols // 128
    group_tiles = HEADS * per_span
    group_lines = group_tiles * per_tile
    tiles = 4 * group_tiles
    group_pairs = group_tiles // 2
    chunk = min(512, points)
    chunks = points // chunk
    block = points // YS
    half = block // 2
    chips = count // 2
    nz = 4 if chips % 4 == 0 else chips
    nx = chips // nz
    heights = 2 * nz
    near = nz // 2
    rows_out = latents // count
    slice_rows = span // (2 * nx)
    lines = stats.shape[2] // nx

    me = lax.axis_index("pts")
    lat = lax.axis_index("lat")
    core = lax.rem(me, 2)
    chip = me // 2
    z, y = lat // YS, lax.rem(lat, YS)
    up = z * YS + lax.rem(y + 1, YS)
    down = z * YS + lax.rem(y + YS - 1, YS)
    x, zl = chip // nz, lax.rem(chip, nz)
    height = z * nz + zl
    sibling = {"pts": me + 1 - 2 * core}

    def x_peer(k):
        return {"pts": (lax.rem(x + k, nx) * nz + zl) * 2 + core}

    def y_peer(k):
        there = lax.rem(y * 2 + core + k, 2 * YS)
        return {"pts": chip * 2 + lax.rem(there, 2), "lat": z * YS + there // 2}

    def at_height(there):
        return {"pts": (x * nz + lax.rem(there, nz)) * 2 + core, "lat": (there // nz) * YS + y}

    def height_peer(k):
        return at_height(lax.rem(height + k, heights))

    def remote(src, dst, sent, got, device):
        return pltpu.make_async_remote_copy(
            src_ref=src,
            dst_ref=dst,
            send_sem=sent,
            recv_sem=got,
            device_id=device,
            device_id_type=MESH,
        )

    barrier = pltpu.get_barrier_semaphore()
    greeted = (
        [x_peer(k) for k in range(1, nx)]
        + [height_peer(k) for k in range(1, heights)]
        + [y_peer(k) for k in range(1, 2 * YS)]
    )
    for device in greeted:
        pl.semaphore_signal(barrier, inc=1, device_id=device, device_id_type=MESH)

    order = [p for parity in range(2) for p in range(count) if (p // 2) % 2 == parity]
    for at, p in enumerate(order):
        to, of = slice(at * rows_out, (at + 1) * rows_out), slice(p * rows_out, (p + 1) * rows_out)
        own_rows[to, :WIDTH] = latents_ref[of, :].astype(F32)
        own_rows[to, WIDTH:] = grad_out_ref[of, :].astype(F32)

    def other_z(s):
        first = s * span + (core * nx + x) * slice_rows
        return remote(
            own_rows.at[pl.ds(pl.multiple_of(first, slice_rows), slice_rows)],
            other_rows.at[s, core, x],
            sent_lz.at[s],
            got_lz.at[s],
            at_height(heights - 1 - height),
        )

    def other_x(s, k):
        return remote(
            other_rows.at[s, core, x],
            other_rows.at[s, core, x],
            sent_lx.at[s, k],
            got_lx.at[s, k],
            x_peer(k),
        )

    def other_core(s):
        return remote(
            other_rows.at[s, core], other_rows.at[s, core], sent_lc.at[s], got_lc.at[s], sibling
        )

    def forward_x(s):
        other_z(s).wait_recv()
        for k in range(1, nx):
            other_x(s, k).start()

    def forward_core(s):
        for k in range(1, nx):
            other_x(s, k).wait_recv()
        other_core(s).start()

    pl.semaphore_wait(barrier, len(greeted))
    for s in range(2):
        other_z(s).start()

    base = z * points
    k_aux[:, :WIDTH] = keys_ref[pl.ds(pl.multiple_of(base, points), points), :]

    def build(c, unused):
        rows = pl.ds(pl.multiple_of(c * chunk, chunk), chunk)
        source = pl.ds(pl.multiple_of(base + c * chunk, chunk), chunk)
        swept = sweep_ref[:, source]
        row = lax.broadcasted_iota(jnp.int32, (WIDTH, chunk), 0)
        marked = (row < ONES_ROW) & (lax.rem(row, SWEEPS) == swept)
        ones = (row >= ONES_ROW) & (row < ONES_ROW + 3)
        aux_t = jnp.where(marked | ones, 1.0, 0.0)
        onehot_t[:, rows] = aux_t[:SWEEPS].astype(BF)
        k_aux[rows, WIDTH:] = aux_t.T.astype(BF)
        value_t = values_ref[source, :].T
        for h in range(HEADS):
            value_rows[h, :HEAD_DIM, rows] = value_t[h * HEAD_DIM : (h + 1) * HEAD_DIM, :]
            value_rows[h, HEAD_DIM:, rows] = jnp.where(row[:16] == 0, 1.0, 0.0).astype(BF)
        return unused

    lax.fori_loop(0, chunks, build, 0)
    eye = lax.broadcasted_iota(jnp.int32, (SWEEPS, SWEEPS), 0) == lax.broadcasted_iota(
        jnp.int32, (SWEEPS, SWEEPS), 1
    )

    def features(g, both):
        q_t = both[:, :WIDTH].T.astype(BF)
        out_t = both[:, WIDTH:].T.astype(BF)
        g_t[:, g * span : (g + 1) * span] = out_t
        for h in range(HEADS):
            rows = slice(h * HEAD_DIM, (h + 1) * HEAD_DIM)
            column = jnp.sum(
                jnp.where(eye, sweep_bias_ref[h : h + 1, :], 0.0), axis=1, keepdims=True
            ) * (1.0 / SCALE)
            n = g * HEADS + h
            q_feat[n] = jnp.zeros((2 * WIDTH, span), BF)
            g_feat[n] = jnp.zeros((2 * WIDTH, span), BF)
            q_feat[n, rows, :] = q_t[rows]
            g_feat[n, rows, :] = out_t[rows]
            for index, piece in enumerate(
                three_pieces(jnp.broadcast_to(column, (SWEEPS, span)))
            ):
                q_feat[n, WIDTH + index * SWEEPS : WIDTH + (index + 1) * SWEEPS, :] = piece

    def take_other(s):
        other_core(s).wait_recv()
        features(2 + s, other_rows[s].reshape(span, 2 * WIDTH))

    for s in range(2):
        features(s, own_rows[s * span : (s + 1) * span, :])
    forward_x(0)
    grad_q_t[...] = jnp.zeros_like(grad_q_t)
    bias_sum[...] = jnp.zeros_like(bias_sum)
    part_sum[...] = jnp.zeros_like(part_sum)

    def merge(parts):
        best = functools.reduce(jnp.maximum, [part[0] for part in parts])
        weights = [jnp.exp2(part[0] - best) for part in parts]
        sums = [sum(w * part[kind] for w, part in zip(weights, parts)) for kind in (1, 2)]
        return [best] + sums

    def share_of(there):
        return pl.ds(pl.multiple_of(there * lines, lines), lines)

    def to_sibling(s):
        return remote(stats.at[s], from_sibling.at[s], sent_s1.at[s], got_s1.at[s], sibling)

    def along_x(s, k):
        return remote(
            stats_1.at[s, :, share_of(lax.rem(x + k, nx))],
            stats_x.at[s, x],
            sent_sx.at[s, k],
            got_sx.at[s, k],
            x_peer(k),
        )

    def along_z(s, k):
        return remote(
            stats_2.at[s], stats_z.at[s, height], sent_sz.at[s, k], got_sz.at[s, k], height_peer(k)
        )

    def results_x(s, k):
        return remote(
            result.at[s], results.at[s, x], sent_sr.at[s, k], got_sr.at[s, k], x_peer(k)
        )

    def exchange_x(s):
        to_sibling(s).wait_recv()
        merged = merge([stats[s], from_sibling[s]])
        for kind, value in enumerate(merged):
            stats_1[s, kind] = value
        for k in range(1, nx):
            along_x(s, k).start()
        stats_x[s, x] = stats_1[s, :, share_of(x), :]

    def exchange_z(s):
        for k in range(1, nx):
            along_x(s, k).wait_recv()
        for kind, value in enumerate(merge([stats_x[s, i] for i in range(nx)])):
            stats_2[s, kind] = value
        for k in range(1, heights):
            along_z(s, k).start()
        stats_z[s, height] = stats_2[s]

    def exchange_results(s):
        for k in range(1, heights):
            along_z(s, k).wait_recv()
        best, total, weighted = merge([stats_z[s, i] for i in range(heights)])
        result[s, 0] = (best + jnp.log(total) * LOG2E) * (-1.0 / TO_LOG2)
        result[s, 1] = -(weighted / total)
        for k in range(1, nx):
            results_x(s, k).start()
        results[s, x] = result[s]

    def take_results(s):
        for k in range(1, nx):
            results_x(s, k).wait_recv()
        row16 = lax.broadcasted_iota(jnp.int32, (16, 128), 0)
        for side in range(2):
            whose = z if side == 0 else 1 - z
            for n in range(group_tiles):
                it, h = n // HEADS, n % HEADS
                for part in range(per_tile):
                    line = whose * group_lines + n * per_tile + part
                    left = it * cols + part * 128
                    for kind, feat in ((0, q_feat), (1, g_feat)):
                        value = results[s, line // lines, kind, pl.ds(lax.rem(line, lines), 1), :]
                        hi, mid, low = three_pieces(value)
                        feat[
                            (2 * side + s) * HEADS + h,
                            WIDTH + ONES_ROW : WIDTH + ONES_ROW + 16,
                            left : left + 128,
                        ] = jnp.where(
                            row16 == 0,
                            hi.astype(F32),
                            jnp.where(
                                row16 == 1,
                                mid.astype(F32),
                                jnp.where(row16 == 2, low.astype(F32), 0.0),
                            ),
                        ).astype(BF)

    lowest = jnp.full((32, cols), -jnp.inf, F32)

    def tile_lanes(n):
        return pl.ds(pl.multiple_of((lax.rem(n, group_tiles) // HEADS) * cols, cols), cols)

    def score_chunk(n, into, c, top):
        index = (n // group_tiles) * HEADS + lax.rem(n, HEADS)
        rows = pl.ds(c * chunk, chunk)
        s = dot(k_aux[rows, :], q_feat[index, :, tile_lanes(n)]) * TO_LOG2
        into[rows, :] = s
        return jnp.maximum(top, jnp.max(s.reshape(chunk // 32, 32, cols), axis=0))

    def tile_sums(n, scores, top_rows, following, into):
        top = jnp.max(top_rows, axis=0, keepdims=True)
        head = lax.rem(n, HEADS)
        next_top = lowest
        out = jnp.zeros((48, cols), F32)
        for c in range(chunks):
            rows = pl.ds(c * chunk, chunk)
            e = jnp.exp2(scores[rows, :] - top)
            out = out + dot(value_rows[head, :, rows], e.astype(BF))
            next_top = score_chunk(following, into, c, next_top)
        group = n // group_tiles
        g = g_t[
            pl.ds(pl.multiple_of(head * HEAD_DIM, HEAD_DIM), HEAD_DIM),
            pl.ds(
                pl.multiple_of(group * span + (lax.rem(n, group_tiles) // HEADS) * cols, cols), cols
            ),
        ].astype(F32)
        weighted = jnp.sum(out[:HEAD_DIM] * g, axis=0, keepdims=True)
        total = out[HEAD_DIM : HEAD_DIM + 1]
        whose = jnp.where(group < 2, z, 1 - z)
        for kind, value in enumerate((top, total, weighted)):
            for part in range(per_tile):
                line = whose * group_lines + lax.rem(n, group_tiles) * per_tile + part
                stats[lax.rem(group, 2), kind, pl.ds(line, 1), :] = value[
                    :, part * 128 : (part + 1) * 128
                ]
        return next_top

    first_top = lowest
    for c in range(chunks):
        first_top = score_chunk(0, scores_0, c, first_top)

    def per_pair(pair, top_rows):
        n = pair * 2

        @pl.when(pair == 2 * group_pairs - 1)
        def _():
            take_other(0)

        @pl.when(pair == 3 * group_pairs - 1)
        def _():
            take_other(1)

        top_rows = tile_sums(n, scores_0, top_rows, n + 1, scores_1)
        top_rows = tile_sums(n + 1, scores_1, top_rows, lax.rem(n + 2, tiles), scores_0)

        @pl.when(pair == group_pairs // 2 - 1)
        def _():
            forward_x(1)

        @pl.when(pair == group_pairs - 1)
        def _():
            forward_core(0)

        @pl.when(pair == group_pairs + group_pairs // 2)
        def _():
            forward_core(1)

        @pl.when(pair == 3 * group_pairs - 1)
        def _():
            to_sibling(0).start()

        @pl.when(pair == 3 * group_pairs)
        def _():
            exchange_x(0)

        @pl.when(pair == max(3 * group_pairs + 1, 4 * group_pairs - 3))
        def _():
            exchange_z(0)

        @pl.when(pair == 4 * group_pairs - 1)
        def _():
            exchange_results(0)

        return top_rows

    lax.fori_loop(0, 4 * group_pairs, per_pair, first_top)
    to_sibling(1).start()
    take_results(0)

    lane_row = lax.broadcasted_iota(jnp.int32, (block, 128), 1)

    def compute(step, g):
        y_up = lax.rem(y + 2 * YS - 1 - step, YS)
        y_down = lax.rem(y + 1 + step, YS)
        for row, at in ((0, y_up * block), (half, y_down * block + half)):
            here = pl.ds(pl.multiple_of(at, half), half)
            rows = pl.ds(row, half)
            k_stage[rows, :] = k_aux[here, :]
            v_stage[rows, :WIDTH] = values_ref[pl.ds(pl.multiple_of(base + at, half), half), :]
            v_stage[rows, WIDTH:] = k_aux[here, WIDTH:]
            mark_stage[:, row : row + half] = onehot_t[:, here]
        k_t = k_stage[:, :WIDTH].T
        row_sums = jnp.zeros((block, 128), F32)
        lanes = pl.ds(pl.multiple_of(g * span, span), span)
        for h in range(HEADS):
            n = g * HEADS + h
            rows = slice(h * HEAD_DIM, (h + 1) * HEAD_DIM)
            p = jnp.exp2(dot(k_stage[...], q_feat[n]) * TO_LOG2)
            score_grad = p * dot(v_stage[...], g_feat[n])
            probs[h] = p.astype(BF)
            scaled[h] = (score_grad * SCALE).astype(BF)
            folded = score_grad[:, :128]
            for part in range(1, span // 128):
                folded = folded + score_grad[:, part * 128 : (part + 1) * 128]
            row_sums = row_sums + jnp.where(
                lane_row == h, jnp.sum(folded, axis=1, keepdims=True), 0.0
            )
            part_sum[step, rows, :] += dot_transposed(q_feat[n, rows, :], scaled[h])
            part_sum[step, WIDTH + h * HEAD_DIM : WIDTH + (h + 1) * HEAD_DIM, :] += dot_transposed(
                g_feat[n, rows, :], probs[h]
            )
            grad_q_t[rows, lanes] += dot(k_t[rows, :], scaled[h])
        for piece in three_pieces(row_sums):
            bias_sum[:SWEEPS, :] += dot(mark_stage[...], piece)

    def ring(step, way):
        here = pl.ds(way * half, half)
        return remote(
            part_sum.at[step, :, here],
            from_ring.at[step, :, here],
            sent_ring.at[step, way],
            got_ring.at[step, way],
            {"lat": down if way else up},
        )

    def finish(step):
        if step > 0:
            for way in range(2):
                ring(step - 1, way).wait_recv()
            part_sum[step] += from_ring[step - 1]
        if step < YS - 1:
            for way in range(2):
                ring(step, way).start()

    def swap(s):
        return remote(
            q_parts.at[s, 1 - core], from_core.at[s], sent_core.at[s], got_core.at[s], sibling
        )

    def q_along_x(s, k):
        rows = near * 2 * rows_out + s * SWEEPS
        return remote(
            q_x.at[s, lax.rem(x + k, nx), pl.ds(0, rows)],
            got_q_x.at[s, x, pl.ds(0, rows)],
            sent_qx.at[s, k],
            got_qx.at[s, k],
            x_peer(k),
        )

    def start_swap(s):
        for side in range(2):
            g = 2 * side + s
            whose = z if side == 0 else 1 - z
            grad_q = grad_q_t[:, g * span : (g + 1) * span].T
            for j in range(chips):
                m = j // 2
                q_parts[s, j % 2, m // near, whose * near + m % near] = grad_q[
                    j * rows_out : (j + 1) * rows_out
                ]
        swap(s).start()

    def send_x(s, bias):
        swap(s).wait_recv()
        for i in range(nx):
            for j in range(2 * near):
                q_x[s, i, j * rows_out : (j + 1) * rows_out, :] = (
                    q_parts[s, core, i, j] + from_core[s, i, j]
                )
            if bias is not None:
                q_x[s, i, 2 * near * rows_out :, :] = bias
        for k in range(1, nx):
            q_along_x(s, k).start()
        got_q_x[s, x] = q_x[s, x]

    def height_copies(s, action):
        for j in range(2 * near):
            there = (j // near) * nz + 2 * (j % near) + s

            @pl.when(height != there)
            def _():
                action(
                    remote(
                        q_z.at[s, j],
                        got_q_z.at[height],
                        sent_qz.at[there],
                        got_qz.at[height],
                        at_height(there),
                    )
                )

            if action is start:

                @pl.when(height == there)
                def _():
                    got_q_z[height] = q_z[s, j]

    def start(copy):
        copy.start()

    def wait_send(copy):
        copy.wait_send()

    def send_z(s):
        for k in range(1, nx):
            q_along_x(s, k).wait_recv()
        summed = jnp.sum(got_q_x[s, :, : 2 * near * rows_out, :], axis=0)
        for j in range(2 * near):
            q_z[s, j] = summed[j * rows_out : (j + 1) * rows_out]
        height_copies(s, start)

    def per_item(t, unused):
        step = t // 4
        g = lax.rem(t, 4)
        g = jnp.where(g == 1, 2, jnp.where(g == 2, 1, g))
        for when, at, group in (
            (2, 1, 0), (3, 1, 2), (4, 0, 1), (5, 0, 3), (6, 1, 1), (7, 1, 3),
        ):
            step = jnp.where(t == when, at, step)
            g = jnp.where(t == when, group, g)

        @pl.when(t == 4)
        def _():
            take_results(1)

        compute(step, g)

        for when, action in (
            (0, lambda: exchange_x(1)),
            (1, lambda: exchange_z(1)),
            (2, lambda: exchange_results(1)),
            (5, lambda: finish(0)),
            (8, lambda: finish(1)),
            (11, lambda: finish(2)),
            (13, lambda: start_swap(0)),
            (14, lambda: send_x(0, None)),
        ):
            pl.when(t == when)(action)
        return unused

    lax.fori_loop(0, 4 * YS, per_item, 0)

    def bias_y(k):
        return remote(
            bias_sum.at[pl.ds(0, SWEEPS)],
            bias_1.at[y * 2 + core],
            sent_b1.at[k],
            got_b1.at[k],
            y_peer(k),
        )

    def bias_along_z(k):
        return remote(bias_2, bias_z.at[height], sent_b2.at[k], got_b2.at[k], height_peer(k))

    bias_copies = [bias_y(k) for k in range(1, 2 * YS)]
    bias_z_copies = [bias_along_z(k) for k in range(1, heights)]

    for copy in bias_copies:
        copy.start()
    start_swap(1)
    send_z(0)
    bias_1[y * 2 + core] = bias_sum[:SWEEPS, :]
    for copy in bias_copies:
        copy.wait_recv()
    send_x(1, jnp.sum(bias_1[...], axis=0))
    finish(YS - 1)
    grads_ref[...] = part_sum[YS - 1]
    send_z(1)
    bias_2[...] = jnp.sum(got_q_x[1, :, 2 * near * rows_out :, :], axis=0)
    for copy in bias_z_copies:
        copy.start()
    bias_z[height] = bias_2[...]
    for source in range(heights):

        @pl.when(height != source)
        def _():
            remote(
                q_z.at[0, 0],
                got_q_z.at[source],
                sent_qz.at[source],
                got_qz.at[source],
                at_height(source),
            ).wait_recv()

    for copy in bias_z_copies:
        copy.wait_recv()
    small_ref[:rows_out, :] = jnp.sum(got_q_z[...], axis=0)
    small_ref[rows_out:, :] = jnp.sum(bias_z[...], axis=0)

    for s in range(2):
        other_z(s).wait_send()
        other_core(s).wait_send()
        to_sibling(s).wait_send()
        swap(s).wait_send()
        for k in range(1, nx):
            other_x(s, k).wait_send()
            along_x(s, k).wait_send()
            results_x(s, k).wait_send()
            q_along_x(s, k).wait_send()
        for k in range(1, heights):
            along_z(s, k).wait_send()
        height_copies(s, wait_send)
    for step in range(YS - 1):
        for way in range(2):
            ring(step, way).wait_send()
    for copy in bias_copies + bias_z_copies:
        copy.wait_send()


def whole(latents, keys, values, sweep, sweep_bias, grad_out, count, lats):
    rows, points = latents.shape[0], keys.shape[0] // 2
    block, span, chips = points // YS, rows // 2, count // 2
    cols = min(256, span)
    lines = 2 * HEADS * span // 128
    nz = 4 if chips % 4 == 0 else chips
    nx = chips // nz
    heights, near = 2 * nz, nz // 2
    rows_out = rows // count
    x_rows = 2 * near * rows_out
    dma = pltpu.SemaphoreType.DMA
    return pl.pallas_call(
        functools.partial(whole_kernel, count, lats),
        out_shape=[
            jax.ShapeDtypeStruct((2 * WIDTH, block), F32),
            jax.ShapeDtypeStruct((rows_out + SWEEPS, WIDTH), F32),
        ],
        in_specs=vmem_specs(6),
        out_specs=vmem_specs(2),
        scratch_shapes=[
            pltpu.VMEM((points, 2 * WIDTH), BF),
            pltpu.VMEM((HEADS, 48, points), BF),
            pltpu.VMEM((SWEEPS, points), BF),
            pltpu.VMEM((rows, 2 * WIDTH), F32),
            pltpu.VMEM((2, 2, nx, span // (2 * nx), 2 * WIDTH), F32),
            pltpu.VMEM((WIDTH, 4 * span), BF),
            pltpu.VMEM((4 * HEADS, 2 * WIDTH, span), BF),
            pltpu.VMEM((4 * HEADS, 2 * WIDTH, span), BF),
            pltpu.VMEM((points, cols), F32),
            pltpu.VMEM((points, cols), F32),
            pltpu.VMEM((2, 3, lines, 128), F32),
            pltpu.VMEM((2, 3, lines, 128), F32),
            pltpu.VMEM((2, 3, lines, 128), F32),
            pltpu.VMEM((2, nx, 3, lines // nx, 128), F32),
            pltpu.VMEM((2, 3, lines // nx, 128), F32),
            pltpu.VMEM((2, heights, 3, lines // nx, 128), F32),
            pltpu.VMEM((2, 2, lines // nx, 128), F32),
            pltpu.VMEM((2, nx, 2, lines // nx, 128), F32),
            pltpu.VMEM((block, 2 * WIDTH), BF),
            pltpu.VMEM((block, 2 * WIDTH), BF),
            pltpu.VMEM((SWEEPS, block), BF),
            pltpu.VMEM((HEADS, block, span), BF),
            pltpu.VMEM((HEADS, block, span), BF),
            pltpu.VMEM((YS, 2 * WIDTH, block), F32),
            pltpu.VMEM((YS, 2 * WIDTH, block), F32),
            pltpu.VMEM((WIDTH, 4 * span), F32),
            pltpu.VMEM((128, 128), F32),
            pltpu.VMEM((2, 2, nx, 2 * near, rows_out, WIDTH), F32),
            pltpu.VMEM((2, nx, 2 * near, rows_out, WIDTH), F32),
            pltpu.VMEM((2 * YS, SWEEPS, 128), F32),
            pltpu.VMEM((2, nx, x_rows + SWEEPS, WIDTH), F32),
            pltpu.VMEM((2, nx, x_rows + SWEEPS, WIDTH), F32),
            pltpu.VMEM((2, 2 * near, rows_out, WIDTH), F32),
            pltpu.VMEM((heights, rows_out, WIDTH), F32),
            pltpu.VMEM((SWEEPS, 128), F32),
            pltpu.VMEM((heights, SWEEPS, 128), F32),
            dma((2,)),
            dma((2,)),
            dma((2, nx)),
            dma((2, nx)),
            dma((2,)),
            dma((2,)),
            dma((2,)),
            dma((2,)),
            dma((2, nx)),
            dma((2, nx)),
            dma((2, heights)),
            dma((2, heights)),
            dma((2, nx)),
            dma((2, nx)),
            dma((YS, 2)),
            dma((YS, 2)),
            dma((2,)),
            dma((2,)),
            dma((2 * YS,)),
            dma((2 * YS,)),
            dma((2, nx)),
            dma((2, nx)),
            dma((heights,)),
            dma((heights,)),
            dma((heights,)),
            dma((heights,)),
        ],
        compiler_params=pltpu.CompilerParams(
            collective_id=0, has_side_effects=True, vmem_limit_bytes=VMEM_BYTES
        ),
    )(latents, keys, values, sweep, sweep_bias, grad_out)


def deliver_kernel(small_ref, grads_ref, q_out, k_out, v_out, bias_out, square):
    rows_out = q_out.shape[0]
    q_out[...] = small_ref[:rows_out, :]
    k_out[...] = grads_ref[:WIDTH, :].T
    v_out[...] = grads_ref[WIDTH:, :].T
    square[...] = jnp.zeros_like(square)
    square[:SWEEPS, :] = small_ref[rows_out:, :]
    bias_out[...] = square[...].T[:HEADS, :SWEEPS]


def deliver(small, grads):
    block = grads.shape[1]
    return pl.pallas_call(
        deliver_kernel,
        out_shape=[
            jax.ShapeDtypeStruct((small.shape[0] - SWEEPS, WIDTH), F32),
            jax.ShapeDtypeStruct((block, WIDTH), F32),
            jax.ShapeDtypeStruct((block, WIDTH), F32),
            jax.ShapeDtypeStruct((HEADS, SWEEPS), F32),
        ],
        in_specs=vmem_specs(2),
        out_specs=vmem_specs(4),
        scratch_shapes=[pltpu.VMEM((128, 128), F32)],
    )(small, grads)


def per_device(count, lats, latents, keys, values, sweep, sweep_bias, grad_out):
    grads, small = whole(
        latents, keys, values, sweep.reshape(1, -1), sweep_bias, grad_out, count, lats
    )
    return tuple(deliver(small, grads))


def solution(mesh):
    return jax.shard_map(
        functools.partial(per_device, mesh.shape["pts"], mesh.shape["lat"]),
        mesh=mesh,
        in_specs=(P("lat", None), P("pts", None), P("pts", None), P("pts"), P(), P("lat", None)),
        out_specs=(P(("lat", "pts"), None), P(("pts", "lat"), None), P(("pts", "lat"), None), P()),
        check_vma=False,
    )
```

time: 108 us -> 125 us (1.16)
  Pallas kernels: 107 us -> 124 us
    pallas_call x1, Pallas kernels: 105 us -> 122 us  [whole(): pl.pallas_call(functools.partial(whole_kernel, count, lats), out_shape=[j...]
where the time goes in v6:
time: 125 us
  Pallas kernels  124 us (99%)
    pallas_call x1, Pallas kernels, whole(): pl.pallas_call(functools.partial(whole_kernel, count, lats), out_shape=[j...  122 us

profile of v6, /device:TPU:1, one launch (start us, length us, event | category | flops | bytes accessed | tf_op | source)
XLA Modules:
  0.0 124.6 jit_solution(8361693384051595039)
XLA Ops:
  0.6 122.0 %shard_map.93 = (f32[256,512]{1,0:T(8,128)}, f32[48,128]{1,0:T(8,128)}) custom-call(bf16[1024,128]{1,0:T(8,128)(2,1)} %latents_ref.1, bf16[4096,128]{1,0:T(8,128)(2,1)} %keys_ref.1, bf16[4096,128]{1,0:T(8,128)(2,1)} %values_ref.1, s32[1,4096]{1,0:T(1,128)} %bitcast.1, f32[4,16]{1,0:T(4,128)} %sweep_bias_ref.1, bf16[1024,128]{1,0:T(8,128)(2,1)} %grad_out_ref.1), custom_call_target="tpu_custom_call" | custom-call | tf_op jit(solution)/shard_map/pallas_call | solution.py:703
  122.7 2.0 %shard_map.94 = (f32[32,128]{1,0:T(8,128)}, f32[512,128]{1,0:T(8,128)}, f32[512,128]{1,0:T(8,128)}, f32[4,16]{1,0:T(4,128)}) custom-call(f32[48,128]{1,0:T(8,128)} %get-tuple-element.6.small_ref, f32[256,512]{1,0:T(8,128)} %get-tuple-element.7.grads_ref), custom_call_target="tpu_custom_call" | custom-call | tf_op jit(solution)/shard_map/pallas_call | solution.py:793

commit v7 on v5

--- a/solution.py
+++ b/solution.py
@@ -62,6 +62,9 @@
     g_feat,
     scores_0,
     scores_1,
+    kept,
+    factors,
+    g_factored,
     stats,
     from_sibling,
     stats_1,
@@ -183,16 +186,17 @@
     def build(c):
         rows = pl.ds(pl.multiple_of(c * chunk, chunk), chunk)
         swept = sweep_ref[:, rows]
-        row = lax.broadcasted_iota(jnp.int32, (WIDTH, chunk), 0)
-        marked = (row < ONES_ROW) & (lax.rem(row, SWEEPS) == swept)
-        ones = (row >= ONES_ROW) & (row < ONES_ROW + 3)
-        aux_t = jnp.where(marked | ones, 1.0, 0.0)
-        onehot_t[:, rows] = aux_t[:SWEEPS].astype(BF)
+        row = lax.broadcasted_iota(jnp.int32, (SWEEPS, chunk), 0)
+        marked = jnp.where(row == swept, 1.0, 0.0)
+        ones = jnp.where(row < 3, 1.0, 0.0)
+        rest = jnp.zeros((WIDTH - 4 * SWEEPS, chunk), F32)
+        aux_t = jnp.concatenate([marked, marked, marked, ones, rest], axis=0)
+        onehot_t[:, rows] = marked.astype(BF)
         k_aux[rows, WIDTH:] = aux_t.T.astype(BF)
         value_t = values_ref[rows, :].T
         for h in range(HEADS):
             value_rows[h, :HEAD_DIM, rows] = value_t[h * HEAD_DIM : (h + 1) * HEAD_DIM, :]
-            value_rows[h, HEAD_DIM:, rows] = jnp.where(row[:16] == 0, 1.0, 0.0).astype(BF)
+            value_rows[h, HEAD_DIM:, rows] = jnp.where(row == 0, 1.0, 0.0).astype(BF)
 
     every(0, chunks, build)
     q_t = latents_ref[...].T
@@ -217,7 +221,6 @@
                 q_feat[n, WIDTH + index * SWEEPS : WIDTH + (index + 1) * SWEEPS, :] = piece
     grad_q_t[...] = jnp.zeros_like(grad_q_t)
     bias_sum[...] = jnp.zeros_like(bias_sum)
-    part_sum[...] = jnp.zeros_like(part_sum)
 
     def merge(parts):
         best = functools.reduce(jnp.maximum, [part[0] for part in parts])
@@ -265,7 +268,10 @@
         for k in range(1, nz):
             along_z(s, k).wait_recv()
         best, total, weighted = merge([stats_z[s, i] for i in range(nz)])
-        offset = (best + jnp.log(total) * LOG2E) * (-1.0 / TO_LOG2)
+        if s == 0:
+            first = (best + jnp.log(total) * LOG2E) * (-1.0 / TO_LOG2)
+        else:
+            first = jnp.exp2(stats[s, 0] - best) / total
         delta = -(weighted / total)
         row16 = lax.broadcasted_iota(jnp.int32, (16, 128), 0)
         per_tile = cols // 128
@@ -274,7 +280,9 @@
             for part in range(per_tile):
                 line = n * per_tile + part
                 left = it * cols + part * 128
-                for value, feat in ((offset, q_feat), (delta, g_feat)):
+                if s == 1:
+                    factors[h : h + 1, left : left + 128] = first[line : line + 1, :]
+                for value, feat in ((first, q_feat), (delta, g_feat))[s:]:
                     hi, mid, low = three_pieces(value[line : line + 1, :])
                     feat[
                         s * HEADS + h,
@@ -288,6 +296,14 @@
                         ),
                     ).astype(BF)
 
+        if s == 1:
+            for h in range(HEADS):
+                rows = slice(h * HEAD_DIM, (h + 1) * HEAD_DIM)
+                product = g_t[rows, span:].astype(F32) * factors[h : h + 1, :]
+                hi, mid, _ = three_pieces(product)
+                g_factored[h, :HEAD_DIM, :] = hi
+                g_factored[h, HEAD_DIM:, :] = mid
+
     lowest = jnp.full((32, cols), -jnp.inf, F32)
 
     def feature_of(n):
@@ -304,15 +320,18 @@
         into[rows, :] = s
         return jnp.maximum(top, jnp.max(s.reshape(chunk // 32, 32, cols), axis=0))
 
-    def tile_sums(n, scores, top_rows, following, into):
+    def tile_sums(keep_e, n, scores, top_rows, following, into):
         top = jnp.max(top_rows, axis=0, keepdims=True)
         head = lax.rem(n, HEADS)
         next_top = lowest
+        unused_index, lanes = feature_of(n)
         out = jnp.zeros((48, cols), F32)
         for c in range(chunks):
             rows = pl.ds(c * chunk, chunk)
-            e = jnp.exp2(scores[rows, :] - top)
-            out = out + dot(value_rows[head, :, rows], e.astype(BF))
+            e = jnp.exp2(scores[rows, :] - top).astype(BF)
+            if keep_e:
+                kept[head, rows, lanes] = e
+            out = out + dot(value_rows[head, :, rows], e)
             next_top = score_chunk(following, into, c, next_top)
         g = g_t[
             pl.ds(pl.multiple_of(head * HEAD_DIM, HEAD_DIM), HEAD_DIM),
@@ -333,10 +352,12 @@
     for c in range(chunks):
         first_top = score_chunk(0, scores_0, c, first_top)
 
-    def per_pair(pair, top_rows):
+    def per_pair(keep_e, pair, top_rows):
         n = pair * 2
-        top_rows = tile_sums(n, scores_0, top_rows, n + 1, scores_1)
-        top_rows = tile_sums(n + 1, scores_1, top_rows, lax.rem(n + 2, tiles), scores_0)
+        top_rows = tile_sums(keep_e, n, scores_0, top_rows, n + 1, scores_1)
+        top_rows = tile_sums(
+            keep_e, n + 1, scores_1, top_rows, lax.rem(n + 2, tiles), scores_0
+        )
 
         @pl.when(pair == pairs // 2 - 1)
         def _():
@@ -353,7 +374,8 @@
 
         return top_rows
 
-    lax.fori_loop(0, pairs, per_pair, first_top)
+    first_top = lax.fori_loop(0, pairs // 2, functools.partial(per_pair, False), first_top)
+    lax.fori_loop(pairs // 2, pairs, functools.partial(per_pair, True), first_top)
     to_sibling(1).start()
     take_results(0)
 
@@ -364,36 +386,57 @@
         owner_z = jnp.where(step < YS, 1 - z, z)
         at_up = (owner_z * YS + lax.rem(y + 2 * YS - 1 - turn, YS)) * block
         at_down = (owner_z * YS + lax.rem(y + 1 + turn, YS)) * block + half
+        places = []
         for row, at in ((0, at_up), (half, at_down)):
             source = pl.ds(pl.multiple_of(at, half), half)
             rows = pl.ds(row, half)
-            k_stage[rows, :] = k_aux[source, :]
+            if s == 0:
+                k_stage[rows, :] = k_aux[source, :]
+            else:
+                k_stage[rows, :WIDTH] = keys_ref[source, :]
             v_stage[rows, :WIDTH] = values_ref[source, :]
             v_stage[rows, WIDTH:] = k_aux[source, WIDTH:]
             mark_stage[:, row : row + half] = onehot_t[:, source]
+            places.append((slice(row, row + half), source))
         k_t = k_stage[:, :WIDTH].T
         row_sums = jnp.zeros((block, 128), F32)
-        lanes = pl.ds(pl.multiple_of(s * span, span), span)
+        lanes = slice(s * span, (s + 1) * span)
         for h in range(HEADS):
             n = s * HEADS + h
             rows = slice(h * HEAD_DIM, (h + 1) * HEAD_DIM)
-            p = jnp.exp2(dot(k_stage[...], q_feat[n]) * TO_LOG2)
-            score_grad = p * dot(v_stage[...], g_feat[n])
-            probs[h] = p.astype(BF)
-            scaled[h] = (score_grad * SCALE).astype(BF)
-            folded = score_grad[:, :128]
+            rows_v = slice(WIDTH + h * HEAD_DIM, WIDTH + (h + 1) * HEAD_DIM)
+            out_prod = dot(v_stage[...], g_feat[n])
+            if s == 0:
+                p = jnp.exp2(dot(k_stage[...], q_feat[n]) * TO_LOG2)
+                low = (p * out_prod) * SCALE
+                probs[h] = p.astype(BF)
+                part_sum[step, rows_v, :] = dot_transposed(g_feat[n, rows, :], probs[h])
+            else:
+                out_prod = out_prod * (factors[h : h + 1, :] * SCALE)
+                low = jnp.concatenate(
+                    [
+                        kept[h, source, :].astype(F32) * out_prod[place]
+                        for place, source in places
+                    ],
+                    axis=0,
+                )
+                for place, source in places:
+                    both = dot_transposed(g_factored[h], kept[h, source, :])
+                    part_sum[step, rows_v, place] += both[:HEAD_DIM] + both[HEAD_DIM:]
+            scaled[h] = low.astype(BF)
+            folded = low[:, :128]
             for part in range(1, span // 128):
-                folded = folded + score_grad[:, part * 128 : (part + 1) * 128]
+                folded = folded + low[:, part * 128 : (part + 1) * 128]
             row_sums = row_sums + jnp.where(
                 lane_row == h, jnp.sum(folded, axis=1, keepdims=True), 0.0
             )
-            part_sum[step, rows, :] += dot_transposed(q_feat[n, rows, :], scaled[h])
-            part_sum[step, WIDTH + h * HEAD_DIM : WIDTH + (h + 1) * HEAD_DIM, :] += dot_transposed(
-                g_feat[n, rows, :], probs[h]
-            )
+            grad_k = dot_transposed(q_feat[n, rows, :], scaled[h])
+            if s == 0:
+                part_sum[step, rows, :] = grad_k
+            else:
+                part_sum[step, rows, :] += grad_k
             grad_q_t[rows, lanes] += dot(k_t[rows, :], scaled[h])
-
-        for piece in three_pieces(row_sums):
+        for piece in three_pieces(row_sums * (1.0 / SCALE)):
             bias_sum[:SWEEPS, :] += dot(mark_stage[...], piece)
 
     def lanes_of(part, way):
@@ -457,7 +500,8 @@
         def _():
             take_results(1)
 
-        compute(step, s)
+        for index in range(2):
+            pl.when(s == index)(functools.partial(compute, step, index))
 
         @pl.when(t == 0)
         def _():
@@ -601,6 +645,9 @@
             pltpu.VMEM((2 * HEADS, 2 * WIDTH, span), BF),
             pltpu.VMEM((points, cols), F32),
             pltpu.VMEM((points, cols), F32),
+            pltpu.VMEM((HEADS, points, span), BF),
+            pltpu.VMEM((8, span), F32),
+            pltpu.VMEM((HEADS, 2 * HEAD_DIM, span), BF),
             pltpu.VMEM((2, 3, lines, 128), F32),
             pltpu.VMEM((2, 3, lines, 128), F32),
             pltpu.VMEM((2, 3, lines, 128), F32),

time: 108 us -> 103 us (0.954)
  Pallas kernels: 107 us -> 103 us
    pallas_call x1, Pallas kernels: 105 us -> 101 us  [whole(): pl.pallas_call(functools.partial(whole_kernel, count, lats), out_shape=[j...]
where the time goes in v7:
time: 103 us
  Pallas kernels  103 us (100%)
    pallas_call x1, Pallas kernels, whole(): pl.pallas_call(functools.partial(whole_kernel, count, lats), out_shape=[j...  101 us

profile of v7, /device:TPU:1, one launch (start us, length us, event | category | flops | bytes accessed | tf_op | source)
XLA Modules:
  0.0 103.2 jit_solution(18091563581170921344)
XLA Ops:
  0.6 100.6 %shard_map.93 = (f32[256,512]{1,0:T(8,128)}, f32[48,128]{1,0:T(8,128)}) custom-call(bf16[1024,128]{1,0:T(8,128)(2,1)} %latents_ref.1, bf16[4096,128]{1,0:T(8,128)(2,1)} %keys_ref.1, bf16[4096,128]{1,0:T(8,128)(2,1)} %values_ref.1, s32[1,4096]{1,0:T(1,128)} %bitcast.1, f32[4,16]{1,0:T(4,128)} %sweep_bias_ref.1, bf16[1024,128]{1,0:T(8,128)(2,1)} %grad_out_ref.1), custom_call_target="tpu_custom_call" | custom-call | tf_op jit(solution)/shard_map/pallas_call | solution.py:631
  101.2 2.0 %shard_map.94 = (f32[32,128]{1,0:T(8,128)}, f32[512,128]{1,0:T(8,128)}, f32[512,128]{1,0:T(8,128)}, f32[4,16]{1,0:T(4,128)}) custom-call(f32[48,128]{1,0:T(8,128)} %get-tuple-element.6.small_ref, f32[256,512]{1,0:T(8,128)} %get-tuple-element.7.grads_ref), custom_call_target="tpu_custom_call" | custom-call | tf_op jit(solution)/shard_map/pallas_call | solution.py:718

commit v8 on v7

--- a/solution.py
+++ b/solution.py
@@ -378,6 +378,7 @@
     lax.fori_loop(pairs // 2, pairs, functools.partial(per_pair, True), first_top)
     to_sibling(1).start()
     take_results(0)
+    exchange_x(1)
 
     lane_row = lax.broadcasted_iota(jnp.int32, (block, 128), 1)
 
@@ -491,12 +492,11 @@
                 near(part, way).start()
 
     def per_item(t, unused):
-        step = t // 2
-        for when, value in ((1, 1), (2, 2), (3, 0), (4, 1), (5, 3), (6, 2)):
-            step = jnp.where(t == when, value, step)
-        s = jnp.where((t < 3) | (t == 5), 0, jnp.where(t < 8, 1, lax.rem(t, 2)))
-
-        @pl.when(t == 3)
+        swapped = (t == 1) | (t == 2)
+        step = jnp.where(swapped, 2 - t, t // 2)
+        s = jnp.where(swapped, t - 1, lax.rem(t, 2))
+
+        @pl.when(t == 2)
         def _():
             take_results(1)
 
@@ -505,15 +505,14 @@
 
         @pl.when(t == 0)
         def _():
-            exchange_x(1)
-
-        @pl.when(t == 1)
-        def _():
             exchange_z(1)
 
-        @pl.when(t >= 3)
-        def _():
-            finish(jnp.where(t < 11, (t - 3) // 2, (t - 1) // 2), lax.rem(t + 1, 2))
+        @pl.when((t >= 2) & (t != 10))
+        def _():
+            finish(
+                jnp.where(t < 10, (t - 2) // 2, (t - 1) // 2),
+                jnp.where(t < 10, lax.rem(t, 2), lax.rem(t + 1, 2)),
+            )
 
         @pl.when((t == 9) | (t == 10))
         def _():
@@ -521,7 +520,7 @@
 
         for part in range(2):
 
-            @pl.when(t == 11 + part)
+            @pl.when(t == 10 + part)
             def _():
                 for way in range(2):
                     near(part, way).wait_recv()
@@ -581,25 +580,6 @@
         copy.start()
     got_q_x[x] = q_x[x]
     finish(2 * YS - 1, 1)
-    for copy in x_copies:
-        copy.wait_recv()
-    summed = jnp.sum(got_q_x[...], axis=0)
-    bias_2[...] = summed[nz * rows_out :]
-    for j in range(nz):
-        q_z[j] = summed[j * rows_out : (j + 1) * rows_out]
-    for copy in bias_z_copies + z_copies:
-        copy.start()
-    got_q_z[zl] = q_z[zl]
-    bias_z[height] = bias_2[...]
-    for part in range(2):
-        for way in range(2):
-            far(part, way).wait_recv()
-    grads_ref[...] = part_sum[2 * YS - 1] + from_z[...]
-    for copy in bias_z_copies + z_copies:
-        copy.wait_recv()
-    small_ref[:rows_out, :] = jnp.sum(got_q_z[...], axis=0)
-    small_ref[rows_out:, :] = jnp.sum(bias_z[...], axis=0)
-
     for s in range(2):
         to_sibling(s).wait_send()
         for k in range(1, nx):
@@ -612,9 +592,30 @@
                 if step % YS < YS - 1:
                     ring(step, part, way).wait_send()
             near(part, way).wait_send()
+    for copy in x_copies:
+        copy.wait_recv()
+    summed = jnp.sum(got_q_x[...], axis=0)
+    bias_2[...] = summed[nz * rows_out :]
+    for j in range(nz):
+        q_z[j] = summed[j * rows_out : (j + 1) * rows_out]
+    for copy in bias_z_copies + z_copies:
+        copy.start()
+    got_q_z[zl] = q_z[zl]
+    bias_z[height] = bias_2[...]
+    swap.wait_send()
+    for copy in bias_copies + x_copies:
+        copy.wait_send()
+    for part in range(2):
+        for way in range(2):
             far(part, way).wait_send()
-    swap.wait_send()
-    for copy in bias_copies + x_copies + z_copies + bias_z_copies:
+            far(part, way).wait_recv()
+    grads_ref[...] = part_sum[2 * YS - 1] + from_z[...]
+    for copy in bias_z_copies + z_copies:
+        copy.wait_recv()
+    small_ref[:rows_out, :] = jnp.sum(got_q_z[...], axis=0)
+    small_ref[rows_out:, :] = jnp.sum(bias_z[...], axis=0)
+
+    for copy in z_copies + bias_z_copies:
         copy.wait_send()
 
 

time: 103 us -> 101 us (0.981)
  Pallas kernels: 103 us -> 101 us
    pallas_call x1, Pallas kernels: 101 us -> 98.5 us  [whole(): pl.pallas_call(functools.partial(whole_kernel, count, lats), out_shape=[j...]
where the time goes in v8:
time: 101 us
  Pallas kernels  101 us (100%)
    pallas_call x1, Pallas kernels, whole(): pl.pallas_call(functools.partial(whole_kernel, count, lats), out_shape=[j...  98.5 us

profile of v8, /device:TPU:1, one launch (start us, length us, event | category | flops | bytes accessed | tf_op | source)
XLA Modules:
  0.0 101.1 jit_solution(9139926684439237515)
XLA Ops:
  0.6 98.5 %shard_map.93 = (f32[256,512]{1,0:T(8,128)}, f32[48,128]{1,0:T(8,128)}) custom-call(bf16[1024,128]{1,0:T(8,128)(2,1)} %latents_ref.1, bf16[4096,128]{1,0:T(8,128)(2,1)} %keys_ref.1, bf16[4096,128]{1,0:T(8,128)(2,1)} %values_ref.1, s32[1,4096]{1,0:T(1,128)} %bitcast.1, f32[4,16]{1,0:T(4,128)} %sweep_bias_ref.1, bf16[1024,128]{1,0:T(8,128)(2,1)} %grad_out_ref.1), custom_call_target="tpu_custom_call" | custom-call | tf_op jit(solution)/shard_map/pallas_call | solution.py:632
  99.2 2.0 %shard_map.94 = (f32[32,128]{1,0:T(8,128)}, f32[512,128]{1,0:T(8,128)}, f32[512,128]{1,0:T(8,128)}, f32[4,16]{1,0:T(4,128)}) custom-call(f32[48,128]{1,0:T(8,128)} %get-tuple-element.6.small_ref, f32[256,512]{1,0:T(8,128)} %get-tuple-element.7.grads_ref), custom_call_target="tpu_custom_call" | custom-call | tf_op jit(solution)/shard_map/pallas_call | solution.py:719

commit v9 on v8

--- a/solution.py
+++ b/solution.py
@@ -120,7 +120,7 @@
     per_span = span // cols
     tiles = HEADS * 2 * per_span
     pairs = tiles // 2
-    chunk = min(512, points)
+    chunk = min(1024, points)
     chunks = points // chunk
     block = points // (2 * YS)
     half = block // 2
@@ -316,7 +316,7 @@
     def score_chunk(n, into, c, top):
         index, lanes = feature_of(n)
         rows = pl.ds(c * chunk, chunk)
-        s = dot(k_aux[rows, :], q_feat[index, :, lanes]) * TO_LOG2
+        s = dot(k_aux[rows, :], q_feat[index, :, lanes])
         into[rows, :] = s
         return jnp.maximum(top, jnp.max(s.reshape(chunk // 32, 32, cols), axis=0))
 
@@ -328,11 +328,11 @@
         out = jnp.zeros((48, cols), F32)
         for c in range(chunks):
             rows = pl.ds(c * chunk, chunk)
-            e = jnp.exp2(scores[rows, :] - top).astype(BF)
+            next_top = score_chunk(following, into, c, next_top)
+            e = jnp.exp2((scores[rows, :] - top) * TO_LOG2).astype(BF)
             if keep_e:
                 kept[head, rows, lanes] = e
             out = out + dot(value_rows[head, :, rows], e)
-            next_top = score_chunk(following, into, c, next_top)
         g = g_t[
             pl.ds(pl.multiple_of(head * HEAD_DIM, HEAD_DIM), HEAD_DIM),
             pl.ds(pl.multiple_of((n // HEADS) * cols, cols), cols),
@@ -340,7 +340,7 @@
         weighted = jnp.sum(out[:HEAD_DIM] * g, axis=0, keepdims=True)
         total = out[HEAD_DIM : HEAD_DIM + 1]
         per_tile = cols // 128
-        for kind, value in enumerate((top, total, weighted)):
+        for kind, value in enumerate((top * TO_LOG2, total, weighted)):
             for part in range(per_tile):
                 line = lax.rem(n, tiles // 2) * per_tile + part
                 stats[n // (tiles // 2), kind, pl.ds(line, 1), :] = value[

time: 101 us -> 99.5 us (0.985)
  Pallas kernels: 101 us -> 98.8 us
    pallas_call x1, Pallas kernels: 98.5 us -> 96.8 us  [whole(): pl.pallas_call(functools.partial(whole_kernel, count, lats), out_shape=[j...]
where the time goes in v9:
time: 99.5 us; the launch traced here: 99.4 us
  Pallas kernels  98.8 us (99%)
    pallas_call x1, Pallas kernels, whole(): pl.pallas_call(functools.partial(whole_kernel, count, lats), out_shape=[j...  96.8 us

profile of v9, /device:TPU:1, one launch (start us, length us, event | category | flops | bytes accessed | tf_op | source)
XLA Modules:
  0.0 99.4 jit_solution(7771140358288362210)
XLA Ops:
  0.6 96.8 %shard_map.93 = (f32[256,512]{1,0:T(8,128)}, f32[48,128]{1,0:T(8,128)}) custom-call(bf16[1024,128]{1,0:T(8,128)(2,1)} %latents_ref.1, bf16[4096,128]{1,0:T(8,128)(2,1)} %keys_ref.1, bf16[4096,128]{1,0:T(8,128)(2,1)} %values_ref.1, s32[1,4096]{1,0:T(1,128)} %bitcast.1, f32[4,16]{1,0:T(4,128)} %sweep_bias_ref.1, bf16[1024,128]{1,0:T(8,128)(2,1)} %grad_out_ref.1), custom_call_target="tpu_custom_call" | custom-call | tf_op jit(solution)/shard_map/pallas_call | solution.py:632
  97.4 2.0 %shard_map.94 = (f32[32,128]{1,0:T(8,128)}, f32[512,128]{1,0:T(8,128)}, f32[512,128]{1,0:T(8,128)}, f32[4,16]{1,0:T(4,128)}) custom-call(f32[48,128]{1,0:T(8,128)} %get-tuple-element.6.small_ref, f32[256,512]{1,0:T(8,128)} %get-tuple-element.7.grads_ref), custom_call_target="tpu_custom_call" | custom-call | tf_op jit(solution)/shard_map/pallas_call | solution.py:719
